TPU v7x, 32 devices: a whole 2x2x4 slice. The times are simulated.
32 devices in a mesh: band: 8 (over z, y), grid: 4 (over x, core).
Axes of the slice: x: 2, y: 2, z: 4, core: 2. Of those that a mesh axis runs over, the one named last changes fastest.
Arguments:
- orbitals: bfloat16 [32, 96, 9216], P('band', 'grid'), may hold values from -6 to 6
- kernel: float32 [96, 9216], P('grid'), may hold values from 0.02 to 1
Outputs:
- update: float32 [32, 96, 9216], P('band', 'grid')
All inputs are finite; a program needn't handle non-finite values.
Results may differ from a plain program's by a relative error of at most 0.0049.
Values may be sent and summed in bfloat16 or wider, within the bound.
No kernel may reach another device: no remote copies, remote signals or barrier semaphores. Data moves between devices by JAX's collectives and lax.ppermute only.
A program may use at most 128 MiB of HBM per device.

v0:
```python
import math

import jax
import jax.numpy as jnp
from jax import lax
from jax.sharding import PartitionSpec as P

GRID_N = 96
DIST = 1


def passed_along(block, axis, distance):
    devices = range(lax.axis_size(axis))
    route = [((i - distance) % len(devices), i) for i in devices]
    return lax.ppermute(block, axis, route)


def make_tables(count):
    indices = jnp.arange(count, dtype=jnp.int32)
    angles = (indices[:, None] * indices[None, :] % count).astype(jnp.float32) * (
        2.0 * math.pi / count
    )
    cosine = jnp.cos(angles).astype(jnp.bfloat16)
    sine = jnp.sin(angles).astype(jnp.bfloat16)
    real_table = jnp.stack([cosine, -sine])
    forward = jnp.stack([jnp.stack([cosine, sine]), jnp.stack([-sine, cosine])])
    backward = jnp.stack([jnp.stack([cosine, -sine]), jnp.stack([sine, cosine])])
    return (real_table, forward, backward)


def contract(form, table, operand):
    return jnp.einsum(form, table, operand, preferred_element_type=jnp.float32)


def first_passes(density, real_table, forward):
    along_z = contract("ckz,xyzp->xykcp", real_table, density).astype(jnp.bfloat16)
    return contract("dcjy,xykcp->xjkdp", forward, along_z).astype(jnp.bfloat16)


def middle_passes(along_zy, scaled, forward, backward):
    summed = contract("dcgx,xjkcp->gjkdp", forward, along_zy)
    spectrum = (summed * scaled[:, :, :, None, None]).astype(jnp.bfloat16)
    return contract("dcxg,gjkcp->xjkdp", backward, spectrum).astype(jnp.bfloat16)


def last_passes(back_x, real_table, backward):
    back_xy = contract("dcyj,xjkcp->xykdp", backward, back_x).astype(jnp.bfloat16)
    return contract("ckz,xykcp->xyzp", real_table, back_xy)


def local(orbitals, kernel):
    count = GRID_N
    band_count = orbitals.shape[0]
    plane_count = orbitals.shape[1]
    pair_count = band_count * band_count
    real_table, forward, backward = make_tables(count)
    partner = passed_along(orbitals, "band", DIST)
    own_last = orbitals.reshape(band_count, plane_count, count, count).transpose(1, 2, 3, 0)
    other_last = partner.reshape(band_count, plane_count, count, count).transpose(1, 2, 3, 0)
    density = (
        own_last.astype(jnp.float32)[..., :, None] * other_last.astype(jnp.float32)[..., None, :]
    ).astype(jnp.bfloat16)
    density = density.reshape(plane_count, count, count, pair_count)
    scaled = kernel / count**3
    column_kernel = scaled.reshape(-1, count, count).transpose(1, 0, 2)
    along_zy = first_passes(density, real_table, forward)
    back_x = middle_passes(
        lax.all_to_all(along_zy, "grid", split_axis=1, concat_axis=0, tiled=True),
        column_kernel,
        forward,
        backward,
    )
    back_x = lax.all_to_all(back_x, "grid", split_axis=0, concat_axis=1, tiled=True)
    potential = last_passes(back_x, real_table, backward)
    potential = potential.reshape(plane_count, count, count, band_count, band_count)
    kept = -jnp.einsum("xyzab,xyzb->xyza", potential, other_last.astype(jnp.float32))
    sent = -jnp.einsum("xyzab,xyza->xyzb", potential, own_last.astype(jnp.float32))
    kept = kept.transpose(3, 0, 1, 2).reshape(band_count, plane_count, count * count)
    sent = sent.transpose(3, 0, 1, 2).reshape(band_count, plane_count, count * count)
    returned = passed_along(sent, "band", -DIST)
    return kept + returned


def solution(mesh):
    placed = (P("band", "grid", None), P("grid", None))
    return jax.shard_map(
        local, mesh=mesh, in_specs=placed, out_specs=P("band", "grid", None), check_vma=False
    )
```

profile of v0, /device:TPU:0, one launch (start us, length us, event | category | flops | bytes accessed | tf_op | source)
XLA Modules:
  0.0 769.5 jit_solution(9436087757402899785)
XLA Ops:
  0.0 3.0 collective-permute-start
  3.0 3.7 reshape.95
  6.7 0.2 fusion.47
  6.9 0.2 sine_convert_fusion
  7.1 2.8 bitcast_convert_fusion.4
  10.0 35.0 %collective-permute-done = bf16[4,24,9216]{2,1,0:T(8,128)(2,1)} collective-permute-done((bf16[4,24,9216]{2,1,0:T(8,128)(2,1)}, bf16[4,24,9216]{2,1,0:T(8,128)(2,1)}, u32[]{:S(2)}, u32[]{:S(2)}) %collective-permute-start) | collective-permute-done | bytes 1769504 | tf_op jit(solution)/shard_map/ppermute | solution.py:15
  44.9 3.7 reshape.96
  48.6 0.6 bitcast_convert_fusion.3
  49.2 0.0 copy-start
  49.2 2.1 copy-done
  51.4 7.3 multiply_convert_fusion
  58.7 15.9 %fusion.1 = bf16[24,96,96,2,16]{1,2,3,4,0:T(8,128)(2,1)} fusion(bf16[24,96,96,16,1]{2,1,4,3,0:T(8,128)(2,1)} %bitcast.124, bf16[1,2,96,96]{3,2,1,0:T(8,128)(2,1)S(1)} %get-tuple-element.6, bf16[1,2,96,96]{3,2,1,0:T(8,128)(2,1)S(1)} %get-tuple-element.9, bf16[1,96,96]{2,1,0:T(8,128)(2,1)S(1)} %get-tuple-element.12, bf16[1,96,96]{2,1,0:T(8,128)(2,1)S(1)} %fusion.47), kind=kOutput, calls=%fused_computation.5 | convolution fusion | flops 4091240448 | bytes 21344256 | tf_op jit(solution)/shard_map/dcjy,xykcp->xjkdp/dot_general | solution.py:32
  74.6 42.2 %copy.16 = bf16[24,96,96,2,16]{2,3,4,0,1:T(2,128)(2,1)} copy(bf16[24,96,96,2,16]{1,2,3,4,0:T(8,128)(2,1)} %fusion.1) | data formatting | bytes 28311552 | tf_op jit(solution)/shard_map/convert_element_type | solution.py:37
  116.8 0.0 copy-start.1
  116.8 7.6 all-to-all-start
  124.5 0.0 copy-done.1
  124.5 0.1 broadcast_multiply_fusion
  124.6 0.5 reshape.97
  125.0 0.4 copy.20
  125.4 204.4 %all-to-all-done = bf16[24,96,96,2,16]{2,3,4,0,1:T(2,128)(2,1)} async-done(((bf16[24,96,96,2,16]{2,3,4,0,1:T(2,128)(2,1)}), bf16[24,96,96,2,16]{2,3,4,0,1:T(2,128)(2,1)}, u32[]{:S(2)}, u32[]{:S(2)}) %all-to-all-start) | async-done | bytes 14155808 | tf_op jit(solution)/shard_map/all_to_all | solution.py:68
  329.8 12.2 %copy.17 = bf16[24,96,96,2,16]{2,4,3,1,0:T(8,128)(2,1)S(1)} copy(bf16[24,96,96,2,16]{2,3,4,0,1:T(2,128)(2,1)} %all-to-all-done) | data formatting | bytes 28311552 | tf_op jit(solution)/shard_map/all_to_all | solution.py:68
  342.0 7.0 copy.18
  349.0 33.2 %fusion.2 = bf16[96,24,96,2,16]{0,2,3,4,1:T(8,128)(2,1)} fusion(f32[96,24,96]{0,2,1:T(8,128)S(1)} %bitcast.127, bf16[96,24,96,2,16,1]{2,4,3,1,0,5:T(8,128)(2,1)} %bitcast.125, bf16[1,2,96,96]{3,2,1,0:T(8,128)(2,1)S(1)} %get-tuple-element.10, bf16[1,2,96,96]{3,2,1,0:T(8,128)(2,1)S(1)} %get-tuple-element.5, bf16[1,2,96,96]{3,2,1,0:T(8,128)(2,1)S(1)} %get-tuple-element.6, ...), kind=kOutput, calls=%fused_computation.6 | convolution fusion | flops 5457346560 | bytes 29343744 | tf_op jit(solution)/shard_map/dcxg,gjkcp->xjkdp/dot_general | solution.py:32
  382.2 42.2 %copy.21 = bf16[96,24,96,2,16]{2,3,4,1,0:T(2,128)(2,1)} copy(bf16[96,24,96,2,16]{0,2,3,4,1:T(8,128)(2,1)} %fusion.2) | data formatting | bytes 28311552 | tf_op jit(solution)/shard_map/convert_element_type | solution.py:43
  424.4 210.3 %all_to_all.36 = bf16[96,24,96,2,16]{2,3,4,1,0:T(2,128)(2,1)S(1)} all-to-all(bf16[96,24,96,2,16]{2,3,4,1,0:T(2,128)(2,1)} %copy.21), channel_id=1, replica_groups=mesh['band'=8,'grid'=4] {'grid'}, dimensions={0} | all-to-all | bytes 28311552 | tf_op jit(solution)/shard_map/all_to_all | solution.py:73
  634.7 4.9 copy.22
  639.6 7.0 copy.23
  646.6 22.6 %fusion.4 = f32[24,96,16,96,1]{3,1,4,2,0:T(8,128)} fusion(bf16[24,96,96,2,16,1]{2,4,3,1,0,5:T(8,128)(2,1)} %bitcast.126, bf16[1,2,96,96]{3,2,1,0:T(8,128)(2,1)S(1)} %get-tuple-element.10, bf16[1,2,96,96]{3,2,1,0:T(8,128)(2,1)S(1)} %get-tuple-element.5, bf16[1,96,96]{2,1,0:T(8,128)(2,1)S(1)} %get-tuple-element.12, bf16[1,96,96]{2,1,0:T(8,128)(2,1)S(1)} %fusion.47), kind=kOutput, calls=%fused_computation.8 | convolution fusion | flops 4084107264 | bytes 28422144 | tf_op jit(solution)/shard_map/ckz,xykcp->xyzp/dot_general | solution.py:32
  669.2 9.2 %multiply_reduce_fusion = f32[24,96,96,4]{2,1,3,0:T(8,128)S(1)} fusion(f32[24,96,96,4,4]{2,1,4,3,0:T(8,128)} %bitcast.120, f32[24,96,96,4]{2,1,3,0:T(8,128)} %bitcast_convert_fusion.4), kind=kLoop, calls=%fused_computation.17 | loop fusion | flops 6193152 | bytes 21233664
  678.4 2.6 fusion.33
  681.0 6.1 reshape.100
  687.1 1.7 collective-permute-start.1
  688.8 9.2 %multiply_reduce_fusion.1 = f32[24,96,96,4]{2,1,3,0:T(8,128)S(1)} fusion(f32[24,96,96,4,4]{2,1,3,4,0:T(8,128)} %bitcast.121, f32[24,96,96,4]{2,1,3,0:T(8,128)} %copy-done), kind=kLoop, calls=%fused_computation.18 | loop fusion | flops 6193152 | bytes 21233664
  698.0 2.6 fusion.34
  700.6 4.6 reshape.99
  705.2 60.1 %collective-permute-done.1 = f32[4,24,9216]{2,1,0:T(8,128)} collective-permute-done((f32[4,24,9216]{2,1,0:T(8,128)}, f32[4,24,9216]{2,1,0:T(8,128)}, u32[]{:S(2)}, u32[]{:S(2)}) %collective-permute-start.1) | collective-permute-done | bytes 3538976 | tf_op jit(solution)/shard_map/ppermute | solution.py:15
  765.3 4.2 add.39
  (1 shorter events, 0.0 us)
Async XLA Ops:
  0.0 44.9 %collective-permute-start = (bf16[4,24,9216]{2,1,0:T(8,128)(2,1)}, bf16[4,24,9216]{2,1,0:T(8,128)(2,1)}, u32[]{:S(2)}, u32[]{:S(2)}) collective-permute-start(bf16[4,24,9216]{2,1,0:T(8,128)(2,1)} %param.2), channel_id=1, source_target_pairs={{28,0},{0,4},{4,8},{8,12},{12,16},{16,20},{20,24},{24,28},{29,1},{... | collective-permute-start | bytes 5308424 | tf_op jit(solution)/shard_map/ppermute | solution.py:15
  49.2 2.2 copy-start
  116.8 7.7 copy-start.1
  116.8 213.0 %all-to-all-start = ((bf16[24,96,96,2,16]{2,3,4,0,1:T(2,128)(2,1)}), bf16[24,96,96,2,16]{2,3,4,0,1:T(2,128)(2,1)}, u32[]{:S(2)}, u32[]{:S(2)}) async-start(bf16[24,96,96,2,16]{2,3,4,0,1:T(2,128)(2,1)} %copy.16), calls=%async_computation | async-start | bytes 37748736 | tf_op jit(solution)/shard_map/all_to_all | solution.py:68
  687.1 78.2 %collective-permute-start.1 = (f32[4,24,9216]{2,1,0:T(8,128)}, f32[4,24,9216]{2,1,0:T(8,128)}, u32[]{:S(2)}, u32[]{:S(2)}) collective-permute-start(f32[4,24,9216]{2,1,0:T(8,128)} %reshape.100), channel_id=1, source_target_pairs={{4,0},{8,4},{12,8},{16,12},{20,16},{24,20},{28,24},{0,28},{5,1},{9... | collective-permute-start | bytes 10616840 | tf_op jit(solution)/shard_map/ppermute | solution.py:15
where the time goes:
time: 772 us; the launch traced here: 769 us
  waiting for transfers between devices  299 us (39%)
  blocking collectives  210 us (27%)
  local copies, waits for them, and re-layouts  136 us (18%)
  matrix products  71.7 us (9%)
  other arithmetic  39 us (5%)
  starting transfers between devices  12.4 us (2%)
    all_to_all x1, blocking collectives, local(): lax.all_to_all(back_x, 'grid', split_axis=0, concat_axis=1, tiled=True)  210 us
    all_to_all x1, waiting for transfers between devices, local(): lax.all_to_all(along_zy, 'grid', split_axis=1, concat_axis=0, tiled=True)  204 us
    ppermute x2, waiting for transfers between devices, passed_along(): return lax.ppermute(block, axis, route)  95 us
    dot_general x3, matrix products, contract(): return jnp.einsum(form, table, operand, preferred_element_type=jnp.float32)  71.7 us
    convert_element_type x1, local copies, waits for them, and re-layouts, first_passes(): return contract('dcjy,xykcp->xjkdp', forward, along_z).astype(jnp.bfloat16)  42.2 us
    convert_element_type x1, local copies, waits for them, and re-layouts, middle_passes(): contract('dcxg,gjkcp->xjkdp', backward, spectrum).astype(jnp.bfloat16)  42.2 us
    all_to_all x2, local copies, waits for them, and re-layouts, local(): lax.all_to_all(along_zy, 'grid', split_axis=1, concat_axis=0, tiled=True)  19.2 us
    unnamed x2, other arithmetic  18.4 us
  transfers between devices with their start and end apart: 3, of which 3 were waited for; matrix products, arithmetic and copies ran while one was open for 3% of the time, Pallas kernels for 0%

commit v1 on v0

v1 whole, which is shorter than its diff:
```python
import functools

import jax
import jax.numpy as jnp
import ml_dtypes
import numpy as np
from jax import lax
from jax.experimental import pallas as pl
from jax.experimental.pallas import tpu as pltpu
from jax.sharding import PartitionSpec as P

DIST = 1
LANES = 128
TILES = 3
GROUPS = 3
UNROLL = 8
BF = jnp.bfloat16
F32 = jnp.float32
VMEM_BYTES = 60 * 1024 * 1024


def dot(a, b):
    return jnp.dot(a, b, preferred_element_type=F32)


def half(a):
    return np.asarray(a, np.float32).astype(ml_dtypes.bfloat16)


def complex_tables(count):
    j = np.arange(count)
    angles = (j[:, None] * j[None, :] % count).astype(np.float32) * np.float32(2.0 * np.pi / count)
    cosine = half(np.cos(angles)).astype(np.float32)
    sine = half(np.sin(angles)).astype(np.float32)
    forward = np.block([[cosine, sine], [-sine, cosine]])
    backward = np.block([[cosine, -sine], [sine, cosine]])
    return forward, backward


def line_spans(count):
    per = TILES * LANES // count
    lines = [(s * count // LANES, -(-(s + 1) * count // LANES)) for s in range(per)]
    tiles = [(t * LANES // count, -(-(t + 1) * LANES // count)) for t in range(TILES)]
    return lines, tiles


def z_tables(count):
    forward, backward = complex_tables(count)
    lines, tiles = line_spans(count)
    cut, lay = [], []
    for s, (t0, t1) in enumerate(lines):
        w = np.zeros((2, (t1 - t0) * LANES, 2, LANES), np.float32)
        first = s * count - t0 * LANES
        for c in range(2):
            for d in range(2):
                w[c, first:first + count, d, :count] = forward[d * count:(d + 1) * count, c * count:(c + 1) * count].T
        cut.append(half(w.reshape(-1, 2 * LANES)))
    for t, (s0, s1) in enumerate(tiles):
        w = np.zeros((s1 - s0, 2, LANES, 2, LANES), np.float32)
        for s in range(s0, s1):
            for z in range(count):
                lane = s * count + z - t * LANES
                if 0 <= lane < LANES:
                    for c in range(2):
                        for d in range(2):
                            w[s - s0, c, :count, d, lane] = backward[d * count + z, c * count:(c + 1) * count]
        lay.append(half(w.reshape(-1, 2 * LANES)))
    return cut, lay


def piece_planes(count, ga, gb, device):
    rows = count // (ga * gb)
    ai, bi = divmod(device, gb)
    owners = [((ai + s) % ga) * gb + (bi + t) % gb for s in range(ga) for t in range(gb)]
    return np.concatenate([np.arange(o * rows, (o + 1) * rows) for o in owners])


def device_tables(count, ga, gb):
    forward, backward = complex_tables(count)
    near = count // ga
    fwd, bwd, mirror = [], [], []
    for device in range(ga * gb):
        planes = piece_planes(count, ga, gb, device)
        fwd.append(np.concatenate([forward[:, planes], forward[:, count + planes]], axis=1))
        bwd.append(np.concatenate([backward[planes[:near]], backward[count + planes[:near]]], axis=0))
        place = np.eye(count, dtype=np.float32)[:, planes]
        flip = place[(-np.arange(count)) % count]
        mirror.append(np.concatenate([place, flip], axis=1))
    return half(np.stack(fwd)), half(np.stack(bwd)), half(np.stack(mirror))


def line_selectors(count):
    lines, _ = line_spans(count)
    picks = []
    for s, (t0, t1) in enumerate(lines):
        w = np.zeros(((t1 - t0) * LANES, 2, LANES), np.float32)
        for z in range(count):
            w[s * count + z - t0 * LANES, 0, z] = 1
            w[s * count + z - t0 * LANES, 1, (-z) % count] = 1
        picks.append(half(w.reshape(-1, 2 * LANES)))
    return picks


def kernel_body(count, n, *refs):
    pieces, mirror = refs[:n], refs[n]
    lines, _ = line_spans(count)
    picks = refs[n + 1:n + 1 + len(lines)]
    out_ref, cut_ref = refs[n + 1 + len(lines):]
    per = len(lines)
    width = TILES * LANES

    def cut(group, carry):
        lanes = pl.ds(pl.multiple_of(group * width, LANES), width)
        k = jnp.concatenate([r[:, lanes].astype(F32) for r in pieces], axis=0).astype(BF)
        for s, (t0, t1) in enumerate(lines):
            cut_ref[group * per + s] = dot(k[:, t0 * LANES:t1 * LANES], picks[s][...]).astype(BF)
        return carry

    lax.fori_loop(0, count // per, cut, 0)

    def join(step, carry):
        for u in range(4):
            gx = step * 4 + u
            back = lax.rem(count - gx, count)
            both = jnp.concatenate([cut_ref[gx][:, :LANES], cut_ref[back][:, LANES:]], axis=0)
            out_ref[gx] = dot(mirror[...], both) * (0.5 / count**3)
        return carry

    lax.fori_loop(0, count // 4, join, 0)


def whole_kernel(pieces, mirror, count):
    picks = line_selectors(count)
    vmem = pl.BlockSpec(memory_space=pltpu.VMEM)
    ins = [*pieces, mirror, *picks]
    return pl.pallas_call(
        functools.partial(kernel_body, count, len(pieces)),
        out_shape=jax.ShapeDtypeStruct((count, count, LANES), F32),
        in_specs=[vmem] * len(ins),
        out_specs=vmem,
        scratch_shapes=[pltpu.VMEM((count, count, 2 * LANES), BF)],
        compiler_params=pltpu.CompilerParams(vmem_limit_bytes=VMEM_BYTES),
        name="symmetric_kernel",
    )(*ins)


def unit_body(count, n, near, has_prev, *refs):
    refs = list(refs)

    def take(k):
        return [refs.pop(0) for _ in range(k)]

    lines, tiles = line_spans(count)
    per = len(lines)
    width = TILES * LANES
    a_refs, b_refs = take(n), take(n)
    k_ref, x_fwd, x_bwd, y_fwd, y_bwd = take(5)
    cut, lay = take(per), take(TILES)
    prev = take(1)[0] if has_prev else None
    sent_refs, kept_ref = take(near), take(1)[0]
    s_ref, r_ref = take(2)
    ra, rows = a_refs[0].shape[:2]
    planes = near * rows
    steps = count // (per * GROUPS)

    def stack(pieces):
        return jnp.concatenate([p.astype(F32) for p in pieces], axis=0)

    def forward(step, carry):
        rho = [[], []]
        for g in range(GROUPS):
            lanes = pl.ds(pl.multiple_of((step * GROUPS + g) * width, LANES), width)
            b = stack([r[:, lanes] for r in b_refs])
            for k in range(2):
                if k < ra:
                    rho[k].append((stack([r[k, :, lanes] for r in a_refs]) * b).astype(BF))
                else:
                    rho[k].append(jnp.zeros((count, width), BF))
        rho = [jnp.concatenate(r, axis=0) for r in rho]
        along = []
        for s, (t0, t1) in enumerate(lines):
            lhs = jnp.concatenate([r[:, t0 * LANES:t1 * LANES] for r in rho], axis=1)
            along.append(dot(lhs, cut[s][...]).astype(BF))
        for g in range(GROUPS):
            for s in range(0, per, 2):
                pair = []
                for e in range(2):
                    w = along[s + e][g * count:(g + 1) * count]
                    pair.append(jnp.concatenate([w[:, :LANES], w[:, LANES:]], axis=0))
                out = dot(x_fwd[...], jnp.concatenate(pair, axis=1))
                y = (step * GROUPS + g) * per + s
                for e in range(2):
                    s_ref[pl.ds(y + e, 2 * count, count), :] = out[:, e * LANES:(e + 1) * LANES]
        return carry

    lax.fori_loop(0, steps, forward, 0)

    def plane_pair(ref, first, second):
        return jnp.concatenate(
            [
                jnp.concatenate(
                    [ref[pl.ds(pl.multiple_of((c * count + i) * count, 8), count), :].astype(BF) for c in range(2)],
                    axis=0,
                )
                for i in (first, second)
            ],
            axis=1,
        )

    def middle(step, carry):
        firsts = [(step * UNROLL + u) * 2 for u in range(UNROLL)]
        summed = [dot(y_fwd[...], plane_pair(s_ref, gx, gx + 1)) for gx in firsts]
        spectra = []
        for gx, value in zip(firsts, summed):
            scale = jnp.concatenate([k_ref[gx], k_ref[gx + 1]], axis=1)
            spectra.append(
                jnp.concatenate([(value[:count] * scale).astype(BF), (value[count:] * scale).astype(BF)], axis=0)
            )
        backs = [dot(y_bwd[...], spectrum) for spectrum in spectra]
        for gx, value in zip(firsts, backs):
            for e in range(2):
                r_ref[pl.ds(gx + e, 2 * count, count), :] = value[:, e * LANES:(e + 1) * LANES]
        return carry

    lax.fori_loop(0, count // (2 * UNROLL), middle, 0)

    def backward(step, carry):
        columns = []
        for g in range(GROUPS):
            row = []
            for s in range(0, per, 2):
                y = (step * GROUPS + g) * per + s
                out = dot(x_bwd[...], plane_pair(r_ref, y, y + 1)).astype(BF)
                for e in range(2):
                    w = out[:, e * LANES:(e + 1) * LANES]
                    row.append(jnp.concatenate([w[:planes], w[planes:]], axis=1))
            columns.append(row)
        for t, (s0, s1) in enumerate(tiles):
            lhs = jnp.concatenate([jnp.concatenate(row[s0:s1], axis=1) for row in columns], axis=0)
            potential = dot(lhs, lay[t][...])
            for g in range(GROUPS):
                lanes = pl.ds(pl.multiple_of((step * GROUPS + g) * width + t * LANES, LANES), LANES)
                v = potential[g * planes:(g + 1) * planes]
                b = stack([r[:, lanes] for r in b_refs[:near]])
                sent = None
                for k in range(ra):
                    minus = -v[:, k * LANES:(k + 1) * LANES]
                    term = minus * stack([r[k, :, lanes] for r in a_refs[:near]])
                    sent = term if sent is None else sent + term
                    kept = minus * b
                    for p in range(near):
                        piece = kept[p * rows:(p + 1) * rows]
                        if has_prev:
                            piece = piece + prev[p, k, :, lanes]
                        kept_ref[p, k, :, lanes] = piece
                for p in range(near):
                    sent_refs[p][:, lanes] = sent[p * rows:(p + 1) * rows].astype(BF)
        return carry

    lax.fori_loop(0, steps, backward, 0)


def unit(a, b, kern, x_fwd, x_bwd, near, prev):
    count = kern.shape[0]
    n = len(a)
    ra, rows, width = a[0].shape
    y_fwd, y_bwd = (half(t) for t in complex_tables(count))
    cut, lay = z_tables(count)
    ins = [*a, *b, kern, x_fwd, x_bwd, y_fwd, y_bwd, *cut, *lay] + ([] if prev is None else [prev])
    vmem = pl.BlockSpec(memory_space=pltpu.VMEM)
    outs = pl.pallas_call(
        functools.partial(unit_body, count, n, near, prev is not None),
        out_shape=[jax.ShapeDtypeStruct((rows, width), BF)] * near
        + [jax.ShapeDtypeStruct((near, ra, rows, width), F32)],
        in_specs=[vmem] * len(ins),
        out_specs=[vmem] * (near + 1),
        scratch_shapes=[pltpu.VMEM((2 * count * count, LANES), F32)] * 2,
        compiler_params=pltpu.CompilerParams(vmem_limit_bytes=VMEM_BYTES),
        cost_estimate=pl.CostEstimate(flops=10 * 10**9, bytes_accessed=16 * 10**6, transcendentals=0),
        name="pair_potentials",
    )(*ins)
    return outs[:near], outs[near]


def split_of(n):
    gb = 1
    while gb * gb < n and gb < 4:
        gb *= 2
    return n // gb, gb


def local(orbitals, kernel, *, ga, gb):
    band_count, rows, width = orbitals.shape
    n = ga * gb
    count = rows * n
    na = band_count // gb
    blocks = lax.axis_size("band")
    me = lax.axis_index("grid")
    ai, bi = me // gb, me % gb

    def hop(x, distance):
        return lax.ppermute(x, "band", [(i, (i + distance) % blocks) for i in range(blocks)])

    def to_a(x, s):
        return lax.ppermute(x, "grid", [(((i // gb + s) % ga) * gb + i % gb, i) for i in range(n)])

    def to_b(x, t):
        return lax.ppermute(x, "grid", [((i // gb) * gb + (i % gb + t) % gb, i) for i in range(n)])

    def bands_of(core):
        return lax.dynamic_slice_in_dim(orbitals, core * na, na, 0)

    fwd, bwd, mirror = device_tables(count, ga, gb)
    x_fwd, x_bwd, mirror = (lax.dynamic_index_in_dim(jnp.asarray(t), me, 0, False) for t in (fwd, bwd, mirror))

    a = {(0, 0): bands_of(bi)}
    for t in range(1, gb):
        a[0, t] = to_b(bands_of((bi + gb - t) % gb), t)
    hops = [hop(orbitals[j], DIST) for j in range(band_count)]
    for s in range(1, ga):
        for t in range(gb):
            a[s, t] = to_a(a[0, t], s)
    k = {(0, 0): kernel.astype(BF)}
    for s in range(1, ga):
        k[s, 0] = to_a(k[0, 0], s)
    for s in range(ga):
        for t in range(1, gb):
            k[s, t] = to_b(k[s, 0], t)
    order = [(s, t) for s in range(ga) for t in range(gb)]
    kern = whole_kernel([k[o] for o in order], mirror, count)

    kept = None
    returned = []
    for j in range(band_count):
        b = {(0, 0): hops[j]}
        for s in range(1, ga):
            b[s, 0] = to_a(b[0, 0], s)
        for s in range(ga):
            for t in range(1, gb):
                b[s, t] = to_b(b[s, 0], t)
        sent, kept = unit([a[o] for o in order], [b[o] for o in order], kern, x_fwd, x_bwd, gb, kept)
        total = sent[0].astype(F32)
        for t in range(1, gb):
            total = total + to_b(sent[t], gb - t).astype(F32)
        returned.append(hop(total.astype(BF), -DIST))

    shares = [kept[0]] + [to_b(kept[t].astype(BF), gb - t).astype(F32) for t in range(1, gb)]
    blocks_kept = []
    for block in range(gb):
        which = (bi - block + gb) % gb
        value = shares[0]
        for t in range(1, gb):
            value = jnp.where(which == t, shares[t], value)
        blocks_kept.append(value)
    return jnp.concatenate(blocks_kept, axis=0) + jnp.stack(returned).astype(F32)


def solution(mesh):
    ga, gb = split_of(mesh.shape["grid"])
    placed = (P("band", "grid", None), P("grid", None))
    return jax.shard_map(
        functools.partial(local, ga=ga, gb=gb),
        mesh=mesh,
        in_specs=placed,
        out_specs=P("band", "grid", None),
        check_vma=False,
    )
```

time: 772 us -> 247 us (0.32)
  waiting for transfers between devices: 299 us -> 84.5 us
  blocking collectives: 210 us -> 0 us
  local copies, waits for them, and re-layouts: 136 us -> 8.89 us
  Pallas kernels: 0 us -> 127 us
  matrix products: 71.7 us -> 0 us
  other arithmetic: 39 us -> 4.14 us
  starting transfers between devices: 12.4 us -> 22 us
    all_to_all x1 -> x0, blocking collectives: 210 us -> none  [local(): lax.all_to_all(back_x, 'grid', split_axis=0, concat_axis=1, tiled=True)]
    all_to_all x1 -> x0, waiting for transfers between devices: 204 us -> none  [local(): lax.all_to_all(along_zy, 'grid', split_axis=1, concat_axis=0, tiled=True)]
    pallas_call x0 -> x5, Pallas kernels: none -> 127 us  [the longest x4 113 us: unit(): pl.pallas_call(functools.partial(unit_body, count, n, near, prev is not N...]
    convert_element_type x2 -> x1, local copies, waits for them, and re-layouts: 84.4 us -> 1.56 us  [local(): kept[t].astype(BF)]
    dot_general x3 -> x0, matrix products: 71.7 us -> none  [contract(): return jnp.einsum(form, table, operand, preferred_element_type=jnp.float32)]
    all_to_all x4 -> x0, local copies, waits for them, and re-layouts: 31.1 us -> none  [the longest x2 19.2 us: local(): lax.all_to_all(along_zy, 'grid', split_axis=1, concat_axis=0, tiled=True)]
    reshape x6 -> x0, local copies, waits for them, and re-layouts: 18.9 us -> none  [the longest x1 6.07 us: local(): sent.transpose(3, 0, 1, 2).reshape(band_count, plane_count, count * count)]
    unnamed x2 -> x0, other arithmetic: 18.4 us -> none
  transfers between devices with their start and end apart: 3 -> 31, of which waited for: 3 -> 11; matrix products, arithmetic and copies ran while one was open for 3% -> 3% of each run, Pallas kernels for 0% -> 51%
where the time goes in v1:
time: 247 us
  Pallas kernels  127 us (51%)
  waiting for transfers between devices  84.5 us (34%)
  starting transfers between devices  22 us (9%)
  local copies, waits for them, and re-layouts  8.89 us (4%)
  other arithmetic  4.14 us (2%)
    pallas_call x4, Pallas kernels, unit(): pl.pallas_call(functools.partial(unit_body, count, n, near, prev is not N...  113 us
    ppermute x8, waiting for transfers between devices, hop(): lax.ppermute(x, 'band', [(i, (i + distance) % blocks) for i in range(bloc...  65.1 us
    ppermute x7, waiting for transfers between devices, to_a(): lax.ppermute(x, 'grid', [((i // gb + s) % ga * gb + i % gb, i) for i in r...  19.4 us
    pallas_call x1, Pallas kernels, whole_kernel(): pl.pallas_call(functools.partial(kernel_body, count, len(pieces)), out_sh...  13.8 us
    ppermute x8, starting transfers between devices, hop(): lax.ppermute(x, 'band', [(i, (i + distance) % blocks) for i in range(bloc...  10.5 us
    ppermute x7, starting transfers between devices, to_a(): lax.ppermute(x, 'grid', [((i // gb + s) % ga * gb + i % gb, i) for i in r...  7.89 us
  transfers between devices with their start and end apart: 31, of which 11 were waited for; matrix products, arithmetic and copies ran while one was open for 3% of the time, Pallas kernels for 51%

profile of v1, /device:TPU:0, one launch (start us, length us, event | category | flops | bytes accessed | tf_op | source)
XLA Modules:
  0.0 246.7 jit_solution(9828177697563737194)
XLA Ops:
  0.0 1.2 convert_element_type.49.refs_0_
  1.2 3.0 %collective-permute-start.8 = (bf16[24,9216]{1,0:T(8,128)(2,1)S(1)}, bf16[24,9216]{1,0:T(8,128)(2,1)S(1)}, u32[]{:S(2)}, u32[]{:S(2)}) collective-permute-start(bf16[24,9216]{1,0:T(8,128)(2,1)S(1)} %convert_element_type.49.refs_0_), channel_id=1, source_target_pairs={{2,0},{3,1},{0,2},{1,3},{6,4},{7,5},{4,6},{5,7},{10,8},{11,9},{8,1... | collective-permute-start | bytes 1327112 | tf_op jit(solution)/shard_map/ppermute | solution.py:305
  4.2 1.7 constant_dynamic-slice_fusion
  5.9 0.6 collective-permute-start
  6.6 1.6 collective-permute-start.18
  8.2 1.5 collective-permute-start.14
  9.7 4.7 %collective-permute-done.8.refs_2_ = bf16[24,9216]{1,0:T(8,128)(2,1)S(1)} collective-permute-done((bf16[24,9216]{1,0:T(8,128)(2,1)S(1)}, bf16[24,9216]{1,0:T(8,128)(2,1)S(1)}, u32[]{:S(2)}, u32[]{:S(2)}) %collective-permute-start.8) | collective-permute-done | bytes 442400 | tf_op jit(solution)/shard_map/ppermute | solution.py:305
  14.4 1.8 collective-permute-start.10
  16.2 1.6 collective-permute-start.1
  17.7 4.7 %collective-permute-done.18.refs_4_ = bf16[24,9216]{1,0:T(8,128)(2,1)} collective-permute-done((bf16[24,9216]{1,0:T(8,128)(2,1)S(1)}, bf16[24,9216]{1,0:T(8,128)(2,1)}, u32[]{:S(2)}, u32[]{:S(2)}) %collective-permute-start.18) | collective-permute-done | bytes 442400 | tf_op jit(solution)/shard_map/ppermute | solution.py:302
  22.5 9.5 %collective-permute-done.14.refs_4_ = bf16[24,9216]{1,0:T(8,128)(2,1)} collective-permute-done((bf16[24,9216]{1,0:T(8,128)(2,1)S(1)}, bf16[24,9216]{1,0:T(8,128)(2,1)}, u32[]{:S(2)}, u32[]{:S(2)}) %collective-permute-start.14) | collective-permute-done | bytes 442400 | tf_op jit(solution)/shard_map/ppermute | solution.py:302
  32.0 9.5 %collective-permute-done.10.refs_4_ = bf16[24,9216]{1,0:T(8,128)(2,1)} collective-permute-done((bf16[24,9216]{1,0:T(8,128)(2,1)S(1)}, bf16[24,9216]{1,0:T(8,128)(2,1)}, u32[]{:S(2)}, u32[]{:S(2)}) %collective-permute-start.10) | collective-permute-done | bytes 442400 | tf_op jit(solution)/shard_map/ppermute | solution.py:302
  41.4 0.4 collective-permute-start.20
  41.8 1.7 collective-permute-start.2
  43.5 6.8 %collective-permute-done.3.refs_4_ = bf16[24,9216]{1,0:T(8,128)(2,1)S(1)} collective-permute-done((bf16[24,9216]{1,0:T(8,128)(2,1)S(1)}, bf16[24,9216]{1,0:T(8,128)(2,1)S(1)}, u32[]{:S(2)}, u32[]{:S(2)}) %collective-permute-start.3) | collective-permute-done | bytes 442400 | tf_op jit(solution)/shard_map/ppermute | solution.py:302
  50.3 0.6 collective-permute-start.16
  50.9 4.0 %collective-permute-done.20.refs_6_ = bf16[24,9216]{1,0:T(8,128)(2,1)} collective-permute-done((bf16[24,9216]{1,0:T(8,128)(2,1)}, bf16[24,9216]{1,0:T(8,128)(2,1)}, u32[]{:S(2)}, u32[]{:S(2)}) %collective-permute-start.20) | collective-permute-done | bytes 442400 | tf_op jit(solution)/shard_map/ppermute | solution.py:305
  54.9 1.5 dynamic-slice_bitcast_fusion.refs_9_
  56.4 1.5 dynamic-slice_bitcast_fusion.1
  57.9 13.8 %symmetric_kernel.1.refs_8_ = f32[96,96,128]{2,1,0:T(8,128)} custom-call(bf16[24,9216]{1,0:T(8,128)(2,1)} %copy-done.2, bf16[24,9216]{1,0:T(8,128)(2,1)} %copy-done.9, bf16[24,9216]{1,0:T(8,128)(2,1)} %copy-done.8, bf16[24,9216]{1,0:T(8,128)(2,1)} %copy-done.10, bf16[96,192]{1,0:T(8,128)(2,1)} %get-tuple-element.38.refs_4_, ...), custom_call_target="tpu_custom_call" | custom-call | tf_op jit(solution)/shard_map/symmetric_kernel/pallas_call | solution.py:136
  71.7 0.5 collective-permute-start.15
  72.2 0.4 collective-permute-start.12
  72.5 10.8 %collective-permute-done.16.refs_6_ = bf16[24,9216]{1,0:T(8,128)(2,1)} collective-permute-done((bf16[24,9216]{1,0:T(8,128)(2,1)}, bf16[24,9216]{1,0:T(8,128)(2,1)}, u32[]{:S(2)}, u32[]{:S(2)}) %collective-permute-start.16) | collective-permute-done | bytes 442400 | tf_op jit(solution)/shard_map/ppermute | solution.py:305
  83.3 0.4 collective-permute-start.5
  83.9 27.3 %pair_potentials.4 = (bf16[24,9216]{1,0:T(8,128)(2,1)}, bf16[24,9216]{1,0:T(8,128)(2,1)}, f32[2,2,24,9216]{3,2,1,0:T(8,128)}) custom-call(bf16[2,24,9216]{2,1,0:T(8,128)(2,1)} %copy-done.3, bf16[2,24,9216]{2,1,0:T(8,128)(2,1)} %copy-done.11, bf16[2,24,9216]{2,1,0:T(8,128)(2,1)} %collective-permute-done.1.refs_2_, ...), custom_call_target="tpu_custom_call" | custom-call | flops 10000000000 | bytes 16000000 | tf_op jit(solution)/shard_map/pair_potentials/pallas_call | solution.py:271
  111.2 0.4 collective-permute-start.4
  111.8 0.3 collective-permute-start.6
  112.1 0.8 copy-done.19
  113.1 28.6 %pair_potentials.5 = (bf16[24,9216]{1,0:T(8,128)(2,1)}, bf16[24,9216]{1,0:T(8,128)(2,1)}, f32[2,2,24,9216]{3,2,1,0:T(8,128)}) custom-call(bf16[2,24,9216]{2,1,0:T(8,128)(2,1)} %copy-done.3, bf16[2,24,9216]{2,1,0:T(8,128)(2,1)} %copy-done.11, bf16[2,24,9216]{2,1,0:T(8,128)(2,1)} %collective-permute-done.1.refs_2_, ...), custom_call_target="tpu_custom_call" | custom-call | flops 10000000000 | bytes 16000000 | tf_op jit(solution)/shard_map/pair_potentials/pallas_call | solution.py:271
  141.7 0.4 collective-permute-start.25
  142.0 0.4 copy-done.16
  142.4 0.4 copy-done.20
  142.8 28.6 %pair_potentials.6 = (bf16[24,9216]{1,0:T(8,128)(2,1)}, bf16[24,9216]{1,0:T(8,128)(2,1)}, f32[2,2,24,9216]{3,2,1,0:T(8,128)}) custom-call(bf16[2,24,9216]{2,1,0:T(8,128)(2,1)} %copy-done.3, bf16[2,24,9216]{2,1,0:T(8,128)(2,1)} %copy-done.11, bf16[2,24,9216]{2,1,0:T(8,128)(2,1)} %collective-permute-done.1.refs_2_, ...), custom_call_target="tpu_custom_call" | custom-call | flops 10000000000 | bytes 16000000 | tf_op jit(solution)/shard_map/pair_potentials/pallas_call | solution.py:271
  171.6 0.8 copy-done.15
  172.5 28.7 %pair_potentials.7 = (bf16[24,9216]{1,0:T(8,128)(2,1)}, bf16[24,9216]{1,0:T(8,128)(2,1)}, f32[2,2,24,9216]{3,2,1,0:T(8,128)}) custom-call(bf16[2,24,9216]{2,1,0:T(8,128)(2,1)} %copy-done.3, bf16[2,24,9216]{2,1,0:T(8,128)(2,1)} %copy-done.11, bf16[2,24,9216]{2,1,0:T(8,128)(2,1)} %collective-permute-done.1.refs_2_, ...), custom_call_target="tpu_custom_call" | custom-call | flops 10000000000 | bytes 16000000 | tf_op jit(solution)/shard_map/pair_potentials/pallas_call | solution.py:271
  201.3 0.3 collective-permute-start.29
  201.6 1.6 fusion
  203.2 0.3 collective-permute-start.22
  203.6 2.1 collective-permute-start.24
  205.8 1.5 collective-permute-start.26
  207.4 0.5 collective-permute-start.28
  208.1 1.5 collective-permute-start.30
  209.6 0.3 convert_select_fusion.1
  209.9 6.8 %collective-permute-done.24 = bf16[24,9216]{1,0:T(8,128)(2,1)S(1)} collective-permute-done((bf16[24,9216]{1,0:T(8,128)(2,1)S(1)}, bf16[24,9216]{1,0:T(8,128)(2,1)S(1)}, u32[]{:S(2)}, u32[]{:S(2)}) %collective-permute-start.24) | collective-permute-done | bytes 442400 | tf_op jit(solution)/shard_map/ppermute | solution.py:302
  216.7 9.5 %collective-permute-done.26 = bf16[24,9216]{1,0:T(8,128)(2,1)S(1)} collective-permute-done((bf16[24,9216]{1,0:T(8,128)(2,1)S(1)}, bf16[24,9216]{1,0:T(8,128)(2,1)S(1)}, u32[]{:S(2)}, u32[]{:S(2)}) %collective-permute-start.26) | collective-permute-done | bytes 442400 | tf_op jit(solution)/shard_map/ppermute | solution.py:302
  226.1 9.5 %collective-permute-done.28 = bf16[24,9216]{1,0:T(8,128)(2,1)S(1)} collective-permute-done((bf16[24,9216]{1,0:T(8,128)(2,1)S(1)}, bf16[24,9216]{1,0:T(8,128)(2,1)S(1)}, u32[]{:S(2)}, u32[]{:S(2)}) %collective-permute-start.28) | collective-permute-done | bytes 442400 | tf_op jit(solution)/shard_map/ppermute | solution.py:302
  235.6 8.8 %collective-permute-done.30 = bf16[24,9216]{1,0:T(8,128)(2,1)S(1)} collective-permute-done((bf16[24,9216]{1,0:T(8,128)(2,1)S(1)}, bf16[24,9216]{1,0:T(8,128)(2,1)S(1)}, u32[]{:S(2)}, u32[]{:S(2)}) %collective-permute-start.30) | collective-permute-done | bytes 442400 | tf_op jit(solution)/shard_map/ppermute | solution.py:302
  244.5 2.2 maximum_add_fusion
  (73 shorter events, 1.7 us)
Async XLA Ops:
  1.2 4.7 %copy-start.2 = (bf16[24,9216]{1,0:T(8,128)(2,1)}, bf16[24,9216]{1,0:T(8,128)(2,1)S(1)}, u32[]{:S(2)}) copy-start(bf16[24,9216]{1,0:T(8,128)(2,1)S(1)} %convert_element_type.49.refs_0_) | copy-start | bytes 1327108
  1.2 13.2 %collective-permute-start.8 = (bf16[24,9216]{1,0:T(8,128)(2,1)S(1)}, bf16[24,9216]{1,0:T(8,128)(2,1)S(1)}, u32[]{:S(2)}, u32[]{:S(2)}) collective-permute-start(bf16[24,9216]{1,0:T(8,128)(2,1)S(1)} %convert_element_type.49.refs_0_), channel_id=1, source_target_pairs={{2,0},{3,1},{0,2},{1,3},{6,4},{7,5},{4,6},{5,7},{10,8},{11,9},{8,1... | collective-permute-start | bytes 1327112 | tf_op jit(solution)/shard_map/ppermute | solution.py:305
  4.2 11.9 %collective-permute-start.7 = (bf16[24,9216]{1,0:T(8,128)(2,1)S(1)}, bf16[24,9216]{1,0:T(8,128)(2,1)S(1)}, u32[]{:S(2)}, u32[]{:S(2)}) collective-permute-start(bf16[24,9216]{1,0:T(8,128)(2,1)S(1)} %convert_element_type.49.refs_0_), channel_id=1, source_target_pairs={{1,0},{0,1},{3,2},{2,3},{5,4},{4,5},{7,6},{6,7},{9,8},{8,9},{11,10... | collective-permute-start | bytes 1327112 | tf_op jit(solution)/shard_map/ppermute | solution.py:308
  4.2 2.3 copy-start
  5.9 10.2 %copy-start.3 = (bf16[2,24,9216]{2,1,0:T(8,128)(2,1)}, bf16[2,24,9216]{2,1,0:T(8,128)(2,1)S(1)}, u32[]{:S(2)}) copy-start(bf16[2,24,9216]{2,1,0:T(8,128)(2,1)S(1)} %get-tuple-element.36.refs_0_) | copy-start | bytes 2654212
  5.9 35.9 %collective-permute-start = (bf16[2,24,9216]{2,1,0:T(8,128)(2,1)S(1)}, bf16[2,24,9216]{2,1,0:T(8,128)(2,1)S(1)}, u32[]{:S(2)}, u32[]{:S(2)}) collective-permute-start(bf16[2,24,9216]{2,1,0:T(8,128)(2,1)S(1)} %get-tuple-element.35), channel_id=1, source_target_pairs={{1,0},{0,1},{3,2},{2,3},{5,4},{4,5},{7,6},{6,7},{9,8},{8,9},{11,10... | collective-permute-start | bytes 2654216 | tf_op jit(solution)/shard_map/ppermute | solution.py:308
  6.6 15.8 %collective-permute-start.18 = (bf16[24,9216]{1,0:T(8,128)(2,1)S(1)}, bf16[24,9216]{1,0:T(8,128)(2,1)}, u32[]{:S(2)}, u32[]{:S(2)}) collective-permute-start(bf16[24,9216]{1,0:T(8,128)(2,1)S(1)} %get-tuple-element.31), channel_id=1, source_target_pairs={{0,4},{4,8},{8,12},{12,16},{16,20},{20,24},{24,28},{28,0},{1,5},{5... | collective-permute-start | bytes 1327112 | tf_op jit(solution)/shard_map/ppermute | solution.py:302
  8.2 23.7 %collective-permute-start.14 = (bf16[24,9216]{1,0:T(8,128)(2,1)S(1)}, bf16[24,9216]{1,0:T(8,128)(2,1)}, u32[]{:S(2)}, u32[]{:S(2)}) collective-permute-start(bf16[24,9216]{1,0:T(8,128)(2,1)S(1)} %get-tuple-element.34), channel_id=1, source_target_pairs={{0,4},{4,8},{8,12},{12,16},{16,20},{20,24},{24,28},{28,0},{1,5},{5... | collective-permute-start | bytes 1327112 | tf_op jit(solution)/shard_map/ppermute | solution.py:302
  14.4 43.5 %copy-start.8 = (bf16[24,9216]{1,0:T(8,128)(2,1)}, bf16[24,9216]{1,0:T(8,128)(2,1)S(1)}, u32[]{:S(2)}) copy-start(bf16[24,9216]{1,0:T(8,128)(2,1)S(1)} %collective-permute-done.8.refs_2_) | copy-start | bytes 1327108
  14.4 27.0 %collective-permute-start.10 = (bf16[24,9216]{1,0:T(8,128)(2,1)S(1)}, bf16[24,9216]{1,0:T(8,128)(2,1)}, u32[]{:S(2)}, u32[]{:S(2)}) collective-permute-start(bf16[24,9216]{1,0:T(8,128)(2,1)S(1)} %get-tuple-element.32), channel_id=1, source_target_pairs={{0,4},{4,8},{8,12},{12,16},{16,20},{20,24},{24,28},{28,0},{1,5},{5... | collective-permute-start | bytes 1327112 | tf_op jit(solution)/shard_map/ppermute | solution.py:302
  16.2 41.7 %copy-start.9 = (bf16[24,9216]{1,0:T(8,128)(2,1)}, bf16[24,9216]{1,0:T(8,128)(2,1)S(1)}, u32[]{:S(2)}) copy-start(bf16[24,9216]{1,0:T(8,128)(2,1)S(1)} %collective-permute-done.7.refs_1_) | copy-start | bytes 1327108
  16.2 55.5 %collective-permute-start.1 = (bf16[2,24,9216]{2,1,0:T(8,128)(2,1)S(1)}, bf16[2,24,9216]{2,1,0:T(8,128)(2,1)}, u32[]{:S(2)}, u32[]{:S(2)}) collective-permute-start(bf16[2,24,9216]{2,1,0:T(8,128)(2,1)S(1)} %get-tuple-element.36.refs_0_), channel_id=1, source_target_pairs={{2,0},{3,1},{0,2},{1,3},{6,4},{7,5},{4,6},{5,7},{10,8},{11,9},{8,1... | collective-permute-start | bytes 2654216 | tf_op jit(solution)/shard_map/ppermute | solution.py:305
  22.5 27.8 %collective-permute-start.3 = (bf16[24,9216]{1,0:T(8,128)(2,1)S(1)}, bf16[24,9216]{1,0:T(8,128)(2,1)S(1)}, u32[]{:S(2)}, u32[]{:S(2)}) collective-permute-start(bf16[24,9216]{1,0:T(8,128)(2,1)S(1)} %get-tuple-element.33), channel_id=1, source_target_pairs={{0,4},{4,8},{8,12},{12,16},{16,20},{20,24},{24,28},{28,0},{1,5},{5... | collective-permute-start | bytes 1327112 | tf_op jit(solution)/shard_map/ppermute | solution.py:302
  32.0 18.3 %collective-permute-start.9 = (bf16[24,9216]{1,0:T(8,128)(2,1)S(1)}, bf16[24,9216]{1,0:T(8,128)(2,1)S(1)}, u32[]{:S(2)}, u32[]{:S(2)}) collective-permute-start(bf16[24,9216]{1,0:T(8,128)(2,1)S(1)} %collective-permute-done.8.refs_2_), channel_id=1, source_target_pairs={{1,0},{0,1},{3,2},{2,3},{5,4},{4,5},{7,6},{6,7},{9,8},{8,9},{11,10... | collective-permute-start | bytes 1327112 | tf_op jit(solution)/shard_map/ppermute | solution.py:308
  41.4 13.4 %collective-permute-start.20 = (bf16[24,9216]{1,0:T(8,128)(2,1)}, bf16[24,9216]{1,0:T(8,128)(2,1)}, u32[]{:S(2)}, u32[]{:S(2)}) collective-permute-start(bf16[24,9216]{1,0:T(8,128)(2,1)} %collective-permute-done.18.refs_4_), channel_id=1, source_target_pairs={{2,0},{3,1},{0,2},{1,3},{6,4},{7,5},{4,6},{5,7},{10,8},{11,9},{8,1... | collective-permute-start | bytes 1327112 | tf_op jit(solution)/shard_map/ppermute | solution.py:305
  41.8 42.1 %copy-start.11 = (bf16[2,24,9216]{2,1,0:T(8,128)(2,1)}, bf16[2,24,9216]{2,1,0:T(8,128)(2,1)S(1)}, u32[]{:S(2)}) copy-start(bf16[2,24,9216]{2,1,0:T(8,128)(2,1)S(1)} %collective-permute-done.refs_1_) | copy-start | bytes 2654212
  41.8 41.9 %collective-permute-start.2 = (bf16[2,24,9216]{2,1,0:T(8,128)(2,1)S(1)}, bf16[2,24,9216]{2,1,0:T(8,128)(2,1)}, u32[]{:S(2)}, u32[]{:S(2)}) collective-permute-start(bf16[2,24,9216]{2,1,0:T(8,128)(2,1)S(1)} %collective-permute-done.refs_1_), channel_id=1, source_target_pairs={{2,0},{3,1},{0,2},{1,3},{6,4},{7,5},{4,6},{5,7},{10,8},{11,9},{8,1... | collective-permute-start | bytes 2654216 | tf_op jit(solution)/shard_map/ppermute | solution.py:305
  50.3 60.9 %copy-start.12 = (bf16[24,9216]{1,0:T(8,128)(2,1)}, bf16[24,9216]{1,0:T(8,128)(2,1)S(1)}, u32[]{:S(2)}) copy-start(bf16[24,9216]{1,0:T(8,128)(2,1)S(1)} %collective-permute-done.3.refs_4_) | copy-start | bytes 1327108
  50.3 21.9 %collective-permute-start.19 = (bf16[24,9216]{1,0:T(8,128)(2,1)}, bf16[24,9216]{1,0:T(8,128)(2,1)}, u32[]{:S(2)}, u32[]{:S(2)}) collective-permute-start(bf16[24,9216]{1,0:T(8,128)(2,1)} %collective-permute-done.18.refs_4_), channel_id=1, source_target_pairs={{1,0},{0,1},{3,2},{2,3},{5,4},{4,5},{7,6},{6,7},{9,8},{8,9},{11,10... | collective-permute-start | bytes 1327112 | tf_op jit(solution)/shard_map/ppermute | solution.py:308
  50.3 7.6 %copy-start.10 = (bf16[24,9216]{1,0:T(8,128)(2,1)}, bf16[24,9216]{1,0:T(8,128)(2,1)S(1)}, u32[]{:S(2)}) copy-start(bf16[24,9216]{1,0:T(8,128)(2,1)S(1)} %collective-permute-done.9.refs_3_) | copy-start | bytes 1327108
  50.3 33.0 %collective-permute-start.16 = (bf16[24,9216]{1,0:T(8,128)(2,1)}, bf16[24,9216]{1,0:T(8,128)(2,1)}, u32[]{:S(2)}, u32[]{:S(2)}) collective-permute-start(bf16[24,9216]{1,0:T(8,128)(2,1)} %collective-permute-done.14.refs_4_), channel_id=1, source_target_pairs={{2,0},{3,1},{0,2},{1,3},{6,4},{7,5},{4,6},{5,7},{10,8},{11,9},{8,1... | collective-permute-start | bytes 1327112 | tf_op jit(solution)/shard_map/ppermute | solution.py:305
  54.9 28.4 %collective-permute-start.21 = (bf16[24,9216]{1,0:T(8,128)(2,1)}, bf16[24,9216]{1,0:T(8,128)(2,1)}, u32[]{:S(2)}, u32[]{:S(2)}) collective-permute-start(bf16[24,9216]{1,0:T(8,128)(2,1)} %collective-permute-done.20.refs_6_), channel_id=1, source_target_pairs={{1,0},{0,1},{3,2},{2,3},{5,4},{4,5},{7,6},{6,7},{9,8},{8,9},{11,10... | collective-permute-start | bytes 1327112 | tf_op jit(solution)/shard_map/ppermute | solution.py:308
  71.7 39.5 %collective-permute-start.15 = (bf16[24,9216]{1,0:T(8,128)(2,1)}, bf16[24,9216]{1,0:T(8,128)(2,1)S(1)}, u32[]{:S(2)}, u32[]{:S(2)}) collective-permute-start(bf16[24,9216]{1,0:T(8,128)(2,1)} %collective-permute-done.14.refs_4_), channel_id=1, source_target_pairs={{1,0},{0,1},{3,2},{2,3},{5,4},{4,5},{7,6},{6,7},{9,8},{8,9},{11,10... | collective-permute-start | bytes 1327112 | tf_op jit(solution)/shard_map/ppermute | solution.py:308
  72.2 39.4 %collective-permute-start.12 = (bf16[24,9216]{1,0:T(8,128)(2,1)}, bf16[24,9216]{1,0:T(8,128)(2,1)S(1)}, u32[]{:S(2)}, u32[]{:S(2)}) collective-permute-start(bf16[24,9216]{1,0:T(8,128)(2,1)} %collective-permute-done.10.refs_4_), channel_id=1, source_target_pairs={{2,0},{3,1},{0,2},{1,3},{6,4},{7,5},{4,6},{5,7},{10,8},{11,9},{8,1... | collective-permute-start | bytes 1327112 | tf_op jit(solution)/shard_map/ppermute | solution.py:305
  83.3 58.3 %collective-permute-start.11 = (bf16[24,9216]{1,0:T(8,128)(2,1)}, bf16[24,9216]{1,0:T(8,128)(2,1)S(1)}, u32[]{:S(2)}, u32[]{:S(2)}) collective-permute-start(bf16[24,9216]{1,0:T(8,128)(2,1)} %collective-permute-done.10.refs_4_), channel_id=1, source_target_pairs={{1,0},{0,1},{3,2},{2,3},{5,4},{4,5},{7,6},{6,7},{9,8},{8,9},{11,10... | collective-permute-start | bytes 1327112 | tf_op jit(solution)/shard_map/ppermute | solution.py:308
  83.3 28.5 %collective-permute-start.5 = (bf16[24,9216]{1,0:T(8,128)(2,1)S(1)}, bf16[24,9216]{1,0:T(8,128)(2,1)S(1)}, u32[]{:S(2)}, u32[]{:S(2)}) collective-permute-start(bf16[24,9216]{1,0:T(8,128)(2,1)S(1)} %collective-permute-done.3.refs_4_), channel_id=1, source_target_pairs={{2,0},{3,1},{0,2},{1,3},{6,4},{7,5},{4,6},{5,7},{10,8},{11,9},{8,1... | collective-permute-start | bytes 1327112 | tf_op jit(solution)/shard_map/ppermute | solution.py:305
  83.7 28.4 %collective-permute-start.17 = (bf16[24,9216]{1,0:T(8,128)(2,1)}, bf16[24,9216]{1,0:T(8,128)(2,1)S(1)}, u32[]{:S(2)}, u32[]{:S(2)}) collective-permute-start(bf16[24,9216]{1,0:T(8,128)(2,1)} %collective-permute-done.16.refs_6_), channel_id=1, source_target_pairs={{1,0},{0,1},{3,2},{2,3},{5,4},{4,5},{7,6},{6,7},{9,8},{8,9},{11,10... | collective-permute-start | bytes 1327112 | tf_op jit(solution)/shard_map/ppermute | solution.py:308
  111.2 1.9 copy-start.17
  111.2 60.4 %collective-permute-start.4 = (bf16[24,9216]{1,0:T(8,128)(2,1)S(1)}, bf16[24,9216]{1,0:T(8,128)(2,1)S(1)}, u32[]{:S(2)}, u32[]{:S(2)}) collective-permute-start(bf16[24,9216]{1,0:T(8,128)(2,1)S(1)} %collective-permute-done.3.refs_4_), channel_id=1, source_target_pairs={{1,0},{0,1},{3,2},{2,3},{5,4},{4,5},{7,6},{6,7},{9,8},{8,9},{11,10... | collective-permute-start | bytes 1327112 | tf_op jit(solution)/shard_map/ppermute | solution.py:308
  111.5 30.1 %copy-start.14 = (bf16[24,9216]{1,0:T(8,128)(2,1)}, bf16[24,9216]{1,0:T(8,128)(2,1)S(1)}, u32[]{:S(2)}) copy-start(bf16[24,9216]{1,0:T(8,128)(2,1)S(1)} %collective-permute-done.12.refs_6_) | copy-start | bytes 1327108
  111.5 30.5 %collective-permute-start.13 = (bf16[24,9216]{1,0:T(8,128)(2,1)S(1)}, bf16[24,9216]{1,0:T(8,128)(2,1)S(1)}, u32[]{:S(2)}, u32[]{:S(2)}) collective-permute-start(bf16[24,9216]{1,0:T(8,128)(2,1)S(1)} %collective-permute-done.12.refs_6_), channel_id=1, source_target_pairs={{1,0},{0,1},{3,2},{2,3},{5,4},{4,5},{7,6},{6,7},{9,8},{8,9},{11,10... | collective-permute-start | bytes 1327112 | tf_op jit(solution)/shard_map/ppermute | solution.py:308
  111.8 29.9 %copy-start.13 = (bf16[24,9216]{1,0:T(8,128)(2,1)}, bf16[24,9216]{1,0:T(8,128)(2,1)S(1)}, u32[]{:S(2)}) copy-start(bf16[24,9216]{1,0:T(8,128)(2,1)S(1)} %collective-permute-done.5.refs_6_) | copy-start | bytes 1327108
  111.8 59.8 %collective-permute-start.6 = (bf16[24,9216]{1,0:T(8,128)(2,1)S(1)}, bf16[24,9216]{1,0:T(8,128)(2,1)S(1)}, u32[]{:S(2)}, u32[]{:S(2)}) collective-permute-start(bf16[24,9216]{1,0:T(8,128)(2,1)S(1)} %collective-permute-done.5.refs_6_), channel_id=1, source_target_pairs={{1,0},{0,1},{3,2},{2,3},{5,4},{4,5},{7,6},{6,7},{9,8},{8,9},{11,10... | collective-permute-start | bytes 1327112 | tf_op jit(solution)/shard_map/ppermute | solution.py:308
  112.8 90.7 %collective-permute-start.23 = (bf16[24,9216]{1,0:T(8,128)(2,1)}, bf16[24,9216]{1,0:T(8,128)(2,1)S(1)}, u32[]{:S(2)}, u32[]{:S(2)}) collective-permute-start(bf16[24,9216]{1,0:T(8,128)(2,1)} %get-tuple-element.22), channel_id=1, source_target_pairs={{1,0},{0,1},{3,2},{2,3},{5,4},{4,5},{7,6},{6,7},{9,8},{8,9},{11,10... | collective-permute-start | bytes 1327112 | tf_op jit(solution)/shard_map/ppermute | solution.py:308
  141.7 64.1 %collective-permute-start.25 = (bf16[24,9216]{1,0:T(8,128)(2,1)}, bf16[24,9216]{1,0:T(8,128)(2,1)S(1)}, u32[]{:S(2)}, u32[]{:S(2)}) collective-permute-start(bf16[24,9216]{1,0:T(8,128)(2,1)} %get-tuple-element.24), channel_id=1, source_target_pairs={{1,0},{0,1},{3,2},{2,3},{5,4},{4,5},{7,6},{6,7},{9,8},{8,9},{11,10... | collective-permute-start | bytes 1327112 | tf_op jit(solution)/shard_map/ppermute | solution.py:308
  171.4 36.0 %collective-permute-start.27 = (bf16[24,9216]{1,0:T(8,128)(2,1)}, bf16[24,9216]{1,0:T(8,128)(2,1)S(1)}, u32[]{:S(2)}, u32[]{:S(2)}) collective-permute-start(bf16[24,9216]{1,0:T(8,128)(2,1)} %get-tuple-element.26), channel_id=1, source_target_pairs={{1,0},{0,1},{3,2},{2,3},{5,4},{4,5},{7,6},{6,7},{9,8},{8,9},{11,10... | collective-permute-start | bytes 1327112 | tf_op jit(solution)/shard_map/ppermute | solution.py:308
  171.6 0.9 copy-start.18
  201.3 2.2 copy-start.4
  201.3 4.5 %copy-start.5 = (bf16[24,9216]{1,0:T(8,128)(2,1)S(1)}, bf16[24,9216]{1,0:T(8,128)(2,1)}, u32[]{:S(2)}) copy-start(bf16[24,9216]{1,0:T(8,128)(2,1)} %get-tuple-element.23) | copy-start | bytes 1327108
  201.3 6.7 %collective-permute-start.29 = (bf16[24,9216]{1,0:T(8,128)(2,1)}, bf16[24,9216]{1,0:T(8,128)(2,1)S(1)}, u32[]{:S(2)}, u32[]{:S(2)}) collective-permute-start(bf16[24,9216]{1,0:T(8,128)(2,1)} %get-tuple-element.28), channel_id=1, source_target_pairs={{1,0},{0,1},{3,2},{2,3},{5,4},{4,5},{7,6},{6,7},{9,8},{8,9},{11,10... | collective-permute-start | bytes 1327112 | tf_op jit(solution)/shard_map/ppermute | solution.py:308
  203.2 4.1 %copy-start.6 = (bf16[24,9216]{1,0:T(8,128)(2,1)S(1)}, bf16[24,9216]{1,0:T(8,128)(2,1)}, u32[]{:S(2)}) copy-start(bf16[24,9216]{1,0:T(8,128)(2,1)} %get-tuple-element.25) | copy-start | bytes 1327108
  203.2 6.4 %collective-permute-start.22 = (bf16[2,24,9216]{2,1,0:T(8,128)(2,1)S(1)}, bf16[2,24,9216]{2,1,0:T(8,128)(2,1)S(1)}, u32[]{:S(2)}, u32[]{:S(2)}) collective-permute-start(bf16[2,24,9216]{2,1,0:T(8,128)(2,1)S(1)} %fusion), channel_id=1, source_target_pairs={{1,0},{0,1},{3,2},{2,3},{5,4},{4,5},{7,6},{6,7},{9,8},{8,9},{11,10... | collective-permute-start | bytes 2654216 | tf_op jit(solution)/shard_map/ppermute | solution.py:308
  203.5 4.5 %copy-start.7 = (bf16[24,9216]{1,0:T(8,128)(2,1)S(1)}, bf16[24,9216]{1,0:T(8,128)(2,1)}, u32[]{:S(2)}) copy-start(bf16[24,9216]{1,0:T(8,128)(2,1)} %get-tuple-element.27) | copy-start | bytes 1327108
  203.6 13.0 %collective-permute-start.24 = (bf16[24,9216]{1,0:T(8,128)(2,1)S(1)}, bf16[24,9216]{1,0:T(8,128)(2,1)S(1)}, u32[]{:S(2)}, u32[]{:S(2)}) collective-permute-start(bf16[24,9216]{1,0:T(8,128)(2,1)S(1)} %add_convert_fusion.3), channel_id=1, source_target_pairs={{0,28},{4,0},{8,4},{12,8},{16,12},{20,16},{24,20},{28,24},{1,29},{... | collective-permute-start | bytes 1327112 | tf_op jit(solution)/shard_map/ppermute | solution.py:302
  205.7 3.8 %copy-start.1 = (f32[2,2,24,9216]{3,2,1,0:T(8,128)S(1)}, f32[2,2,24,9216]{3,2,1,0:T(8,128)}, u32[]{:S(2)}) copy-start(f32[2,2,24,9216]{3,2,1,0:T(8,128)} %get-tuple-element.20) | copy-start | bytes 10616836
  205.8 20.3 %collective-permute-start.26 = (bf16[24,9216]{1,0:T(8,128)(2,1)S(1)}, bf16[24,9216]{1,0:T(8,128)(2,1)S(1)}, u32[]{:S(2)}, u32[]{:S(2)}) collective-permute-start(bf16[24,9216]{1,0:T(8,128)(2,1)S(1)} %add_convert_fusion.2), channel_id=1, source_target_pairs={{0,28},{4,0},{8,4},{12,8},{16,12},{20,16},{24,20},{28,24},{1,29},{... | collective-permute-start | bytes 1327112 | tf_op jit(solution)/shard_map/ppermute | solution.py:302
  207.4 28.2 %collective-permute-start.28 = (bf16[24,9216]{1,0:T(8,128)(2,1)S(1)}, bf16[24,9216]{1,0:T(8,128)(2,1)S(1)}, u32[]{:S(2)}, u32[]{:S(2)}) collective-permute-start(bf16[24,9216]{1,0:T(8,128)(2,1)S(1)} %add_convert_fusion.1), channel_id=1, source_target_pairs={{0,28},{4,0},{8,4},{12,8},{16,12},{20,16},{24,20},{28,24},{1,29},{... | collective-permute-start | bytes 1327112 | tf_op jit(solution)/shard_map/ppermute | solution.py:302
  208.1 36.4 %collective-permute-start.30 = (bf16[24,9216]{1,0:T(8,128)(2,1)S(1)}, bf16[24,9216]{1,0:T(8,128)(2,1)S(1)}, u32[]{:S(2)}, u32[]{:S(2)}) collective-permute-start(bf16[24,9216]{1,0:T(8,128)(2,1)S(1)} %add_convert_fusion), channel_id=1, source_target_pairs={{0,28},{4,0},{8,4},{12,8},{16,12},{20,16},{24,20},{28,24},{1,29},{... | collective-permute-start | bytes 1327112 | tf_op jit(solution)/shard_map/ppermute | solution.py:302
  (4 other events, 3.1 us)

commit v2 on v1

v2 whole, which is shorter than its diff:
```python
import functools

import jax
import jax.numpy as jnp
import ml_dtypes
import numpy as np
from jax import lax
from jax.experimental import pallas as pl
from jax.experimental.pallas import tpu as pltpu
from jax.sharding import PartitionSpec as P

DIST = 1
LANES = 128
TILES = 3
GROUPS = 12
UNROLL = 12
CHUNKS = 2
PITCH = 4
BF = jnp.bfloat16
F32 = jnp.float32
FLOPS = 10**11
VMEM_BYTES = 62 * 1024 * 1024


def dot(a, b):
    return jnp.dot(a, b, preferred_element_type=F32)


def half(a):
    return np.asarray(a, np.float32).astype(ml_dtypes.bfloat16)


def complex_tables(count):
    j = np.arange(count)
    angles = (j[:, None] * j[None, :] % count).astype(np.float32) * np.float32(2.0 * np.pi / count)
    cosine = half(np.cos(angles)).astype(np.float32)
    sine = half(np.sin(angles)).astype(np.float32)
    forward = np.block([[cosine, sine], [-sine, cosine]])
    backward = np.block([[cosine, -sine], [sine, cosine]])
    return forward, backward


def line_spans(count):
    per = TILES * LANES // count
    lines = [(s * count // LANES, -(-(s + 1) * count // LANES)) for s in range(per)]
    tiles = [(t * LANES // count, -(-(t + 1) * LANES // count)) for t in range(TILES)]
    return lines, tiles


def z_tables(count):
    forward, backward = complex_tables(count)
    lines, tiles = line_spans(count)
    cut, lay = [], []
    for s, (t0, t1) in enumerate(lines):
        w = np.zeros((2, (t1 - t0) * LANES, 2, LANES), np.float32)
        first = s * count - t0 * LANES
        for c in range(2):
            for d in range(2):
                w[c, first:first + count, d, :count] = forward[d * count:(d + 1) * count, c * count:(c + 1) * count].T
        cut.append(half(w.reshape(-1, 2 * LANES)))
    for t, (s0, s1) in enumerate(tiles):
        w = np.zeros((s1 - s0, 2, LANES, 2, LANES), np.float32)
        for s in range(s0, s1):
            for z in range(count):
                lane = s * count + z - t * LANES
                if 0 <= lane < LANES:
                    for c in range(2):
                        for d in range(2):
                            w[s - s0, c, :count, d, lane] = backward[d * count + z, c * count:(c + 1) * count]
        lay.append(half(w.reshape(-1, 2 * LANES)))
    return cut, lay


def piece_planes(count, ga, gb, device):
    rows = count // (ga * gb)
    ai, bi = divmod(device, gb)
    owners = [((ai + s) % ga) * gb + (bi + t) % gb for s in range(ga) for t in range(gb)]
    return np.concatenate([np.arange(o * rows, (o + 1) * rows) for o in owners])


def device_tables(count, ga, gb):
    forward, backward = complex_tables(count)
    near = count // ga
    fwd, bwd, mirror = [], [], []
    for device in range(ga * gb):
        planes = piece_planes(count, ga, gb, device)
        fwd.append(np.concatenate([forward[:, planes], forward[:, count + planes]], axis=1))
        bwd.append(np.concatenate([backward[planes[:near]], backward[count + planes[:near]]], axis=0))
        place = np.eye(count, dtype=np.float32)[:, planes]
        flip = place[(-np.arange(count)) % count]
        mirror.append(np.concatenate([place, flip], axis=1))
    return half(np.stack(fwd)), half(np.stack(bwd)), half(np.stack(mirror))


def line_selectors(count):
    lines, _ = line_spans(count)
    picks = []
    for s, (t0, t1) in enumerate(lines):
        w = np.zeros(((t1 - t0) * LANES, 2, LANES), np.float32)
        for z in range(count):
            w[s * count + z - t0 * LANES, 0, z] = 1
            w[s * count + z - t0 * LANES, 1, (-z) % count] = 1
        picks.append(half(w.reshape(-1, 2 * LANES)))
    return picks


def kernel_body(count, n, *refs):
    pieces, mirror = refs[:n], refs[n]
    lines, _ = line_spans(count)
    picks = refs[n + 1:n + 1 + len(lines)]
    out_ref, cut_ref = refs[n + 1 + len(lines):]
    per = len(lines)
    width = TILES * LANES
    unrolled = 6

    def cut(step, carry):
        for u in range(unrolled):
            group = step * unrolled + u
            lanes = pl.ds(pl.multiple_of(group * width, LANES), width)
            k = jnp.concatenate([r[:, lanes].astype(F32) for r in pieces], axis=0).astype(BF)
            for s, (t0, t1) in enumerate(lines):
                cut_ref[group * per + s] = dot(k[:, t0 * LANES:t1 * LANES], picks[s][...]).astype(BF)
        return carry

    lax.fori_loop(0, count // (per * unrolled), cut, 0)

    def join(step, carry):
        for u in range(0, 16, 2):
            both = []
            for e in range(2):
                gx = step * 16 + u + e
                back = lax.rem(count - gx, count)
                both.append(jnp.concatenate([cut_ref[gx][:, :LANES], cut_ref[back][:, LANES:]], axis=0))
            value = dot(mirror[...], jnp.concatenate(both, axis=1)) * (0.5 / count**3)
            for e in range(2):
                out_ref[step * 16 + u + e] = value[:, e * LANES:(e + 1) * LANES]
        return carry

    lax.fori_loop(0, count // 16, join, 0)


def whole_kernel(pieces, mirror, count):
    picks = line_selectors(count)
    vmem = pl.BlockSpec(memory_space=pltpu.VMEM)
    ins = [*pieces, mirror, *picks]
    return pl.pallas_call(
        functools.partial(kernel_body, count, len(pieces)),
        out_shape=jax.ShapeDtypeStruct((count, count, LANES), F32),
        in_specs=[vmem] * len(ins),
        out_specs=vmem,
        scratch_shapes=[pltpu.VMEM((count, count, 2 * LANES), BF)],
        compiler_params=pltpu.CompilerParams(vmem_limit_bytes=VMEM_BYTES),
        cost_estimate=pl.CostEstimate(flops=FLOPS, bytes_accessed=10**3, transcendentals=0),
        name="symmetric_kernel",
    )(*ins)


def unit_body(count, n, near, a_count, b_count, places, kept_held, core_ref, *refs):
    refs = list(refs)

    def take(k):
        return [refs.pop(0) for _ in range(k)]

    lines, tiles = line_spans(count)
    per = len(lines)
    width = TILES * LANES
    pieces = take((a_count + b_count) * n)
    kern, x_tables, y_tables, z_tables_ref = take(4)
    kept_in = [take(near) for _ in range(a_count)] if kept_held else None
    sent_out, kept_out = take(b_count * near), take(a_count * near)
    held, k_ref, x_ref, y_ref, z_ref, sent_near, sent_rest, kept_ref, s_ref, r_ref = take(10)
    in_sem, table_sem, kept_sem, sent_sem, out_sem = take(5)
    rows = pieces[0].shape[1]
    where = [core_ref[0] * step + offset if step else offset for step, offset in places]
    pitch = count + PITCH
    planes = near * rows
    steps = count // (per * GROUPS)
    chunk = count * count // CHUNKS
    pairs = [(i, j) for i in range(a_count) for j in range(b_count)]

    def lanes_of(part):
        return slice(part * chunk, (part + 1) * chunk)

    def piece_in(step, p):
        return pltpu.make_async_copy(
            pieces[p].at[where[p], :, lanes_of(step)], held.at[p, :, lanes_of(step)], in_sem.at[step, p]
        )

    def outgoing(step):
        lanes = lanes_of(step)
        copies = []
        for j in range(b_count):
            for p in range(near):
                source = sent_rest.at[j, p - 1, :, lanes] if p else sent_near.at[j, :, lanes]
                copies.append(
                    pltpu.make_async_copy(source, sent_out[j * near + p].at[:, lanes], sent_sem.at[step, j * near + p])
                )
        for i in range(a_count):
            for p in range(near):
                copies.append(
                    pltpu.make_async_copy(
                        kept_ref.at[i, p, :, lanes], kept_out[i * near + p].at[:, lanes], out_sem.at[step, i * near + p]
                    )
                )
        return copies

    small = [
        pltpu.make_async_copy(z_tables_ref, z_ref, table_sem.at[0]),
        pltpu.make_async_copy(x_tables, x_ref, table_sem.at[1]),
        pltpu.make_async_copy(y_tables, y_ref, table_sem.at[2]),
    ]
    k_copy = pltpu.make_async_copy(kern, k_ref, table_sem.at[3])
    kept_copies = []
    if kept_held:
        for i in range(a_count):
            for p in range(near):
                kept_copies.append(
                    pltpu.make_async_copy(kept_in[i][p], kept_ref.at[i, p], kept_sem.at[i * near + p])
                )

    small[0].start()
    small[1].start()

    for part in range(CHUNKS):
        for p in range(len(pieces)):
            piece_in(part, p).start()
    small[2].start()
    k_copy.start()
    for copy in kept_copies:
        copy.start()

    spans_cut, spans_lay, at = [], [], 0
    for t0, t1 in lines:
        spans_cut.append(slice(at, at + 2 * (t1 - t0) * LANES))
        at += 2 * (t1 - t0) * LANES
    for s0, s1 in tiles:
        spans_lay.append(slice(at, at + 2 * (s1 - s0) * LANES))
        at += 2 * (s1 - s0) * LANES

    def stack(first, number, lanes):
        return jnp.concatenate([held[first + p, :, lanes].astype(F32) for p in range(number)], axis=0)

    small[0].wait()
    small[1].wait()

    def forward(step, carry):
        for part in range(CHUNKS):

            @pl.when(step == part * steps // CHUNKS)
            def _():
                for p in range(len(pieces)):
                    piece_in(part, p).wait()

        rho = [[], []]
        for g in range(GROUPS):
            lanes = pl.ds(pl.multiple_of((step * GROUPS + g) * width, LANES), width)
            a = [stack(i * n, n, lanes) for i in range(a_count)]
            b = [stack((a_count + j) * n, n, lanes) for j in range(b_count)]
            for k, (i, j) in enumerate(pairs):
                rho[k].append((a[i] * b[j]).astype(BF))
        rho = [jnp.concatenate(r, axis=0) for r in rho]
        along = []
        for s, (t0, t1) in enumerate(lines):
            lhs = jnp.concatenate([r[:, t0 * LANES:t1 * LANES] for r in rho], axis=1)
            along.append(dot(lhs, z_ref[spans_cut[s], :]).astype(BF))
        for g in range(GROUPS):
            parts = []
            for s in range(per):
                w = along[s][g * count:(g + 1) * count]
                parts.append(jnp.concatenate([w[:, :LANES], w[:, LANES:]], axis=0))
            out = dot(x_ref[:2 * count], jnp.concatenate(parts, axis=1))
            y = (step * GROUPS + g) * per
            for s in range(per):
                s_ref[pl.ds(y + s, 2 * count, pitch), :] = out[:, s * LANES:(s + 1) * LANES]
        return carry

    lax.fori_loop(0, steps, forward, 0)
    small[2].wait()
    k_copy.wait()

    def plane_set(ref, first):
        return jnp.concatenate(
            [
                jnp.concatenate(
                    [ref[pl.ds((c * count + first + e) * pitch, count), :].astype(BF) for c in range(2)], axis=0
                )
                for e in range(per)
            ],
            axis=1,
        )

    def middle(step, carry):
        firsts = [(step * UNROLL + u) * per for u in range(UNROLL)]
        summed = [dot(y_ref[:2 * count], plane_set(s_ref, gx)) for gx in firsts]
        spectra = []
        for gx, value in zip(firsts, summed):
            scale = jnp.concatenate([k_ref[gx + e] for e in range(per)], axis=1)
            spectra.append(
                jnp.concatenate([(value[:count] * scale).astype(BF), (value[count:] * scale).astype(BF)], axis=0)
            )
        backs = [dot(y_ref[2 * count:], spectrum) for spectrum in spectra]
        for gx, value in zip(firsts, backs):
            for e in range(per):
                r_ref[pl.ds(gx + e, 2 * count, pitch), :] = value[:, e * LANES:(e + 1) * LANES]
        return carry

    lax.fori_loop(0, count // (per * UNROLL), middle, 0)
    for copy in kept_copies:
        copy.wait()

    def backward(step, carry):
        columns = []
        for g in range(GROUPS):
            out = dot(x_ref[2 * count:], plane_set(r_ref, (step * GROUPS + g) * per)).astype(BF)
            row = []
            for s in range(per):
                w = out[:, s * LANES:(s + 1) * LANES]
                row.append(jnp.concatenate([w[:planes], w[planes:]], axis=1))
            columns.append(row)
        for t, (s0, s1) in enumerate(tiles):
            lhs = jnp.concatenate([jnp.concatenate(row[s0:s1], axis=1) for row in columns], axis=0)
            potential = dot(lhs, z_ref[spans_lay[t], :])
            for g in range(GROUPS):
                lanes = pl.ds(pl.multiple_of((step * GROUPS + g) * width + t * LANES, LANES), LANES)
                minus = -potential[g * planes:(g + 1) * planes]
                a = [stack(i * n, near, lanes) for i in range(a_count)]
                b = [stack((a_count + j) * n, near, lanes) for j in range(b_count)]
                sent, kept = [None] * b_count, [None] * a_count
                for k, (i, j) in enumerate(pairs):
                    v = minus[:, k * LANES:(k + 1) * LANES]
                    sent[j] = v * a[i] if sent[j] is None else sent[j] + v * a[i]
                    kept[i] = v * b[j] if kept[i] is None else kept[i] + v * b[j]
                for p in range(near):
                    part = slice(p * rows, (p + 1) * rows)
                    for j in range(b_count):
                        if p:
                            sent_rest[j, p - 1, :, lanes] = sent[j][part].astype(BF)
                        else:
                            sent_near[j, :, lanes] = sent[j][part]
                    for i in range(a_count):
                        value = kept[i][part]
                        if kept_held:
                            value = value + kept_ref[i, p, :, lanes]
                        kept_ref[i, p, :, lanes] = value
        for part in range(CHUNKS):

            @pl.when(step == (part + 1) * steps // CHUNKS - 1)
            def _():
                for copy in outgoing(part):
                    copy.start()

        return carry

    lax.fori_loop(0, steps, backward, 0)

    for part in range(CHUNKS):
        for copy in outgoing(part):
            copy.wait()


def unit(a, b, core, kern, x_tables, near, kept_in):
    count = kern.shape[0]
    n = len(a[0])
    rows, width = a[0][0][0].shape[1:]
    a_count, b_count = len(a), len(b)
    y_tables = np.concatenate([half(t) for t in complex_tables(count)], axis=0)
    cut, lay = z_tables(count)
    z_all = np.concatenate([*cut, *lay], axis=0)
    chosen = [r for pieces in (*a, *b) for r in pieces]
    ins = [r[0] for r in chosen] + [kern, x_tables, y_tables, z_all]
    if kept_in is not None:
        ins += [k for pieces in kept_in for k in pieces]
    anywhere = pl.BlockSpec(memory_space=pltpu.HBM)
    pieces = (a_count + b_count) * n
    outs = pl.pallas_call(
        functools.partial(
            unit_body, count, n, near, a_count, b_count, [r[1:] for r in chosen], kept_in is not None
        ),
        out_shape=[
            jax.ShapeDtypeStruct((rows, width), BF if p else F32) for _ in range(b_count) for p in range(near)
        ]
        + [jax.ShapeDtypeStruct((rows, width), F32)] * (a_count * near),
        in_specs=[pl.BlockSpec(memory_space=pltpu.SMEM)] + [anywhere] * len(ins),
        out_specs=[anywhere] * ((a_count + b_count) * near),
        scratch_shapes=[
            pltpu.VMEM((pieces, rows, width), BF),
            pltpu.VMEM(kern.shape, F32),
            pltpu.VMEM(x_tables.shape, BF),
            pltpu.VMEM(y_tables.shape, BF),
            pltpu.VMEM(z_all.shape, BF),
            pltpu.VMEM((b_count, rows, width), F32),
            pltpu.VMEM((b_count, near - 1, rows, width), BF),
            pltpu.VMEM((a_count, near, rows, width), F32),
            pltpu.VMEM((2 * count * (count + PITCH), LANES), F32),
            pltpu.VMEM((2 * count * (count + PITCH), LANES), F32),
            pltpu.SemaphoreType.DMA((CHUNKS, pieces)),
            pltpu.SemaphoreType.DMA((4,)),
            pltpu.SemaphoreType.DMA((a_count * near,)),
            pltpu.SemaphoreType.DMA((CHUNKS, b_count * near)),
            pltpu.SemaphoreType.DMA((CHUNKS, a_count * near)),
        ],
        compiler_params=pltpu.CompilerParams(vmem_limit_bytes=VMEM_BYTES),
        cost_estimate=pl.CostEstimate(flops=FLOPS, bytes_accessed=10**3, transcendentals=0),
        name="pair_potentials",
    )(core, *ins)
    sent = [outs[j * near:(j + 1) * near] for j in range(b_count)]
    kept = [outs[(b_count + i) * near:(b_count + i + 1) * near] for i in range(a_count)]
    return sent, kept


def split_of(n):
    gb = 1
    while gb * gb < n and gb < 4:
        gb *= 2
    return n // gb, gb


def after(value, *events):
    return lax.optimization_barrier((value, *events))[0]


def local(orbitals, kernel, *, ga, gb):
    band_count, rows, width = orbitals.shape
    n = ga * gb
    count = rows * n
    na = band_count // gb
    blocks = lax.axis_size("band")
    me = lax.axis_index("grid")
    bi = me % gb

    def hop(x, distance):
        return lax.ppermute(x, "band", [(i, (i + distance) % blocks) for i in range(blocks)])

    def to_a(x, s):
        return lax.ppermute(x, "grid", [(((i // gb + s) % ga) * gb + i % gb, i) for i in range(n)])

    def to_b(x, t):
        return lax.ppermute(x, "grid", [((i // gb) * gb + (i % gb + t) % gb, i) for i in range(n)])

    order = [(s, t) for s in range(ga) for t in range(gb)]
    fwd, bwd, mirror = device_tables(count, ga, gb)
    x_tables, mirror = (
        lax.dynamic_index_in_dim(jnp.asarray(t), me, 0, False) for t in (np.concatenate([fwd, bwd], axis=1), mirror)
    )

    core = bi.astype(jnp.int32).reshape(1)

    def others(x):
        return [to_b(x, t) for t in range(1, gb)]

    k_own = kernel.astype(BF)
    shares = [orbitals[index * gb:(index + 1) * gb] for index in range(na)]
    singles = [orbitals[j:j + 1] for j in range(gb, band_count)]
    own_near = [orbitals, *others(orbitals)]
    k_near = [k_own, *others(k_own)]
    k_far = [to_a(k_own, s) for s in range(1, ga)]
    own_far = [[to_a(shares[0], s) for s in range(1, ga)]]
    block = hop(shares[0], DIST)
    landed = [hop(x, DIST) for x in singles[:1]]
    k_far, own_far, block, landed, shares, singles, own_near, k_near, x_tables, mirror = lax.optimization_barrier(
        (k_far, own_far, block, landed, shares, singles, own_near, k_near, x_tables, mirror)
    )

    own_far += [[to_a(shares[index], s) for s in range(1, ga)] for index in range(1, na)]
    forwarded = [hop(r[:1], DIST) for r in own_far[0]]
    k_rows = list(k_near)
    for r in k_far:
        k_rows += [r, *others(r)]
    kern = whole_kernel(k_rows, mirror, count)
    far_pieces = [[[r, *others(r)] for r in own_far[0]]]
    near_blocks = [[x, *others(x)] for x in [block, *landed[:1]]]
    own_far, forwarded, singles, kern, far_pieces, near_blocks = lax.optimization_barrier(
        (own_far, forwarded, singles, kern, far_pieces, near_blocks)
    )

    far_pieces += [[[r, *others(r)] for r in own_far[index]] for index in range(1, na)]
    landed = [hop(x, DIST) for x in singles[1:]]
    near_blocks += [[x, *others(x)] for x in landed]
    own = []
    for index in range(na):
        pieces = [(r, 1, index * gb) for r in own_near]
        pieces += [(r, 1, 0) for group in far_pieces[index] for r in group]
        own.append(pieces)
    near = [[(r, 0, j) for r in near_blocks[0]] for j in range(gb)]
    near += [[(r, 0, 0) for r in blocks_near] for blocks_near in near_blocks[1:]]

    def partner(j, *events):
        pieces = list(near[j])
        for s in range(1, ga):
            if j == 0:
                r = forwarded[s - 1]
            else:
                r, _, offset = near[j][0]
                r = to_a(r[offset:offset + 1], s)
                if events:
                    r = after(r, *events)
            pieces += [(x, 0, 0) for x in [r, *others(r)]]
        return pieces

    returned = [None] * band_count
    events = []

    def send_back(sent, j):
        total = sent[0]
        for t in range(1, gb):
            total = total + to_b(sent[t], gb - t).astype(F32)
        total = total.astype(BF)
        events.append(total)
        returned[j] = hop(total, -DIST)

    kept = None
    sent_by = []
    per_unit = 2 // na
    for u in range(0, band_count, per_unit):
        b = [partner(j, *(sent_by[-2:-1] or sent_by)) for j in range(u, u + per_unit)]
        tables = after(x_tables, events[-2]) if len(events) > 1 else x_tables
        sent, kept = unit(own, b, core, kern, tables, gb, kept)
        sent_by.append(sent[0][0])
        for e in range(per_unit):
            send_back(sent[e], u + e)

    parts = [[x[0] for x in kept]]
    for t in range(1, gb):
        received = to_b(jnp.stack([x[t] for x in kept]).astype(BF), gb - t)
        parts.append([received[index].astype(F32) for index in range(na)])
    rows_out = []
    for j in range(band_count):
        index, owner = divmod(j, gb)
        which = (bi - owner + gb) % gb
        value = parts[0][index]
        for t in range(1, gb):
            value = jnp.where(which == t, parts[t][index], value)
        rows_out.append(value)
    early = band_count - per_unit
    base = lax.optimization_barrier(
        jnp.stack([v + returned[j].astype(F32) if j < early else v for j, v in enumerate(rows_out)])
    )
    last = base[early:] + jnp.stack(returned[early:]).astype(F32)
    return lax.dynamic_update_slice(base, last, (early, 0, 0))


def solution(mesh):
    ga, gb = split_of(mesh.shape["grid"])
    placed = (P("band", "grid", None), P("grid", None))
    return jax.shard_map(
        functools.partial(local, ga=ga, gb=gb),
        mesh=mesh,
        in_specs=placed,
        out_specs=P("band", "grid", None),
        check_vma=False,
    )
```

time: 247 us -> 162 us (0.66)
  Pallas kernels: 127 us -> 61.9 us
  waiting for transfers between devices: 84.5 us -> 49.9 us
  other arithmetic: 4.14 us -> 10.7 us
  starting transfers between devices: 22 us -> 25.8 us
  local copies, waits for them, and re-layouts: 8.89 us -> 12.6 us
    pallas_call x4, Pallas kernels: 113 us -> 54.6 us  [unit(): pl.pallas_call(functools.partial(unit_body, count, n, near, a_count, b_co...]
    ppermute x8, waiting for transfers between devices: 65.1 us -> 25.9 us  [hop(): lax.ppermute(x, 'band', [(i, (i + distance) % blocks) for i in range(bloc...]
    pallas_call x1, Pallas kernels: 13.8 us -> 7.35 us  [whole_kernel(): pl.pallas_call(functools.partial(kernel_body, count, len(pieces)), out_sh...]
    another operation x0 -> x4, other arithmetic: none -> 5.26 us  [the longest x2 3.66 us: local(): jnp.stack([v + returned[j].astype(F32) if j < early else v for j, v in en...]
    slice x0 -> x4, local copies, waits for them, and re-layouts: none -> 4.84 us  [the longest x1 1.55 us: local(): shares = [orbitals[index * gb:(index + 1) * gb] for index in range(na)]]
    ppermute x7 -> x6, waiting for transfers between devices: 19.4 us -> 23.9 us  [to_a(): lax.ppermute(x, 'grid', [((i // gb + s) % ga * gb + i % gb, i) for i in r...]
    ppermute x8, starting transfers between devices: 10.5 us -> 14.6 us  [hop(): lax.ppermute(x, 'band', [(i, (i + distance) % blocks) for i in range(bloc...]
    ppermute x7 -> x6, starting transfers between devices: 7.89 us -> 7.29 us  [to_a(): lax.ppermute(x, 'grid', [((i // gb + s) % ga * gb + i % gb, i) for i in r...]
  transfers between devices with their start and end apart: 31 -> 31, of which waited for: 11 -> 6; matrix products, arithmetic and copies ran while one was open for 3% -> 10% of each run, Pallas kernels for 51% -> 38%
where the time goes in v2:
time: 162 us; the launch traced here: 161 us
  Pallas kernels  61.9 us (38%)
  waiting for transfers between devices  49.9 us (31%)
  starting transfers between devices  25.8 us (16%)
  local copies, waits for them, and re-layouts  12.6 us (8%)
  other arithmetic  10.7 us (7%)
    pallas_call x4, Pallas kernels, unit(): pl.pallas_call(functools.partial(unit_body, count, n, near, a_count, b_co...  54.6 us
    ppermute x8, waiting for transfers between devices, hop(): lax.ppermute(x, 'band', [(i, (i + distance) % blocks) for i in range(bloc...  25.9 us
    ppermute x6, waiting for transfers between devices, to_a(): lax.ppermute(x, 'grid', [((i // gb + s) % ga * gb + i % gb, i) for i in r...  23.9 us
    ppermute x8, starting transfers between devices, hop(): lax.ppermute(x, 'band', [(i, (i + distance) % blocks) for i in range(bloc...  14.6 us
    pallas_call x1, Pallas kernels, whole_kernel(): pl.pallas_call(functools.partial(kernel_body, count, len(pieces)), out_sh...  7.35 us
    ppermute x6, starting transfers between devices, to_a(): lax.ppermute(x, 'grid', [((i // gb + s) % ga * gb + i % gb, i) for i in r...  7.29 us
    unnamed x26, local copies, waits for them, and re-layouts  4.75 us
    ppermute x17, starting transfers between devices, to_b(): lax.ppermute(x, 'grid', [(i // gb * gb + (i % gb + t) % gb, i) for i in r...  3.9 us
  transfers between devices with their start and end apart: 31, of which 6 were waited for; matrix products, arithmetic and copies ran while one was open for 10% of the time, Pallas kernels for 38%

profile of v2, /device:TPU:0, one launch (start us, length us, event | category | flops | bytes accessed | tf_op | source)
XLA Modules:
  0.0 161.1 jit_solution(333804116116550861)
XLA Ops:
  0.0 0.5 collective-permute-start.4
  0.5 1.2 fusion.8
  1.7 2.6 %collective-permute-start.3 = (bf16[1,24,9216]{2,1,0:T(8,128)(2,1)S(1)}, bf16[1,24,9216]{2,1,0:T(8,128)(2,1)S(1)}, u32[]{:S(2)}, u32[]{:S(2)}) collective-permute-start(bf16[1,24,9216]{2,1,0:T(8,128)(2,1)S(1)} %get-tuple-element.112), channel_id=1, source_target_pairs={{0,4},{4,8},{8,12},{12,16},{16,20},{20,24},{24,28},{28,0},{1,5},{5... | collective-permute-start | bytes 1327112 | tf_op jit(solution)/shard_map/ppermute | solution.py:432
  4.3 1.5 fusion.9
  5.9 1.6 collective-permute-start.1
  7.4 1.5 collective-permute-start.2
  9.0 0.6 collective-permute-start
  9.6 8.8 %collective-permute-done.3.refs_8_ = bf16[1,24,9216]{2,1,0:T(8,128)(2,1)S(1)} collective-permute-done((bf16[1,24,9216]{2,1,0:T(8,128)(2,1)S(1)}, bf16[1,24,9216]{2,1,0:T(8,128)(2,1)S(1)}, u32[]{:S(2)}, u32[]{:S(2)}) %collective-permute-start.3) | collective-permute-done | bytes 442400 | tf_op jit(solution)/shard_map/ppermute | solution.py:432
  18.4 0.8 copy-done.8
  19.1 1.4 dynamic-slice_bitcast_fusion.1.refs_4_
  20.6 1.6 dynamic-slice_bitcast_fusion.refs_13_
  22.1 15.1 %collective-permute-done.refs_2_ = bf16[24,9216]{1,0:T(8,128)(2,1)} collective-permute-done((bf16[24,9216]{1,0:T(8,128)(2,1)S(1)}, bf16[24,9216]{1,0:T(8,128)(2,1)}, u32[]{:S(2)}, u32[]{:S(2)}) %collective-permute-start) | collective-permute-done | bytes 442400 | tf_op jit(solution)/shard_map/ppermute | solution.py:435
  37.3 0.7 copy-done.9
  38.0 1.0 slice.31
  39.1 0.6 collective-permute-start.9
  39.6 1.5 collective-permute-start.7
  41.2 0.5 collective-permute-start.11
  41.7 1.5 collective-permute-start.6
  43.2 7.3 %symmetric_kernel.1.refs_12_ = f32[96,96,128]{2,1,0:T(8,128)} custom-call(bf16[24,9216]{1,0:T(8,128)(2,1)} %copy-done.6, bf16[24,9216]{1,0:T(8,128)(2,1)} %copy-done.9, bf16[24,9216]{1,0:T(8,128)(2,1)} %collective-permute-done.refs_2_, bf16[24,9216]{1,0:T(8,128)(2,1)} %collective-permute-done.8.refs_3_, bf16[96,192]{1,0:T(8,128)(2,1)} %dynamic-slice_bitcast_fusion.1.refs_4_, ...), custom_call_target="tpu_custom_call" | custom-call | flops 99999997952 | bytes 1000 | tf_op jit(solution)/shard_map/symmetric_kernel/pallas_call | solution.py:146
  50.5 4.1 %collective-permute-done.7.refs_10_ = bf16[1,24,9216]{2,1,0:T(8,128)(2,1)} collective-permute-done((bf16[1,24,9216]{2,1,0:T(8,128)(2,1)S(1)}, bf16[1,24,9216]{2,1,0:T(8,128)(2,1)}, u32[]{:S(2)}, u32[]{:S(2)}) %collective-permute-start.7) | collective-permute-done | bytes 442400 | tf_op jit(solution)/shard_map/ppermute | solution.py:432
  54.6 8.7 %collective-permute-done.6.refs_6_ = bf16[2,24,9216]{2,1,0:T(8,128)(2,1)} collective-permute-done((bf16[2,24,9216]{2,1,0:T(8,128)(2,1)S(1)}, bf16[2,24,9216]{2,1,0:T(8,128)(2,1)}, u32[]{:S(2)}, u32[]{:S(2)}) %collective-permute-start.6) | collective-permute-done | bytes 884768 | tf_op jit(solution)/shard_map/ppermute | solution.py:435
  63.3 0.5 collective-permute-start.17
  63.8 1.5 collective-permute-start.21
  65.3 1.0 slice.32
  66.4 0.6 collective-permute-start.16
  67.0 1.5 collective-permute-start.13
  68.5 0.8 copy-done.11
  69.3 0.9 copy-done.7
  70.2 13.5 %pair_potentials.4 = (f32[24,9216]{1,0:T(8,128)}, bf16[24,9216]{1,0:T(8,128)(2,1)}, f32[24,9216]{1,0:T(8,128)}, f32[24,9216]{1,0:T(8,128)}, f32[24,9216]{1,0:T(8,128)}, /*index=5*/f32[24,9216]{1,0:T(8,128)}) custom-call(s32[1]{0:T(128)} %bitcast.core_ref, bf16[4,24,9216]{2,1,0:T(8,128)(2,1)} %refs_4_.3, ...), custom_call_target="tpu_custom_call" | custom-call | flops 99999997952 | bytes 1000 | tf_op jit(solution)/shard_map/pair_potentials/pallas_call | solution.py:375
  83.8 1.6 collective-permute-start.15
  86.0 2.0 %add_convert_fusion.2 = bf16[24,9216]{1,0:T(8,128)(2,1)} fusion(f32[24,9216]{1,0:T(8,128)} %get-tuple-element.76, bf16[24,9216]{1,0:T(8,128)(2,1)S(1)} %collective-permute-done.23), kind=kLoop, calls=%fused_computation.17 | loop fusion | flops 663552 | bytes 1769472 | tf_op jit(solution)/shard_map/convert_element_type | solution.py:507
  88.0 3.2 %collective-permute-start.25 = (bf16[24,9216]{1,0:T(8,128)(2,1)}, bf16[24,9216]{1,0:T(8,128)(2,1)}, u32[]{:S(2)}, u32[]{:S(2)}) collective-permute-start(bf16[24,9216]{1,0:T(8,128)(2,1)} %add_convert_fusion.2), channel_id=1, source_target_pairs={{0,28},{4,0},{8,4},{12,8},{16,12},{20,16},{24,20},{28,24},{1,29},{... | collective-permute-start | bytes 1327112 | tf_op jit(solution)/shard_map/ppermute | solution.py:432
  91.2 0.8 copy-done.12
  92.0 13.6 %pair_potentials.5 = (f32[24,9216]{1,0:T(8,128)}, bf16[24,9216]{1,0:T(8,128)(2,1)}, f32[24,9216]{1,0:T(8,128)}, f32[24,9216]{1,0:T(8,128)}, f32[24,9216]{1,0:T(8,128)}, /*index=5*/f32[24,9216]{1,0:T(8,128)}) custom-call(s32[1]{0:T(128)} %bitcast.core_ref, bf16[4,24,9216]{2,1,0:T(8,128)(2,1)} %refs_4_.3, ...), custom_call_target="tpu_custom_call" | custom-call | flops 99999997952 | bytes 1000 | tf_op jit(solution)/shard_map/pair_potentials/pallas_call | solution.py:375
  105.8 0.4 collective-permute-start.19
  106.2 0.8 copy-done.10
  107.0 13.7 %pair_potentials.6 = (f32[24,9216]{1,0:T(8,128)}, bf16[24,9216]{1,0:T(8,128)(2,1)}, f32[24,9216]{1,0:T(8,128)}, f32[24,9216]{1,0:T(8,128)}, f32[24,9216]{1,0:T(8,128)}, /*index=5*/f32[24,9216]{1,0:T(8,128)}) custom-call(s32[1]{0:T(128)} %bitcast.core_ref, bf16[4,24,9216]{2,1,0:T(8,128)(2,1)} %refs_4_.3, ...), custom_call_target="tpu_custom_call" | custom-call | flops 99999997952 | bytes 1000 | tf_op jit(solution)/shard_map/pair_potentials/pallas_call | solution.py:375
  120.9 1.1 add_convert_fusion.3
  122.0 0.9 collective-permute-start.26
  122.9 13.7 %pair_potentials.7 = (f32[24,9216]{1,0:T(8,128)}, bf16[24,9216]{1,0:T(8,128)(2,1)}, f32[24,9216]{1,0:T(8,128)}, f32[24,9216]{1,0:T(8,128)}, f32[24,9216]{1,0:T(8,128)}, /*index=5*/f32[24,9216]{1,0:T(8,128)}) custom-call(s32[1]{0:T(128)} %bitcast.core_ref, bf16[4,24,9216]{2,1,0:T(8,128)(2,1)} %refs_4_.3, ...), custom_call_target="tpu_custom_call" | custom-call | flops 99999997952 | bytes 1000 | tf_op jit(solution)/shard_map/pair_potentials/pallas_call | solution.py:375
  136.9 2.5 %collective-permute-start.28 = (bf16[24,9216]{1,0:T(8,128)(2,1)S(1)}, bf16[24,9216]{1,0:T(8,128)(2,1)S(1)}, u32[]{:S(2)}, u32[]{:S(2)}) collective-permute-start(bf16[24,9216]{1,0:T(8,128)(2,1)S(1)} %add_convert_fusion.1), channel_id=1, source_target_pairs={{0,28},{4,0},{8,4},{12,8},{16,12},{20,16},{24,20},{28,24},{1,29},{... | collective-permute-start | bytes 1327112 | tf_op jit(solution)/shard_map/ppermute | solution.py:432
  139.4 1.5 convert_bitcast_fusion
  141.4 0.8 collective-permute-start.30
  142.2 7.8 %collective-permute-done.28 = bf16[24,9216]{1,0:T(8,128)(2,1)S(1)} collective-permute-done((bf16[24,9216]{1,0:T(8,128)(2,1)S(1)}, bf16[24,9216]{1,0:T(8,128)(2,1)S(1)}, u32[]{:S(2)}, u32[]{:S(2)}) %collective-permute-start.28) | collective-permute-done | bytes 442400 | tf_op jit(solution)/shard_map/ppermute | solution.py:432
  150.0 1.6 %fusion.1 = (f32[1,24,9216]{2,1,0:T(8,128)S(1)}, f32[1,24,9216]{2,1,0:T(8,128)S(1)}, f32[1,24,9216]{2,1,0:T(8,128)S(1)}, f32[1,24,9216]{2,1,0:T(8,128)S(1)}) fusion(f32[24,9216]{1,0:T(8,128)S(1)} %copy-done.4, bf16[24,9216]{1,0:T(8,128)(2,1)} %collective-permute-done.25, pred[]{:T(512)S(6)} %eq.14, bf16[2,24,9216]{2,1,0:T(8,128)(2,1)S(1)} %collective-permute-done.24, ...), kind=kLoop, calls=%fused_computation.6 | loop fusion | flops 2654208 | bytes 7520258 | tf_op jit(solution)/shard_map/stack | solution.py:536
  151.6 2.0 %pad_maximum_fusion = f32[4,24,9216]{2,1,0:T(8,128)} fusion(f32[1,24,9216]{2,1,0:T(8,128)S(1)} %get-tuple-element.115, f32[1,24,9216]{2,1,0:T(8,128)S(1)} %get-tuple-element.116, f32[1,24,9216]{2,1,0:T(8,128)S(1)} %get-tuple-element.108, f32[1,24,9216]{2,1,0:T(8,128)S(1)} %get-tuple-element.107), kind=kLoop, calls=%fused_computation | loop fusion | flops 2654208 | bytes 7077888 | tf_op jit(solution)/shard_map/stack | solution.py:536
  153.6 5.3 %collective-permute-done.30 = bf16[24,9216]{1,0:T(8,128)(2,1)S(1)} collective-permute-done((bf16[24,9216]{1,0:T(8,128)(2,1)S(1)}, bf16[24,9216]{1,0:T(8,128)(2,1)S(1)}, u32[]{:S(2)}, u32[]{:S(2)}) %collective-permute-start.30) | collective-permute-done | bytes 442400 | tf_op jit(solution)/shard_map/ppermute | solution.py:432
  159.0 2.2 %fusion.7 = f32[4,24,9216]{2,1,0:T(8,128)} fusion(f32[4,24,9216]{2,1,0:T(8,128)} %pad_maximum_fusion, bf16[24,9216]{1,0:T(8,128)(2,1)S(1)} %collective-permute-done.30), kind=kLoop, calls=%fused_computation.13 | loop fusion | flops 442368 | bytes 2211840 | tf_op jit(solution)/shard_map/dynamic_update_slice | solution.py:539
  (61 shorter events, 1.8 us)
Async XLA Ops:
  0.0 8.9 %copy-start.3 = (f32[24,9216]{1,0:T(8,128)S(1)}, f32[24,9216]{1,0:T(8,128)}, u32[]{:S(2)}) copy-start(f32[24,9216]{1,0:T(8,128)} %param.17) | copy-start | bytes 2654212
  0.0 37.3 %collective-permute-start.4 = (bf16[4,24,9216]{2,1,0:T(8,128)(2,1)}, bf16[4,24,9216]{2,1,0:T(8,128)(2,1)}, u32[]{:S(2)}, u32[]{:S(2)}) collective-permute-start(bf16[4,24,9216]{2,1,0:T(8,128)(2,1)} %refs_4_.3), channel_id=1, source_target_pairs={{1,0},{0,1},{3,2},{2,3},{5,4},{4,5},{7,6},{6,7},{9,8},{8,9},{11,10... | collective-permute-start | bytes 5308424 | tf_op jit(solution)/shard_map/ppermute | solution.py:438
  1.7 16.7 %collective-permute-start.3 = (bf16[1,24,9216]{2,1,0:T(8,128)(2,1)S(1)}, bf16[1,24,9216]{2,1,0:T(8,128)(2,1)S(1)}, u32[]{:S(2)}, u32[]{:S(2)}) collective-permute-start(bf16[1,24,9216]{2,1,0:T(8,128)(2,1)S(1)} %get-tuple-element.112), channel_id=1, source_target_pairs={{0,4},{4,8},{8,12},{12,16},{16,20},{20,24},{24,28},{28,0},{1,5},{5... | collective-permute-start | bytes 1327112 | tf_op jit(solution)/shard_map/ppermute | solution.py:432
  5.9 31.4 %collective-permute-start.1 = (bf16[2,24,9216]{2,1,0:T(8,128)(2,1)S(1)}, bf16[2,24,9216]{2,1,0:T(8,128)(2,1)}, u32[]{:S(2)}, u32[]{:S(2)}) collective-permute-start(bf16[2,24,9216]{2,1,0:T(8,128)(2,1)S(1)} %get-tuple-element.114), channel_id=1, source_target_pairs={{2,0},{3,1},{0,2},{1,3},{6,4},{7,5},{4,6},{5,7},{10,8},{11,9},{8,1... | collective-permute-start | bytes 2654216 | tf_op jit(solution)/shard_map/ppermute | solution.py:435
  7.4 29.8 %collective-permute-start.2 = (bf16[2,24,9216]{2,1,0:T(8,128)(2,1)S(1)}, bf16[2,24,9216]{2,1,0:T(8,128)(2,1)}, u32[]{:S(2)}, u32[]{:S(2)}) collective-permute-start(bf16[2,24,9216]{2,1,0:T(8,128)(2,1)S(1)} %get-tuple-element.114), channel_id=1, source_target_pairs={{0,4},{4,8},{8,12},{12,16},{16,20},{20,24},{24,28},{28,0},{1,5},{5... | collective-permute-start | bytes 2654216 | tf_op jit(solution)/shard_map/ppermute | solution.py:432
  9.0 28.3 %copy-start.6 = (bf16[24,9216]{1,0:T(8,128)(2,1)}, bf16[24,9216]{1,0:T(8,128)(2,1)S(1)}, u32[]{:S(2)}) copy-start(bf16[24,9216]{1,0:T(8,128)(2,1)S(1)} %convert_element_type.55.refs_0_) | copy-start | bytes 1327108
  9.0 28.2 %collective-permute-start = (bf16[24,9216]{1,0:T(8,128)(2,1)S(1)}, bf16[24,9216]{1,0:T(8,128)(2,1)}, u32[]{:S(2)}, u32[]{:S(2)}) collective-permute-start(bf16[24,9216]{1,0:T(8,128)(2,1)S(1)} %convert_element_type.55.refs_0_), channel_id=1, source_target_pairs={{2,0},{3,1},{0,2},{1,3},{6,4},{7,5},{4,6},{5,7},{10,8},{11,9},{8,1... | collective-permute-start | bytes 1327112 | tf_op jit(solution)/shard_map/ppermute | solution.py:435
  18.4 0.8 copy-start.8
  19.1 18.1 %collective-permute-start.5 = (bf16[24,9216]{1,0:T(8,128)(2,1)S(1)}, bf16[24,9216]{1,0:T(8,128)(2,1)S(1)}, u32[]{:S(2)}, u32[]{:S(2)}) collective-permute-start(bf16[24,9216]{1,0:T(8,128)(2,1)S(1)} %convert_element_type.55.refs_0_), channel_id=1, source_target_pairs={{1,0},{0,1},{3,2},{2,3},{5,4},{4,5},{7,6},{6,7},{9,8},{8,9},{11,10... | collective-permute-start | bytes 1327112 | tf_op jit(solution)/shard_map/ppermute | solution.py:438
  37.2 0.8 copy-start.9
  38.0 3.7 %collective-permute-start.8 = (bf16[24,9216]{1,0:T(8,128)(2,1)}, bf16[24,9216]{1,0:T(8,128)(2,1)}, u32[]{:S(2)}, u32[]{:S(2)}) collective-permute-start(bf16[24,9216]{1,0:T(8,128)(2,1)} %collective-permute-done.refs_2_), channel_id=1, source_target_pairs={{1,0},{0,1},{3,2},{2,3},{5,4},{4,5},{7,6},{6,7},{9,8},{8,9},{11,10... | collective-permute-start | bytes 1327112 | tf_op jit(solution)/shard_map/ppermute | solution.py:438
  39.1 15.5 %collective-permute-start.9 = (bf16[2,24,9216]{2,1,0:T(8,128)(2,1)}, bf16[2,24,9216]{2,1,0:T(8,128)(2,1)}, u32[]{:S(2)}, u32[]{:S(2)}) collective-permute-start(bf16[2,24,9216]{2,1,0:T(8,128)(2,1)} %collective-permute-done.1.refs_2_), channel_id=1, source_target_pairs={{1,0},{0,1},{3,2},{2,3},{5,4},{4,5},{7,6},{6,7},{9,8},{8,9},{11,10... | collective-permute-start | bytes 2654216 | tf_op jit(solution)/shard_map/ppermute | solution.py:438
  39.6 14.9 %collective-permute-start.7 = (bf16[1,24,9216]{2,1,0:T(8,128)(2,1)S(1)}, bf16[1,24,9216]{2,1,0:T(8,128)(2,1)}, u32[]{:S(2)}, u32[]{:S(2)}) collective-permute-start(bf16[1,24,9216]{2,1,0:T(8,128)(2,1)S(1)} %slice.31), channel_id=1, source_target_pairs={{0,4},{4,8},{8,12},{12,16},{16,20},{20,24},{24,28},{28,0},{1,5},{5... | collective-permute-start | bytes 1327112 | tf_op jit(solution)/shard_map/ppermute | solution.py:432
  41.1 13.4 %collective-permute-start.10 = (bf16[2,24,9216]{2,1,0:T(8,128)(2,1)}, bf16[2,24,9216]{2,1,0:T(8,128)(2,1)}, u32[]{:S(2)}, u32[]{:S(2)}) collective-permute-start(bf16[2,24,9216]{2,1,0:T(8,128)(2,1)} %collective-permute-done.2.refs_8_), channel_id=1, source_target_pairs={{1,0},{0,1},{3,2},{2,3},{5,4},{4,5},{7,6},{6,7},{9,8},{8,9},{11,10... | collective-permute-start | bytes 2654216 | tf_op jit(solution)/shard_map/ppermute | solution.py:438
  41.2 13.4 %collective-permute-start.11 = (bf16[1,24,9216]{2,1,0:T(8,128)(2,1)}, bf16[1,24,9216]{2,1,0:T(8,128)(2,1)}, u32[]{:S(2)}, u32[]{:S(2)}) collective-permute-start(bf16[1,24,9216]{2,1,0:T(8,128)(2,1)} %copy-done.8), channel_id=1, source_target_pairs={{1,0},{0,1},{3,2},{2,3},{5,4},{4,5},{7,6},{6,7},{9,8},{8,9},{11,10... | collective-permute-start | bytes 1327112 | tf_op jit(solution)/shard_map/ppermute | solution.py:438
  41.7 21.7 %collective-permute-start.6 = (bf16[2,24,9216]{2,1,0:T(8,128)(2,1)S(1)}, bf16[2,24,9216]{2,1,0:T(8,128)(2,1)}, u32[]{:S(2)}, u32[]{:S(2)}) collective-permute-start(bf16[2,24,9216]{2,1,0:T(8,128)(2,1)S(1)} %get-tuple-element.59), channel_id=1, source_target_pairs={{2,0},{3,1},{0,2},{1,3},{6,4},{7,5},{4,6},{5,7},{10,8},{11,9},{8,1... | collective-permute-start | bytes 2654216 | tf_op jit(solution)/shard_map/ppermute | solution.py:435
  63.3 5.2 %collective-permute-start.12 = (bf16[2,24,9216]{2,1,0:T(8,128)(2,1)}, bf16[2,24,9216]{2,1,0:T(8,128)(2,1)S(1)}, u32[]{:S(2)}, u32[]{:S(2)}) collective-permute-start(bf16[2,24,9216]{2,1,0:T(8,128)(2,1)} %collective-permute-done.6.refs_6_), channel_id=1, source_target_pairs={{1,0},{0,1},{3,2},{2,3},{5,4},{4,5},{7,6},{6,7},{9,8},{8,9},{11,10... | collective-permute-start | bytes 2654216 | tf_op jit(solution)/shard_map/ppermute | solution.py:438
  63.3 5.2 %collective-permute-start.17 = (bf16[1,24,9216]{2,1,0:T(8,128)(2,1)}, bf16[1,24,9216]{2,1,0:T(8,128)(2,1)S(1)}, u32[]{:S(2)}, u32[]{:S(2)}) collective-permute-start(bf16[1,24,9216]{2,1,0:T(8,128)(2,1)} %collective-permute-done.7.refs_10_), channel_id=1, source_target_pairs={{1,0},{0,1},{3,2},{2,3},{5,4},{4,5},{7,6},{6,7},{9,8},{8,9},{11,10... | collective-permute-start | bytes 1327112 | tf_op jit(solution)/shard_map/ppermute | solution.py:438
  63.8 21.6 %collective-permute-start.21 = (bf16[1,24,9216]{2,1,0:T(8,128)(2,1)}, bf16[1,24,9216]{2,1,0:T(8,128)(2,1)}, u32[]{:S(2)}, u32[]{:S(2)}) collective-permute-start(bf16[1,24,9216]{2,1,0:T(8,128)(2,1)} %copy-done.8), channel_id=1, source_target_pairs={{2,0},{3,1},{0,2},{1,3},{6,4},{7,5},{4,6},{5,7},{10,8},{11,9},{8,1... | collective-permute-start | bytes 1327112 | tf_op jit(solution)/shard_map/ppermute | solution.py:435
  66.4 19.5 %collective-permute-start.16 = (bf16[1,24,9216]{2,1,0:T(8,128)(2,1)S(1)}, bf16[1,24,9216]{2,1,0:T(8,128)(2,1)}, u32[]{:S(2)}, u32[]{:S(2)}) collective-permute-start(bf16[1,24,9216]{2,1,0:T(8,128)(2,1)S(1)} %slice.32), channel_id=1, source_target_pairs={{2,0},{3,1},{0,2},{1,3},{6,4},{7,5},{4,6},{5,7},{10,8},{11,9},{8,1... | collective-permute-start | bytes 1327112 | tf_op jit(solution)/shard_map/ppermute | solution.py:435
  67.0 16.8 %collective-permute-start.13 = (bf16[1,24,9216]{2,1,0:T(8,128)(2,1)S(1)}, bf16[1,24,9216]{2,1,0:T(8,128)(2,1)}, u32[]{:S(2)}, u32[]{:S(2)}) collective-permute-start(bf16[1,24,9216]{2,1,0:T(8,128)(2,1)S(1)} %get-tuple-element.70), channel_id=1, source_target_pairs={{0,4},{4,8},{8,12},{12,16},{16,20},{20,24},{24,28},{28,0},{1,5},{5... | collective-permute-start | bytes 1327112 | tf_op jit(solution)/shard_map/ppermute | solution.py:432
  68.5 0.8 copy-start.11
  69.3 0.9 copy-start.7
  83.7 2.3 %collective-permute-start.23 = (bf16[24,9216]{1,0:T(8,128)(2,1)}, bf16[24,9216]{1,0:T(8,128)(2,1)S(1)}, u32[]{:S(2)}, u32[]{:S(2)}) collective-permute-start(bf16[24,9216]{1,0:T(8,128)(2,1)} %get-tuple-element.89), channel_id=1, source_target_pairs={{1,0},{0,1},{3,2},{2,3},{5,4},{4,5},{7,6},{6,7},{9,8},{8,9},{11,10... | collective-permute-start | bytes 1327112 | tf_op jit(solution)/shard_map/ppermute | solution.py:438
  83.8 22.0 %collective-permute-start.15 = (bf16[1,24,9216]{2,1,0:T(8,128)(2,1)}, bf16[1,24,9216]{2,1,0:T(8,128)(2,1)}, u32[]{:S(2)}, u32[]{:S(2)}) collective-permute-start(bf16[1,24,9216]{2,1,0:T(8,128)(2,1)} %collective-permute-done.13.refs_8_), channel_id=1, source_target_pairs={{2,0},{3,1},{0,2},{1,3},{6,4},{7,5},{4,6},{5,7},{10,8},{11,9},{8,1... | collective-permute-start | bytes 1327112 | tf_op jit(solution)/shard_map/ppermute | solution.py:435
  85.3 37.6 %collective-permute-start.14 = (bf16[1,24,9216]{2,1,0:T(8,128)(2,1)}, bf16[1,24,9216]{2,1,0:T(8,128)(2,1)}, u32[]{:S(2)}, u32[]{:S(2)}) collective-permute-start(bf16[1,24,9216]{2,1,0:T(8,128)(2,1)} %collective-permute-done.13.refs_8_), channel_id=1, source_target_pairs={{1,0},{0,1},{3,2},{2,3},{5,4},{4,5},{7,6},{6,7},{9,8},{8,9},{11,10... | collective-permute-start | bytes 1327112 | tf_op jit(solution)/shard_map/ppermute | solution.py:438
  85.5 20.8 %collective-permute-start.22 = (bf16[1,24,9216]{2,1,0:T(8,128)(2,1)}, bf16[1,24,9216]{2,1,0:T(8,128)(2,1)S(1)}, u32[]{:S(2)}, u32[]{:S(2)}) collective-permute-start(bf16[1,24,9216]{2,1,0:T(8,128)(2,1)} %collective-permute-done.21.refs_10_), channel_id=1, source_target_pairs={{1,0},{0,1},{3,2},{2,3},{5,4},{4,5},{7,6},{6,7},{9,8},{8,9},{11,10... | collective-permute-start | bytes 1327112 | tf_op jit(solution)/shard_map/ppermute | solution.py:438
  85.8 5.4 %collective-permute-start.18 = (bf16[1,24,9216]{2,1,0:T(8,128)(2,1)}, bf16[1,24,9216]{2,1,0:T(8,128)(2,1)S(1)}, u32[]{:S(2)}, u32[]{:S(2)}) collective-permute-start(bf16[1,24,9216]{2,1,0:T(8,128)(2,1)} %collective-permute-done.16.refs_10_), channel_id=1, source_target_pairs={{1,0},{0,1},{3,2},{2,3},{5,4},{4,5},{7,6},{6,7},{9,8},{8,9},{11,10... | collective-permute-start | bytes 1327112 | tf_op jit(solution)/shard_map/ppermute | solution.py:438
  88.0 54.2 %collective-permute-start.25 = (bf16[24,9216]{1,0:T(8,128)(2,1)}, bf16[24,9216]{1,0:T(8,128)(2,1)}, u32[]{:S(2)}, u32[]{:S(2)}) collective-permute-start(bf16[24,9216]{1,0:T(8,128)(2,1)} %add_convert_fusion.2), channel_id=1, source_target_pairs={{0,28},{4,0},{8,4},{12,8},{16,12},{20,16},{24,20},{28,24},{1,29},{... | collective-permute-start | bytes 1327112 | tf_op jit(solution)/shard_map/ppermute | solution.py:432
  91.2 0.8 copy-start.12
  105.6 15.3 %collective-permute-start.20 = (bf16[24,9216]{1,0:T(8,128)(2,1)}, bf16[24,9216]{1,0:T(8,128)(2,1)}, u32[]{:S(2)}, u32[]{:S(2)}) collective-permute-start(bf16[24,9216]{1,0:T(8,128)(2,1)} %get-tuple-element.84), channel_id=1, source_target_pairs={{1,0},{0,1},{3,2},{2,3},{5,4},{4,5},{7,6},{6,7},{9,8},{8,9},{11,10... | collective-permute-start | bytes 1327112 | tf_op jit(solution)/shard_map/ppermute | solution.py:438
  105.8 17.2 %collective-permute-start.19 = (bf16[1,24,9216]{2,1,0:T(8,128)(2,1)}, bf16[1,24,9216]{2,1,0:T(8,128)(2,1)}, u32[]{:S(2)}, u32[]{:S(2)}) collective-permute-start(bf16[1,24,9216]{2,1,0:T(8,128)(2,1)} %collective-permute-done.15.refs_10_), channel_id=1, source_target_pairs={{1,0},{0,1},{3,2},{2,3},{5,4},{4,5},{7,6},{6,7},{9,8},{8,9},{11,10... | collective-permute-start | bytes 1327112 | tf_op jit(solution)/shard_map/ppermute | solution.py:438
  106.2 0.8 copy-start.10
  107.0 13.9 %copy-start.2 = (f32[24,9216]{1,0:T(8,128)S(1)}, f32[24,9216]{1,0:T(8,128)}, u32[]{:S(2)}) copy-start(f32[24,9216]{1,0:T(8,128)} %get-tuple-element.82) | copy-start | bytes 2654212
  120.8 16.1 %collective-permute-start.27 = (bf16[24,9216]{1,0:T(8,128)(2,1)}, bf16[24,9216]{1,0:T(8,128)(2,1)S(1)}, u32[]{:S(2)}, u32[]{:S(2)}) collective-permute-start(bf16[24,9216]{1,0:T(8,128)(2,1)} %get-tuple-element.104), channel_id=1, source_target_pairs={{1,0},{0,1},{3,2},{2,3},{5,4},{4,5},{7,6},{6,7},{9,8},{8,9},{11,10... | collective-permute-start | bytes 1327112 | tf_op jit(solution)/shard_map/ppermute | solution.py:438
  122.0 27.9 %collective-permute-start.26 = (bf16[24,9216]{1,0:T(8,128)(2,1)S(1)}, bf16[24,9216]{1,0:T(8,128)(2,1)}, u32[]{:S(2)}, u32[]{:S(2)}) collective-permute-start(bf16[24,9216]{1,0:T(8,128)(2,1)S(1)} %add_convert_fusion.3), channel_id=1, source_target_pairs={{0,28},{4,0},{8,4},{12,8},{16,12},{20,16},{24,20},{28,24},{1,29},{... | collective-permute-start | bytes 1327112 | tf_op jit(solution)/shard_map/ppermute | solution.py:432
  122.9 13.9 %copy-start = (f32[24,9216]{1,0:T(8,128)S(1)}, f32[24,9216]{1,0:T(8,128)}, u32[]{:S(2)}) copy-start(f32[24,9216]{1,0:T(8,128)} %get-tuple-element.103) | copy-start | bytes 2654212
  136.7 4.6 %copy-start.1 = (f32[24,9216]{1,0:T(8,128)S(1)}, f32[24,9216]{1,0:T(8,128)}, u32[]{:S(2)}) copy-start(f32[24,9216]{1,0:T(8,128)} %get-tuple-element.105) | copy-start | bytes 2654212
  136.7 4.6 %collective-permute-start.29 = (bf16[24,9216]{1,0:T(8,128)(2,1)}, bf16[24,9216]{1,0:T(8,128)(2,1)S(1)}, u32[]{:S(2)}, u32[]{:S(2)}) collective-permute-start(bf16[24,9216]{1,0:T(8,128)(2,1)} %get-tuple-element.106), channel_id=1, source_target_pairs={{1,0},{0,1},{3,2},{2,3},{5,4},{4,5},{7,6},{6,7},{9,8},{8,9},{11,10... | collective-permute-start | bytes 1327112 | tf_op jit(solution)/shard_map/ppermute | solution.py:438
  136.9 13.1 %copy-start.4 = (f32[24,9216]{1,0:T(8,128)S(1)}, f32[24,9216]{1,0:T(8,128)}, u32[]{:S(2)}) copy-start(f32[24,9216]{1,0:T(8,128)} %get-tuple-element.101) | copy-start | bytes 2654212
  136.9 13.0 %copy-start.5 = (f32[24,9216]{1,0:T(8,128)S(1)}, f32[24,9216]{1,0:T(8,128)}, u32[]{:S(2)}) copy-start(f32[24,9216]{1,0:T(8,128)} %get-tuple-element.102) | copy-start | bytes 2654212
  136.9 13.0 %collective-permute-start.28 = (bf16[24,9216]{1,0:T(8,128)(2,1)S(1)}, bf16[24,9216]{1,0:T(8,128)(2,1)S(1)}, u32[]{:S(2)}, u32[]{:S(2)}) collective-permute-start(bf16[24,9216]{1,0:T(8,128)(2,1)S(1)} %add_convert_fusion.1), channel_id=1, source_target_pairs={{0,28},{4,0},{8,4},{12,8},{16,12},{20,16},{24,20},{28,24},{1,29},{... | collective-permute-start | bytes 1327112 | tf_op jit(solution)/shard_map/ppermute | solution.py:432
  141.0 8.9 %collective-permute-start.24 = (bf16[2,24,9216]{2,1,0:T(8,128)(2,1)S(1)}, bf16[2,24,9216]{2,1,0:T(8,128)(2,1)S(1)}, u32[]{:S(2)}, u32[]{:S(2)}) collective-permute-start(bf16[2,24,9216]{2,1,0:T(8,128)(2,1)S(1)} %pad_maximum_fusion.1), channel_id=1, source_target_pairs={{1,0},{0,1},{3,2},{2,3},{5,4},{4,5},{7,6},{6,7},{9,8},{8,9},{11,10... | collective-permute-start | bytes 2654216 | tf_op jit(solution)/shard_map/ppermute | solution.py:438
  141.4 17.6 %collective-permute-start.30 = (bf16[24,9216]{1,0:T(8,128)(2,1)S(1)}, bf16[24,9216]{1,0:T(8,128)(2,1)S(1)}, u32[]{:S(2)}, u32[]{:S(2)}) collective-permute-start(bf16[24,9216]{1,0:T(8,128)(2,1)S(1)} %add_convert_fusion), channel_id=1, source_target_pairs={{0,28},{4,0},{8,4},{12,8},{16,12},{20,16},{24,20},{28,24},{1,29},{... | collective-permute-start | bytes 1327112 | tf_op jit(solution)/shard_map/ppermute | solution.py:432

commit v3 on v2

--- a/solution.py
+++ b/solution.py
@@ -104,7 +104,7 @@
     return picks
 
 
-def kernel_body(count, n, *refs):
+def kernel_body(count, n, place_ref, *refs):
     pieces, mirror = refs[:n], refs[n]
     lines, _ = line_spans(count)
     picks = refs[n + 1:n + 1 + len(lines)]
@@ -131,7 +131,7 @@
                 gx = step * 16 + u + e
                 back = lax.rem(count - gx, count)
                 both.append(jnp.concatenate([cut_ref[gx][:, :LANES], cut_ref[back][:, LANES:]], axis=0))
-            value = dot(mirror[...], jnp.concatenate(both, axis=1)) * (0.5 / count**3)
+            value = dot(mirror[place_ref[0]], jnp.concatenate(both, axis=1)) * (0.5 / count**3)
             for e in range(2):
                 out_ref[step * 16 + u + e] = value[:, e * LANES:(e + 1) * LANES]
         return carry
@@ -139,23 +139,23 @@
     lax.fori_loop(0, count // 16, join, 0)
 
 
-def whole_kernel(pieces, mirror, count):
+def whole_kernel(pieces, place, mirror, count):
     picks = line_selectors(count)
     vmem = pl.BlockSpec(memory_space=pltpu.VMEM)
     ins = [*pieces, mirror, *picks]
     return pl.pallas_call(
         functools.partial(kernel_body, count, len(pieces)),
         out_shape=jax.ShapeDtypeStruct((count, count, LANES), F32),
-        in_specs=[vmem] * len(ins),
+        in_specs=[pl.BlockSpec(memory_space=pltpu.SMEM)] + [vmem] * len(ins),
         out_specs=vmem,
         scratch_shapes=[pltpu.VMEM((count, count, 2 * LANES), BF)],
         compiler_params=pltpu.CompilerParams(vmem_limit_bytes=VMEM_BYTES),
         cost_estimate=pl.CostEstimate(flops=FLOPS, bytes_accessed=10**3, transcendentals=0),
         name="symmetric_kernel",
-    )(*ins)
-
-
-def unit_body(count, n, near, a_count, b_count, places, kept_held, core_ref, *refs):
+    )(place, *ins)
+
+
+def unit_body(count, n, near, a_count, b_count, places, kept_held, place_ref, *refs):
     refs = list(refs)
 
     def take(k):
@@ -171,7 +171,8 @@
     held, k_ref, x_ref, y_ref, z_ref, sent_near, sent_rest, kept_ref, s_ref, r_ref = take(10)
     in_sem, table_sem, kept_sem, sent_sem, out_sem = take(5)
     rows = pieces[0].shape[1]
-    where = [core_ref[0] * step + offset if step else offset for step, offset in places]
+    core = lax.rem(place_ref[0], near)
+    where = [core * step + offset if step else offset for step, offset in places]
     pitch = count + PITCH
     planes = near * rows
     steps = count // (per * GROUPS)
@@ -206,7 +207,7 @@
 
     small = [
         pltpu.make_async_copy(z_tables_ref, z_ref, table_sem.at[0]),
-        pltpu.make_async_copy(x_tables, x_ref, table_sem.at[1]),
+        pltpu.make_async_copy(x_tables.at[place_ref[0]], x_ref, table_sem.at[1]),
         pltpu.make_async_copy(y_tables, y_ref, table_sem.at[2]),
     ]
     k_copy = pltpu.make_async_copy(kern, k_ref, table_sem.at[3])
@@ -334,7 +335,7 @@
                     part = slice(p * rows, (p + 1) * rows)
                     for j in range(b_count):
                         if p:
-                            sent_rest[j, p - 1, :, lanes] = sent[j][part].astype(BF)
+                            sent_rest[j, p - 1, :, lanes] = sent[j][part].astype(sent_rest.dtype)
                         else:
                             sent_near[j, :, lanes] = sent[j][part]
                     for i in range(a_count):
@@ -358,7 +359,7 @@
             copy.wait()
 
 
-def unit(a, b, core, kern, x_tables, near, kept_in):
+def unit(a, b, place, kern, x_tables, near, kept_in):
     count = kern.shape[0]
     n = len(a[0])
     rows, width = a[0][0][0].shape[1:]
@@ -385,7 +386,7 @@
         scratch_shapes=[
             pltpu.VMEM((pieces, rows, width), BF),
             pltpu.VMEM(kern.shape, F32),
-            pltpu.VMEM(x_tables.shape, BF),
+            pltpu.VMEM(x_tables.shape[1:], BF),
             pltpu.VMEM(y_tables.shape, BF),
             pltpu.VMEM(z_all.shape, BF),
             pltpu.VMEM((b_count, rows, width), F32),
@@ -402,7 +403,7 @@
         compiler_params=pltpu.CompilerParams(vmem_limit_bytes=VMEM_BYTES),
         cost_estimate=pl.CostEstimate(flops=FLOPS, bytes_accessed=10**3, transcendentals=0),
         name="pair_potentials",
-    )(core, *ins)
+    )(place, *ins)
     sent = [outs[j * near:(j + 1) * near] for j in range(b_count)]
     kept = [outs[(b_count + i) * near:(b_count + i + 1) * near] for i in range(a_count)]
     return sent, kept
@@ -439,68 +440,63 @@
 
     order = [(s, t) for s in range(ga) for t in range(gb)]
     fwd, bwd, mirror = device_tables(count, ga, gb)
-    x_tables, mirror = (
-        lax.dynamic_index_in_dim(jnp.asarray(t), me, 0, False) for t in (np.concatenate([fwd, bwd], axis=1), mirror)
-    )
-
-    core = bi.astype(jnp.int32).reshape(1)
+    x_tables = jnp.asarray(np.concatenate([fwd, bwd], axis=1))
+
+    place = me.astype(jnp.int32).reshape(1)
 
     def others(x):
         return [to_b(x, t) for t in range(1, gb)]
 
+    own_near = [orbitals, *others(orbitals)]
+    late = after(orbitals, own_near[1])
+    rest = [late[gb + 1:]] if na > 1 else []
+    first_near = late[:gb + 1] if na > 1 else orbitals
     k_own = kernel.astype(BF)
-    shares = [orbitals[index * gb:(index + 1) * gb] for index in range(na)]
-    singles = [orbitals[j:j + 1] for j in range(gb, band_count)]
-    own_near = [orbitals, *others(orbitals)]
     k_near = [k_own, *others(k_own)]
     k_far = [to_a(k_own, s) for s in range(1, ga)]
-    own_far = [[to_a(shares[0], s) for s in range(1, ga)]]
-    block = hop(shares[0], DIST)
-    landed = [hop(x, DIST) for x in singles[:1]]
-    k_far, own_far, block, landed, shares, singles, own_near, k_near, x_tables, mirror = lax.optimization_barrier(
-        (k_far, own_far, block, landed, shares, singles, own_near, k_near, x_tables, mirror)
-    )
-
-    own_far += [[to_a(shares[index], s) for s in range(1, ga)] for index in range(1, na)]
-    forwarded = [hop(r[:1], DIST) for r in own_far[0]]
+    block = hop(first_near, DIST)
+    first_own = [to_a(orbitals[:gb], s) for s in range(1, ga)]
+    first_own, rest, own_near, k_far = lax.optimization_barrier((first_own, rest, own_near, k_far))
+    shares = [after(orbitals, *first_own)[index * gb:(index + 1) * gb] if index else None for index in range(na)]
+    if na > 1:
+        k_far = [after(r, *shares[1:]) for r in k_far]
+
     k_rows = list(k_near)
     for r in k_far:
         k_rows += [r, *others(r)]
-    kern = whole_kernel(k_rows, mirror, count)
-    far_pieces = [[[r, *others(r)] for r in own_far[0]]]
-    near_blocks = [[x, *others(x)] for x in [block, *landed[:1]]]
-    own_far, forwarded, singles, kern, far_pieces, near_blocks = lax.optimization_barrier(
-        (own_far, forwarded, singles, kern, far_pieces, near_blocks)
-    )
-
-    far_pieces += [[[r, *others(r)] for r in own_far[index]] for index in range(1, na)]
-    landed = [hop(x, DIST) for x in singles[1:]]
-    near_blocks += [[x, *others(x)] for x in landed]
+    kern = whole_kernel(k_rows, place, after(jnp.asarray(mirror), block), count)
+    near_blocks = [[x, *others(x)] for x in [block]]
+    far_pieces = [[[r, *others(r)] for r in first_own]]
+    forwarded = [hop(r, DIST) for r in first_own]
+    later_far = [[to_a(shares[index], s) for s in range(1, ga)] for index in range(1, na)]
+    later_far, forwarded, kern, rest = lax.optimization_barrier((later_far, forwarded, kern, rest))
+    far_pieces += [[[r, *others(r)] for r in far] for far in later_far]
+    first_far = [[r, *others(r)] for r in forwarded]
+    landed = [hop(x, DIST) for x in rest]
+
     own = []
     for index in range(na):
         pieces = [(r, 1, index * gb) for r in own_near]
         pieces += [(r, 1, 0) for group in far_pieces[index] for r in group]
         own.append(pieces)
-    near = [[(r, 0, j) for r in near_blocks[0]] for j in range(gb)]
-    near += [[(r, 0, 0) for r in blocks_near] for blocks_near in near_blocks[1:]]
+    near = [[(r, 0, j) for r in near_blocks[0]] for j in range(first_near.shape[0])]
 
     def partner(j, *events):
-        pieces = list(near[j])
+        if j < gb:
+            return near[j] + [(x, 0, j) for group in first_far for x in group]
+        pieces = list(near[j]) if j < len(near) else [(r, 0, 0) for r in [landed[0], *others(landed[0])]]
         for s in range(1, ga):
-            if j == 0:
-                r = forwarded[s - 1]
-            else:
-                r, _, offset = near[j][0]
-                r = to_a(r[offset:offset + 1], s)
-                if events:
-                    r = after(r, *events)
-            pieces += [(x, 0, 0) for x in [r, *others(r)]]
+            x = to_a(singles[j], s)
+            x = after(x, sent_by[j - gb])
+            pieces += [(y, 0, 0) for y in [x, *others(x)]]
         return pieces
 
     returned = [None] * band_count
     events = []
 
     def send_back(sent, j):
+        if j == band_count - 1 and per_unit == 1:
+            sent = [sent[0], *(after(x, returned[j - 2]) for x in sent[1:])]
         total = sent[0]
         for t in range(1, gb):
             total = total + to_b(sent[t], gb - t).astype(F32)
@@ -508,13 +504,23 @@
         events.append(total)
         returned[j] = hop(total, -DIST)
 
+    per_unit = 2 // na
     kept = None
     sent_by = []
-    per_unit = 2 // na
+    one = lax.optimization_barrier(jnp.ones((), BF))
+    singles = {}
     for u in range(0, band_count, per_unit):
-        b = [partner(j, *(sent_by[-2:-1] or sent_by)) for j in range(u, u + per_unit)]
-        tables = after(x_tables, events[-2]) if len(events) > 1 else x_tables
-        sent, kept = unit(own, b, core, kern, tables, gb, kept)
+        b = [partner(j) for j in range(u, u + per_unit)]
+        waits = []
+        if u > 1 and per_unit == 1:
+            waits = [*events[max(u - 2, 0):u if u == band_count - 1 else u - 1], *returned[:u - 2]]
+        if na > 1 and u < 2:
+            if u:
+                landed[0] = after(landed[0], sent_by[-1])
+            singles[gb + u] = landed[0] * one if u else after(block, later_far)[gb:gb + 1]
+            waits = [*waits, singles[gb + u]]
+        tables = after(x_tables, *waits) if waits else x_tables
+        sent, kept = unit(own, b, place, kern, tables, gb, kept)
         sent_by.append(sent[0][0])
         for e in range(per_unit):
             send_back(sent[e], u + e)

time: 162 us -> 150 us (0.926)
  local copies, waits for them, and re-layouts: 12.6 us -> 3.8 us
  starting transfers between devices: 25.8 us -> 20.7 us
    ppermute x8 -> x7, waiting for transfers between devices: 25.9 us -> 16.1 us  [hop(): lax.ppermute(x, 'band', [(i, (i + distance) % blocks) for i in range(bloc...]
    ppermute x6 -> x5, waiting for transfers between devices: 23.9 us -> 31.6 us  [to_a(): lax.ppermute(x, 'grid', [((i // gb + s) % ga * gb + i % gb, i) for i in r...]
    ppermute x8 -> x7, starting transfers between devices: 14.6 us -> 9.6 us  [hop(): lax.ppermute(x, 'band', [(i, (i + distance) % blocks) for i in range(bloc...]
    unnamed x26 -> x16, local copies, waits for them, and re-layouts: 4.75 us -> 0.04 us
    squeeze x2 -> x0, local copies, waits for them, and re-layouts: 2.98 us -> none  [local(): lax.dynamic_index_in_dim(jnp.asarray(t), me, 0, False)]
    ppermute x17 -> x15, waiting for transfers between devices: 0.04 us -> 2.19 us  [to_b(): lax.ppermute(x, 'grid', [(i // gb * gb + (i % gb + t) % gb, i) for i in r...]
    mul x0 -> x1, other arithmetic: none -> 1.86 us  [local(): landed[0] * one]
    slice x4 -> x5, local copies, waits for them, and re-layouts: 4.84 us -> 3.76 us  [the longest x1 1.41 us: local(): first_near = late[:gb + 1] if na > 1 else orbitals]
  transfers between devices with their start and end apart: 31 -> 27, of which waited for: 6 -> 9; matrix products, arithmetic and copies ran while one was open for 10% -> 9% of each run, Pallas kernels for 38% -> 42%
where the time goes in v3:
time: 150 us; the launch traced here: 149 us
  Pallas kernels  62.7 us (42%)
  waiting for transfers between devices  49.8 us (33%)
  starting transfers between devices  20.7 us (14%)
  other arithmetic  12 us (8%)
  local copies, waits for them, and re-layouts  3.8 us (3%)
    pallas_call x4, Pallas kernels, unit(): pl.pallas_call(functools.partial(unit_body, count, n, near, a_count, b_co...  55.3 us
    ppermute x5, waiting for transfers between devices, to_a(): lax.ppermute(x, 'grid', [((i // gb + s) % ga * gb + i % gb, i) for i in r...  31.6 us
    ppermute x7, waiting for transfers between devices, hop(): lax.ppermute(x, 'band', [(i, (i + distance) % blocks) for i in range(bloc...  16.1 us
    ppermute x7, starting transfers between devices, hop(): lax.ppermute(x, 'band', [(i, (i + distance) % blocks) for i in range(bloc...  9.6 us
    ppermute x5, starting transfers between devices, to_a(): lax.ppermute(x, 'grid', [((i // gb + s) % ga * gb + i % gb, i) for i in r...  7.47 us
    pallas_call x1, Pallas kernels, whole_kernel(): pl.pallas_call(functools.partial(kernel_body, count, len(pieces)), out_sh...  7.38 us
    another operation x2, other arithmetic, local(): jnp.stack([v + returned[j].astype(F32) if j < early else v for j, v in en...  3.66 us
    ppermute x15, starting transfers between devices, to_b(): lax.ppermute(x, 'grid', [(i // gb * gb + (i % gb + t) % gb, i) for i in r...  3.66 us
  transfers between devices with their start and end apart: 27, of which 9 were waited for; matrix products, arithmetic and copies ran while one was open for 9% of the time, Pallas kernels for 42%

profile of v3, /device:TPU:0, one launch (start us, length us, event | category | flops | bytes accessed | tf_op | source)
XLA Modules:
  0.0 149.2 jit_solution(15825227865790851999)
XLA Ops:
  0.0 0.5 collective-permute-start.1
  0.5 1.2 slice.24
  1.7 2.7 %collective-permute-start = (bf16[2,24,9216]{2,1,0:T(8,128)(2,1)S(1)}, bf16[2,24,9216]{2,1,0:T(8,128)(2,1)}, u32[]{:S(2)}, u32[]{:S(2)}) collective-permute-start(bf16[2,24,9216]{2,1,0:T(8,128)(2,1)S(1)} %slice.24), channel_id=1, source_target_pairs={{2,0},{3,1},{0,2},{1,3},{6,4},{7,5},{4,6},{5,7},{10,8},{11,9},{8,1... | collective-permute-start | bytes 2654216 | tf_op jit(solution)/shard_map/ppermute | solution.py:436
  4.4 1.4 slice.27
  5.8 2.6 %collective-permute-start.8 = (bf16[3,24,9216]{2,1,0:T(8,128)(2,1)S(1)}, bf16[3,24,9216]{2,1,0:T(8,128)(2,1)}, u32[]{:S(2)}, u32[]{:S(2)}) collective-permute-start(bf16[3,24,9216]{2,1,0:T(8,128)(2,1)S(1)} %slice.27), channel_id=1, source_target_pairs={{0,4},{4,8},{8,12},{12,16},{16,20},{20,24},{24,28},{28,0},{1,5},{5... | collective-permute-start | bytes 3981320 | tf_op jit(solution)/shard_map/ppermute | solution.py:433
  8.5 1.6 %collective-permute-start.2 = (bf16[24,9216]{1,0:T(8,128)(2,1)S(1)}, bf16[24,9216]{1,0:T(8,128)(2,1)}, u32[]{:S(2)}, u32[]{:S(2)}) collective-permute-start(bf16[24,9216]{1,0:T(8,128)(2,1)S(1)} %convert_element_type.55.refs_0_), channel_id=1, source_target_pairs={{2,0},{3,1},{0,2},{1,3},{6,4},{7,5},{4,6},{5,7},{10,8},{11,9},{8,1... | collective-permute-start | bytes 1327112 | tf_op jit(solution)/shard_map/ppermute | solution.py:436
  10.1 24.0 %collective-permute-done.2.refs_2_ = bf16[24,9216]{1,0:T(8,128)(2,1)} collective-permute-done((bf16[24,9216]{1,0:T(8,128)(2,1)S(1)}, bf16[24,9216]{1,0:T(8,128)(2,1)}, u32[]{:S(2)}, u32[]{:S(2)}) %collective-permute-start.2) | collective-permute-done | bytes 442400 | tf_op jit(solution)/shard_map/ppermute | solution.py:436
  34.2 0.1 collective-permute-start.7
  34.3 1.8 %collective-permute-start.4 = (bf16[2,24,9216]{2,1,0:T(8,128)(2,1)S(1)}, bf16[2,24,9216]{2,1,0:T(8,128)(2,1)}, u32[]{:S(2)}, u32[]{:S(2)}) collective-permute-start(bf16[2,24,9216]{2,1,0:T(8,128)(2,1)S(1)} %slice.26), channel_id=1, source_target_pairs={{2,0},{3,1},{0,2},{1,3},{6,4},{7,5},{4,6},{5,7},{10,8},{11,9},{8,1... | collective-permute-start | bytes 2654216 | tf_op jit(solution)/shard_map/ppermute | solution.py:436
  36.1 1.5 %collective-permute-start.5 = (bf16[2,24,9216]{2,1,0:T(8,128)(2,1)}, bf16[2,24,9216]{2,1,0:T(8,128)(2,1)}, u32[]{:S(2)}, u32[]{:S(2)}) collective-permute-start(bf16[2,24,9216]{2,1,0:T(8,128)(2,1)} %collective-permute-done.refs_2_), channel_id=1, source_target_pairs={{0,4},{4,8},{8,12},{12,16},{16,20},{20,24},{24,28},{28,0},{1,5},{5... | collective-permute-start | bytes 2654216 | tf_op jit(solution)/shard_map/ppermute | solution.py:433
  37.6 3.4 %collective-permute-done.8.refs_8_ = bf16[3,24,9216]{2,1,0:T(8,128)(2,1)} collective-permute-done((bf16[3,24,9216]{2,1,0:T(8,128)(2,1)S(1)}, bf16[3,24,9216]{2,1,0:T(8,128)(2,1)}, u32[]{:S(2)}, u32[]{:S(2)}) %collective-permute-start.8) | collective-permute-done | bytes 1327136 | tf_op jit(solution)/shard_map/ppermute | solution.py:433
  41.0 0.5 collective-permute-start.11
  41.6 7.4 %symmetric_kernel.1.refs_12_ = f32[96,96,128]{2,1,0:T(8,128)} custom-call(s32[1]{0:T(128)} %bitcast.place_ref, bf16[24,9216]{1,0:T(8,128)(2,1)} %copy-done.7, bf16[24,9216]{1,0:T(8,128)(2,1)} %collective-permute-done.6.refs_1_, bf16[24,9216]{1,0:T(8,128)(2,1)} %collective-permute-done.2.refs_2_, bf16[24,9216]{1,0:T(8,128)(2,1)} %collective-permute-done.7.refs_3_, ...), custom_call_target="tpu_custom_call" | custom-call | flops 99999997952 | bytes 1000 | tf_op jit(solution)/shard_map/symmetric_kernel/pallas_call | solution.py:146
  48.9 7.5 %collective-permute-done.4.refs_6_ = bf16[2,24,9216]{2,1,0:T(8,128)(2,1)} collective-permute-done((bf16[2,24,9216]{2,1,0:T(8,128)(2,1)S(1)}, bf16[2,24,9216]{2,1,0:T(8,128)(2,1)}, u32[]{:S(2)}, u32[]{:S(2)}) %collective-permute-start.4) | collective-permute-done | bytes 884768 | tf_op jit(solution)/shard_map/ppermute | solution.py:436
  56.5 4.5 %collective-permute-done.5.refs_10_ = bf16[2,24,9216]{2,1,0:T(8,128)(2,1)} collective-permute-done((bf16[2,24,9216]{2,1,0:T(8,128)(2,1)}, bf16[2,24,9216]{2,1,0:T(8,128)(2,1)}, u32[]{:S(2)}, u32[]{:S(2)}) %collective-permute-start.5) | collective-permute-done | bytes 884768 | tf_op jit(solution)/shard_map/ppermute | solution.py:433
  61.0 0.5 collective-permute-start.12
  61.5 1.0 slice.28
  62.5 0.6 collective-permute-start.17
  63.1 0.6 collective-permute-done.9.refs_7_
  63.7 1.3 collective-permute-done.12.refs_11_
  65.0 13.4 %pair_potentials.4 = (f32[24,9216]{1,0:T(8,128)}, bf16[24,9216]{1,0:T(8,128)(2,1)}, f32[24,9216]{1,0:T(8,128)}, f32[24,9216]{1,0:T(8,128)}, f32[24,9216]{1,0:T(8,128)}, /*index=5*/f32[24,9216]{1,0:T(8,128)}) custom-call(s32[1]{0:T(128)} %bitcast.place_ref, bf16[4,24,9216]{2,1,0:T(8,128)(2,1)} %refs_4_.3, ...), custom_call_target="tpu_custom_call" | custom-call | flops 99999997952 | bytes 1000 | tf_op jit(solution)/shard_map/pair_potentials/pallas_call | solution.py:376
  78.4 1.9 %broadcast_multiply_fusion = bf16[1,24,9216]{2,1,0:T(8,128)(2,1)} fusion(bf16[1,24,9216]{2,1,0:T(8,128)(2,1)} %collective-permute-done.10.refs_8_, bf16[]{:T(256)} %constant.51.clone.1), kind=kLoop, calls=%fused_computation.23 | loop fusion | flops 221184 | bytes 884738 | tf_op jit(solution)/shard_map/mul | solution.py:520
  80.3 0.8 collective-permute-start.14
  81.1 0.5 collective-permute-start.19
  81.6 14.0 %pair_potentials.5 = (f32[24,9216]{1,0:T(8,128)}, bf16[24,9216]{1,0:T(8,128)(2,1)}, f32[24,9216]{1,0:T(8,128)}, f32[24,9216]{1,0:T(8,128)}, f32[24,9216]{1,0:T(8,128)}, /*index=5*/f32[24,9216]{1,0:T(8,128)}) custom-call(s32[1]{0:T(128)} %bitcast.place_ref, bf16[4,24,9216]{2,1,0:T(8,128)(2,1)} %refs_4_.3, ...), custom_call_target="tpu_custom_call" | custom-call | flops 99999997952 | bytes 1000 | tf_op jit(solution)/shard_map/pair_potentials/pallas_call | solution.py:376
  95.6 0.6 collective-permute-start.16
  96.1 0.1 add_convert_fusion.2
  96.2 3.8 %collective-permute-start.21 = (bf16[24,9216]{1,0:T(8,128)(2,1)S(1)}, bf16[24,9216]{1,0:T(8,128)(2,1)}, u32[]{:S(2)}, u32[]{:S(2)}) collective-permute-start(bf16[24,9216]{1,0:T(8,128)(2,1)S(1)} %add_convert_fusion.2), channel_id=1, source_target_pairs={{0,28},{4,0},{8,4},{12,8},{16,12},{20,16},{24,20},{28,24},{1,29},{... | collective-permute-start | bytes 1327112 | tf_op jit(solution)/shard_map/ppermute | solution.py:433
  100.1 14.0 %pair_potentials.6 = (f32[24,9216]{1,0:T(8,128)}, bf16[24,9216]{1,0:T(8,128)(2,1)}, f32[24,9216]{1,0:T(8,128)}, f32[24,9216]{1,0:T(8,128)}, f32[24,9216]{1,0:T(8,128)}, /*index=5*/f32[24,9216]{1,0:T(8,128)}) custom-call(s32[1]{0:T(128)} %bitcast.place_ref, bf16[4,24,9216]{2,1,0:T(8,128)(2,1)} %refs_4_.3, ...), custom_call_target="tpu_custom_call" | custom-call | flops 99999997952 | bytes 1000 | tf_op jit(solution)/shard_map/pair_potentials/pallas_call | solution.py:376
  114.0 0.1 collective-permute-start.20
  114.1 0.5 collective-permute-start.15
  114.6 1.1 add_convert_fusion.3
  115.7 0.1 collective-permute-start.23
  115.8 0.3 collective-permute-done.20
  116.1 1.2 add_convert_fusion.1
  117.3 1.1 collective-permute-start.24
  118.4 13.9 %pair_potentials.7 = (f32[24,9216]{1,0:T(8,128)}, bf16[24,9216]{1,0:T(8,128)(2,1)}, f32[24,9216]{1,0:T(8,128)}, f32[24,9216]{1,0:T(8,128)}, f32[24,9216]{1,0:T(8,128)}, /*index=5*/f32[24,9216]{1,0:T(8,128)}) custom-call(s32[1]{0:T(128)} %bitcast.place_ref, bf16[4,24,9216]{2,1,0:T(8,128)(2,1)} %refs_4_.3, ...), custom_call_target="tpu_custom_call" | custom-call | flops 99999997952 | bytes 1000 | tf_op jit(solution)/shard_map/pair_potentials/pallas_call | solution.py:376
  132.4 0.1 collective-permute-start.25
  132.5 1.7 %convert_bitcast_fusion = (bf16[1,24,9216]{2,1,0:T(8,128)(2,1)S(1)}, bf16[1,24,9216]{2,1,0:T(8,128)(2,1)S(1)}) fusion(f32[24,9216]{1,0:T(8,128)} %get-tuple-element.91, f32[24,9216]{1,0:T(8,128)} %get-tuple-element.90), kind=kLoop, calls=%fused_computation.21 | loop fusion | flops 442368 | bytes 2654208 | tf_op jit(solution)/shard_map/stack | solution.py:530
  134.1 0.1 pad_maximum_fusion.1
  134.2 0.4 collective-permute-start.22
  134.7 0.1 add_convert_fusion
  134.7 0.4 collective-permute-start.26
  135.2 2.3 %collective-permute-done.24 = bf16[24,9216]{1,0:T(8,128)(2,1)} collective-permute-done((bf16[24,9216]{1,0:T(8,128)(2,1)S(1)}, bf16[24,9216]{1,0:T(8,128)(2,1)}, u32[]{:S(2)}, u32[]{:S(2)}) %collective-permute-start.24) | collective-permute-done | bytes 442400 | tf_op jit(solution)/shard_map/ppermute | solution.py:433
  137.5 1.6 %fusion.1 = (f32[1,24,9216]{2,1,0:T(8,128)S(1)}, f32[1,24,9216]{2,1,0:T(8,128)S(1)}, f32[1,24,9216]{2,1,0:T(8,128)S(1)}, f32[1,24,9216]{2,1,0:T(8,128)S(1)}) fusion(f32[24,9216]{1,0:T(8,128)S(1)} %copy-done.5, bf16[24,9216]{1,0:T(8,128)(2,1)} %collective-permute-done.21, pred[]{:T(512)S(6)} %eq.14, bf16[2,24,9216]{2,1,0:T(8,128)(2,1)S(1)} %collective-permute-done.22, ...), kind=kLoop, calls=%fused_computation.6 | loop fusion | flops 2654208 | bytes 7520258 | tf_op jit(solution)/shard_map/stack | solution.py:542
  139.1 2.0 %pad_maximum_fusion = f32[4,24,9216]{2,1,0:T(8,128)} fusion(f32[1,24,9216]{2,1,0:T(8,128)S(1)} %get-tuple-element.101, f32[1,24,9216]{2,1,0:T(8,128)S(1)} %get-tuple-element.102, f32[1,24,9216]{2,1,0:T(8,128)S(1)} %get-tuple-element.98, f32[1,24,9216]{2,1,0:T(8,128)S(1)} %get-tuple-element.97), kind=kLoop, calls=%fused_computation | loop fusion | flops 2654208 | bytes 7077888 | tf_op jit(solution)/shard_map/stack | solution.py:542
  141.2 5.8 %collective-permute-done.26 = bf16[24,9216]{1,0:T(8,128)(2,1)S(1)} collective-permute-done((bf16[24,9216]{1,0:T(8,128)(2,1)S(1)}, bf16[24,9216]{1,0:T(8,128)(2,1)S(1)}, u32[]{:S(2)}, u32[]{:S(2)}) %collective-permute-start.26) | collective-permute-done | bytes 442400 | tf_op jit(solution)/shard_map/ppermute | solution.py:433
  147.0 2.2 %fusion.7 = f32[4,24,9216]{2,1,0:T(8,128)} fusion(f32[4,24,9216]{2,1,0:T(8,128)} %pad_maximum_fusion, bf16[24,9216]{1,0:T(8,128)(2,1)S(1)} %collective-permute-done.26), kind=kLoop, calls=%fused_computation.13 | loop fusion | flops 442368 | bytes 2211840 | tf_op jit(solution)/shard_map/dynamic_update_slice | solution.py:545
  (43 shorter events, 0.2 us)
Async XLA Ops:
  0.0 10.1 %copy-start = (bf16[4,24,9216]{2,1,0:T(8,128)(2,1)S(1)}, bf16[4,24,9216]{2,1,0:T(8,128)(2,1)}, u32[]{:S(2)}) copy-start(bf16[4,24,9216]{2,1,0:T(8,128)(2,1)} %refs_4_.3) | copy-start | bytes 5308420
  0.0 8.5 %copy-start.4 = (f32[24,9216]{1,0:T(8,128)S(1)}, f32[24,9216]{1,0:T(8,128)}, u32[]{:S(2)}) copy-start(f32[24,9216]{1,0:T(8,128)} %param.17) | copy-start | bytes 2654212
  0.0 4.4 %collective-permute-start.1 = (bf16[4,24,9216]{2,1,0:T(8,128)(2,1)}, bf16[4,24,9216]{2,1,0:T(8,128)(2,1)}, u32[]{:S(2)}, u32[]{:S(2)}) collective-permute-start(bf16[4,24,9216]{2,1,0:T(8,128)(2,1)} %refs_4_.3), channel_id=1, source_target_pairs={{1,0},{0,1},{3,2},{2,3},{5,4},{4,5},{7,6},{6,7},{9,8},{8,9},{11,10... | collective-permute-start | bytes 5308424 | tf_op jit(solution)/shard_map/ppermute | solution.py:439
  1.7 32.5 %collective-permute-start = (bf16[2,24,9216]{2,1,0:T(8,128)(2,1)S(1)}, bf16[2,24,9216]{2,1,0:T(8,128)(2,1)}, u32[]{:S(2)}, u32[]{:S(2)}) collective-permute-start(bf16[2,24,9216]{2,1,0:T(8,128)(2,1)S(1)} %slice.24), channel_id=1, source_target_pairs={{2,0},{3,1},{0,2},{1,3},{6,4},{7,5},{4,6},{5,7},{10,8},{11,9},{8,1... | collective-permute-start | bytes 2654216 | tf_op jit(solution)/shard_map/ppermute | solution.py:436
  5.8 35.2 %collective-permute-start.8 = (bf16[3,24,9216]{2,1,0:T(8,128)(2,1)S(1)}, bf16[3,24,9216]{2,1,0:T(8,128)(2,1)}, u32[]{:S(2)}, u32[]{:S(2)}) collective-permute-start(bf16[3,24,9216]{2,1,0:T(8,128)(2,1)S(1)} %slice.27), channel_id=1, source_target_pairs={{0,4},{4,8},{8,12},{12,16},{16,20},{20,24},{24,28},{28,0},{1,5},{5... | collective-permute-start | bytes 3981320 | tf_op jit(solution)/shard_map/ppermute | solution.py:433
  8.5 33.0 %copy-start.7 = (bf16[24,9216]{1,0:T(8,128)(2,1)}, bf16[24,9216]{1,0:T(8,128)(2,1)S(1)}, u32[]{:S(2)}) copy-start(bf16[24,9216]{1,0:T(8,128)(2,1)S(1)} %convert_element_type.55.refs_0_) | copy-start | bytes 1327108
  8.5 25.6 %collective-permute-start.2 = (bf16[24,9216]{1,0:T(8,128)(2,1)S(1)}, bf16[24,9216]{1,0:T(8,128)(2,1)}, u32[]{:S(2)}, u32[]{:S(2)}) collective-permute-start(bf16[24,9216]{1,0:T(8,128)(2,1)S(1)} %convert_element_type.55.refs_0_), channel_id=1, source_target_pairs={{2,0},{3,1},{0,2},{1,3},{6,4},{7,5},{4,6},{5,7},{10,8},{11,9},{8,1... | collective-permute-start | bytes 1327112 | tf_op jit(solution)/shard_map/ppermute | solution.py:436
  10.1 31.0 %collective-permute-start.6 = (bf16[24,9216]{1,0:T(8,128)(2,1)S(1)}, bf16[24,9216]{1,0:T(8,128)(2,1)}, u32[]{:S(2)}, u32[]{:S(2)}) collective-permute-start(bf16[24,9216]{1,0:T(8,128)(2,1)S(1)} %convert_element_type.55.refs_0_), channel_id=1, source_target_pairs={{1,0},{0,1},{3,2},{2,3},{5,4},{4,5},{7,6},{6,7},{9,8},{8,9},{11,10... | collective-permute-start | bytes 1327112 | tf_op jit(solution)/shard_map/ppermute | solution.py:439
  34.2 7.3 %collective-permute-start.7 = (bf16[24,9216]{1,0:T(8,128)(2,1)}, bf16[24,9216]{1,0:T(8,128)(2,1)}, u32[]{:S(2)}, u32[]{:S(2)}) collective-permute-start(bf16[24,9216]{1,0:T(8,128)(2,1)} %collective-permute-done.2.refs_2_), channel_id=1, source_target_pairs={{1,0},{0,1},{3,2},{2,3},{5,4},{4,5},{7,6},{6,7},{9,8},{8,9},{11,10... | collective-permute-start | bytes 1327112 | tf_op jit(solution)/shard_map/ppermute | solution.py:439
  34.3 22.2 %collective-permute-start.4 = (bf16[2,24,9216]{2,1,0:T(8,128)(2,1)S(1)}, bf16[2,24,9216]{2,1,0:T(8,128)(2,1)}, u32[]{:S(2)}, u32[]{:S(2)}) collective-permute-start(bf16[2,24,9216]{2,1,0:T(8,128)(2,1)S(1)} %slice.26), channel_id=1, source_target_pairs={{2,0},{3,1},{0,2},{1,3},{6,4},{7,5},{4,6},{5,7},{10,8},{11,9},{8,1... | collective-permute-start | bytes 2654216 | tf_op jit(solution)/shard_map/ppermute | solution.py:436
  36.1 24.8 %collective-permute-start.5 = (bf16[2,24,9216]{2,1,0:T(8,128)(2,1)}, bf16[2,24,9216]{2,1,0:T(8,128)(2,1)}, u32[]{:S(2)}, u32[]{:S(2)}) collective-permute-start(bf16[2,24,9216]{2,1,0:T(8,128)(2,1)} %collective-permute-done.refs_2_), channel_id=1, source_target_pairs={{0,4},{4,8},{8,12},{12,16},{16,20},{20,24},{24,28},{28,0},{1,5},{5... | collective-permute-start | bytes 2654216 | tf_op jit(solution)/shard_map/ppermute | solution.py:433
  41.0 22.1 %collective-permute-start.3 = (bf16[2,24,9216]{2,1,0:T(8,128)(2,1)}, bf16[2,24,9216]{2,1,0:T(8,128)(2,1)}, u32[]{:S(2)}, u32[]{:S(2)}) collective-permute-start(bf16[2,24,9216]{2,1,0:T(8,128)(2,1)} %collective-permute-done.refs_2_), channel_id=1, source_target_pairs={{1,0},{0,1},{3,2},{2,3},{5,4},{4,5},{7,6},{6,7},{9,8},{8,9},{11,10... | collective-permute-start | bytes 2654216 | tf_op jit(solution)/shard_map/ppermute | solution.py:439
  41.0 23.9 %collective-permute-start.11 = (bf16[3,24,9216]{2,1,0:T(8,128)(2,1)}, bf16[3,24,9216]{2,1,0:T(8,128)(2,1)}, u32[]{:S(2)}, u32[]{:S(2)}) collective-permute-start(bf16[3,24,9216]{2,1,0:T(8,128)(2,1)} %collective-permute-done.8.refs_8_), channel_id=1, source_target_pairs={{1,0},{0,1},{3,2},{2,3},{5,4},{4,5},{7,6},{6,7},{9,8},{8,9},{11,10... | collective-permute-start | bytes 3981320 | tf_op jit(solution)/shard_map/ppermute | solution.py:439
  61.0 2.8 %collective-permute-start.9 = (bf16[2,24,9216]{2,1,0:T(8,128)(2,1)}, bf16[2,24,9216]{2,1,0:T(8,128)(2,1)}, u32[]{:S(2)}, u32[]{:S(2)}) collective-permute-start(bf16[2,24,9216]{2,1,0:T(8,128)(2,1)} %collective-permute-done.4.refs_6_), channel_id=1, source_target_pairs={{1,0},{0,1},{3,2},{2,3},{5,4},{4,5},{7,6},{6,7},{9,8},{8,9},{11,10... | collective-permute-start | bytes 2654216 | tf_op jit(solution)/shard_map/ppermute | solution.py:439
  61.0 4.0 %collective-permute-start.12 = (bf16[2,24,9216]{2,1,0:T(8,128)(2,1)}, bf16[2,24,9216]{2,1,0:T(8,128)(2,1)}, u32[]{:S(2)}, u32[]{:S(2)}) collective-permute-start(bf16[2,24,9216]{2,1,0:T(8,128)(2,1)} %collective-permute-done.5.refs_10_), channel_id=1, source_target_pairs={{1,0},{0,1},{3,2},{2,3},{5,4},{4,5},{7,6},{6,7},{9,8},{8,9},{11,10... | collective-permute-start | bytes 2654216 | tf_op jit(solution)/shard_map/ppermute | solution.py:439
  62.5 19.1 %collective-permute-start.17 = (bf16[1,24,9216]{2,1,0:T(8,128)(2,1)S(1)}, bf16[1,24,9216]{2,1,0:T(8,128)(2,1)}, u32[]{:S(2)}, u32[]{:S(2)}) collective-permute-start(bf16[1,24,9216]{2,1,0:T(8,128)(2,1)S(1)} %slice.28), channel_id=1, source_target_pairs={{2,0},{3,1},{0,2},{1,3},{6,4},{7,5},{4,6},{5,7},{10,8},{11,9},{8,1... | collective-permute-start | bytes 1327112 | tf_op jit(solution)/shard_map/ppermute | solution.py:436
  63.1 15.3 %collective-permute-start.10 = (bf16[1,24,9216]{2,1,0:T(8,128)(2,1)S(1)}, bf16[1,24,9216]{2,1,0:T(8,128)(2,1)}, u32[]{:S(2)}, u32[]{:S(2)}) collective-permute-start(bf16[1,24,9216]{2,1,0:T(8,128)(2,1)S(1)} %slice.25), channel_id=1, source_target_pairs={{0,4},{4,8},{8,12},{12,16},{16,20},{20,24},{24,28},{28,0},{1,5},{5... | collective-permute-start | bytes 1327112 | tf_op jit(solution)/shard_map/ppermute | solution.py:433
  80.3 33.8 %collective-permute-start.14 = (bf16[1,24,9216]{2,1,0:T(8,128)(2,1)}, bf16[1,24,9216]{2,1,0:T(8,128)(2,1)}, u32[]{:S(2)}, u32[]{:S(2)}) collective-permute-start(bf16[1,24,9216]{2,1,0:T(8,128)(2,1)} %broadcast_multiply_fusion), channel_id=1, source_target_pairs={{2,0},{3,1},{0,2},{1,3},{6,4},{7,5},{4,6},{5,7},{10,8},{11,9},{8,1... | collective-permute-start | bytes 1327112 | tf_op jit(solution)/shard_map/ppermute | solution.py:436
  81.1 37.3 %collective-permute-start.13 = (bf16[1,24,9216]{2,1,0:T(8,128)(2,1)}, bf16[1,24,9216]{2,1,0:T(8,128)(2,1)}, u32[]{:S(2)}, u32[]{:S(2)}) collective-permute-start(bf16[1,24,9216]{2,1,0:T(8,128)(2,1)} %collective-permute-done.10.refs_8_), channel_id=1, source_target_pairs={{1,0},{0,1},{3,2},{2,3},{5,4},{4,5},{7,6},{6,7},{9,8},{8,9},{11,10... | collective-permute-start | bytes 1327112 | tf_op jit(solution)/shard_map/ppermute | solution.py:439
  81.1 15.1 %collective-permute-start.19 = (bf16[24,9216]{1,0:T(8,128)(2,1)}, bf16[24,9216]{1,0:T(8,128)(2,1)S(1)}, u32[]{:S(2)}, u32[]{:S(2)}) collective-permute-start(bf16[24,9216]{1,0:T(8,128)(2,1)} %get-tuple-element.77), channel_id=1, source_target_pairs={{1,0},{0,1},{3,2},{2,3},{5,4},{4,5},{7,6},{6,7},{9,8},{8,9},{11,10... | collective-permute-start | bytes 1327112 | tf_op jit(solution)/shard_map/ppermute | solution.py:439
  81.6 18.5 %collective-permute-start.18 = (bf16[1,24,9216]{2,1,0:T(8,128)(2,1)}, bf16[1,24,9216]{2,1,0:T(8,128)(2,1)}, u32[]{:S(2)}, u32[]{:S(2)}) collective-permute-start(bf16[1,24,9216]{2,1,0:T(8,128)(2,1)} %collective-permute-done.17.refs_10_), channel_id=1, source_target_pairs={{1,0},{0,1},{3,2},{2,3},{5,4},{4,5},{7,6},{6,7},{9,8},{8,9},{11,10... | collective-permute-start | bytes 1327112 | tf_op jit(solution)/shard_map/ppermute | solution.py:439
  81.6 14.6 %copy-start.2 = (f32[24,9216]{1,0:T(8,128)S(1)}, f32[24,9216]{1,0:T(8,128)}, u32[]{:S(2)}) copy-start(f32[24,9216]{1,0:T(8,128)} %get-tuple-element.66) | copy-start | bytes 2654212
  95.6 19.0 %collective-permute-start.16 = (bf16[24,9216]{1,0:T(8,128)(2,1)}, bf16[24,9216]{1,0:T(8,128)(2,1)}, u32[]{:S(2)}, u32[]{:S(2)}) collective-permute-start(bf16[24,9216]{1,0:T(8,128)(2,1)} %get-tuple-element.75), channel_id=1, source_target_pairs={{1,0},{0,1},{3,2},{2,3},{5,4},{4,5},{7,6},{6,7},{9,8},{8,9},{11,10... | collective-permute-start | bytes 1327112 | tf_op jit(solution)/shard_map/ppermute | solution.py:439
  96.2 22.2 %collective-permute-start.21 = (bf16[24,9216]{1,0:T(8,128)(2,1)S(1)}, bf16[24,9216]{1,0:T(8,128)(2,1)}, u32[]{:S(2)}, u32[]{:S(2)}) collective-permute-start(bf16[24,9216]{1,0:T(8,128)(2,1)S(1)} %add_convert_fusion.2), channel_id=1, source_target_pairs={{0,28},{4,0},{8,4},{12,8},{16,12},{20,16},{24,20},{28,24},{1,29},{... | collective-permute-start | bytes 1327112 | tf_op jit(solution)/shard_map/ppermute | solution.py:433
  100.0 14.6 %copy-start.1 = (f32[24,9216]{1,0:T(8,128)S(1)}, f32[24,9216]{1,0:T(8,128)}, u32[]{:S(2)}) copy-start(f32[24,9216]{1,0:T(8,128)} %get-tuple-element.73) | copy-start | bytes 2654212
  114.0 2.1 %collective-permute-start.20 = (bf16[24,9216]{1,0:T(8,128)(2,1)}, bf16[24,9216]{1,0:T(8,128)(2,1)S(1)}, u32[]{:S(2)}, u32[]{:S(2)}) collective-permute-start(bf16[24,9216]{1,0:T(8,128)(2,1)} %get-tuple-element.84), channel_id=1, source_target_pairs={{1,0},{0,1},{3,2},{2,3},{5,4},{4,5},{7,6},{6,7},{9,8},{8,9},{11,10... | collective-permute-start | bytes 1327112 | tf_op jit(solution)/shard_map/ppermute | solution.py:439
  114.1 4.3 %collective-permute-start.15 = (bf16[1,24,9216]{2,1,0:T(8,128)(2,1)}, bf16[1,24,9216]{2,1,0:T(8,128)(2,1)}, u32[]{:S(2)}, u32[]{:S(2)}) collective-permute-start(bf16[1,24,9216]{2,1,0:T(8,128)(2,1)} %collective-permute-done.14.refs_10_), channel_id=1, source_target_pairs={{1,0},{0,1},{3,2},{2,3},{5,4},{4,5},{7,6},{6,7},{9,8},{8,9},{11,10... | collective-permute-start | bytes 1327112 | tf_op jit(solution)/shard_map/ppermute | solution.py:439
  115.7 16.7 %collective-permute-start.23 = (bf16[24,9216]{1,0:T(8,128)(2,1)S(1)}, bf16[24,9216]{1,0:T(8,128)(2,1)S(1)}, u32[]{:S(2)}, u32[]{:S(2)}) collective-permute-start(bf16[24,9216]{1,0:T(8,128)(2,1)S(1)} %add_convert_fusion.3), channel_id=1, source_target_pairs={{0,28},{4,0},{8,4},{12,8},{16,12},{20,16},{24,20},{28,24},{1,29},{... | collective-permute-start | bytes 1327112 | tf_op jit(solution)/shard_map/ppermute | solution.py:433
  117.3 20.2 %collective-permute-start.24 = (bf16[24,9216]{1,0:T(8,128)(2,1)S(1)}, bf16[24,9216]{1,0:T(8,128)(2,1)}, u32[]{:S(2)}, u32[]{:S(2)}) collective-permute-start(bf16[24,9216]{1,0:T(8,128)(2,1)S(1)} %add_convert_fusion.1), channel_id=1, source_target_pairs={{0,28},{4,0},{8,4},{12,8},{16,12},{20,16},{24,20},{28,24},{1,29},{... | collective-permute-start | bytes 1327112 | tf_op jit(solution)/shard_map/ppermute | solution.py:433
  132.3 2.3 %copy-start.3 = (f32[24,9216]{1,0:T(8,128)S(1)}, f32[24,9216]{1,0:T(8,128)}, u32[]{:S(2)}) copy-start(f32[24,9216]{1,0:T(8,128)} %get-tuple-element.94) | copy-start | bytes 2654212
  132.4 5.1 %copy-start.5 = (f32[24,9216]{1,0:T(8,128)S(1)}, f32[24,9216]{1,0:T(8,128)}, u32[]{:S(2)}) copy-start(f32[24,9216]{1,0:T(8,128)} %get-tuple-element.92) | copy-start | bytes 2654212
  132.4 5.1 %copy-start.6 = (f32[24,9216]{1,0:T(8,128)S(1)}, f32[24,9216]{1,0:T(8,128)}, u32[]{:S(2)}) copy-start(f32[24,9216]{1,0:T(8,128)} %get-tuple-element.93) | copy-start | bytes 2654212
  132.4 2.3 %collective-permute-start.25 = (bf16[24,9216]{1,0:T(8,128)(2,1)}, bf16[24,9216]{1,0:T(8,128)(2,1)S(1)}, u32[]{:S(2)}, u32[]{:S(2)}) collective-permute-start(bf16[24,9216]{1,0:T(8,128)(2,1)} %get-tuple-element.96), channel_id=1, source_target_pairs={{1,0},{0,1},{3,2},{2,3},{5,4},{4,5},{7,6},{6,7},{9,8},{8,9},{11,10... | collective-permute-start | bytes 1327112 | tf_op jit(solution)/shard_map/ppermute | solution.py:439
  134.2 3.3 %collective-permute-start.22 = (bf16[2,24,9216]{2,1,0:T(8,128)(2,1)S(1)}, bf16[2,24,9216]{2,1,0:T(8,128)(2,1)S(1)}, u32[]{:S(2)}, u32[]{:S(2)}) collective-permute-start(bf16[2,24,9216]{2,1,0:T(8,128)(2,1)S(1)} %pad_maximum_fusion.1), channel_id=1, source_target_pairs={{1,0},{0,1},{3,2},{2,3},{5,4},{4,5},{7,6},{6,7},{9,8},{8,9},{11,10... | collective-permute-start | bytes 2654216 | tf_op jit(solution)/shard_map/ppermute | solution.py:439
  134.7 12.3 %collective-permute-start.26 = (bf16[24,9216]{1,0:T(8,128)(2,1)S(1)}, bf16[24,9216]{1,0:T(8,128)(2,1)S(1)}, u32[]{:S(2)}, u32[]{:S(2)}) collective-permute-start(bf16[24,9216]{1,0:T(8,128)(2,1)S(1)} %add_convert_fusion), channel_id=1, source_target_pairs={{0,28},{4,0},{8,4},{12,8},{16,12},{20,16},{24,20},{28,24},{1,29},{... | collective-permute-start | bytes 1327112 | tf_op jit(solution)/shard_map/ppermute | solution.py:433

commit v4 on v3

--- a/solution.py
+++ b/solution.py
@@ -13,7 +13,7 @@
 LANES = 128
 TILES = 3
 GROUPS = 12
-UNROLL = 12
+UNROLL = 24
 CHUNKS = 2
 PITCH = 4
 BF = jnp.bfloat16
@@ -205,12 +205,14 @@
                 )
         return copies
 
+    cut_rows = sum(2 * (t1 - t0) * LANES for t0, t1 in lines)
     small = [
-        pltpu.make_async_copy(z_tables_ref, z_ref, table_sem.at[0]),
+        pltpu.make_async_copy(z_tables_ref.at[:cut_rows], z_ref.at[:cut_rows], table_sem.at[0]),
         pltpu.make_async_copy(x_tables.at[place_ref[0]], x_ref, table_sem.at[1]),
         pltpu.make_async_copy(y_tables, y_ref, table_sem.at[2]),
     ]
     k_copy = pltpu.make_async_copy(kern, k_ref, table_sem.at[3])
+    lay_copy = pltpu.make_async_copy(z_tables_ref.at[cut_rows:], z_ref.at[cut_rows:], table_sem.at[4])
     kept_copies = []
     if kept_held:
         for i in range(a_count):
@@ -227,6 +229,7 @@
             piece_in(part, p).start()
     small[2].start()
     k_copy.start()
+    lay_copy.start()
     for copy in kept_copies:
         copy.start()
 
@@ -306,6 +309,7 @@
         return carry
 
     lax.fori_loop(0, count // (per * UNROLL), middle, 0)
+    lay_copy.wait()
     for copy in kept_copies:
         copy.wait()
 
@@ -395,7 +399,7 @@
             pltpu.VMEM((2 * count * (count + PITCH), LANES), F32),
             pltpu.VMEM((2 * count * (count + PITCH), LANES), F32),
             pltpu.SemaphoreType.DMA((CHUNKS, pieces)),
-            pltpu.SemaphoreType.DMA((4,)),
+            pltpu.SemaphoreType.DMA((5,)),
             pltpu.SemaphoreType.DMA((a_count * near,)),
             pltpu.SemaphoreType.DMA((CHUNKS, b_count * near)),
             pltpu.SemaphoreType.DMA((CHUNKS, a_count * near)),

time: 150 us -> 148 us (0.987)
  transfers between devices with their start and end apart: 27 -> 27, of which waited for: 9 -> 9; matrix products, arithmetic and copies ran while one was open for 9% -> 9% of each run, Pallas kernels for 42% -> 41%
where the time goes in v4:
time: 148 us
  Pallas kernels  61.3 us (41%)
  waiting for transfers between devices  49.8 us (34%)
  starting transfers between devices  21 us (14%)
  other arithmetic  12 us (8%)
  local copies, waits for them, and re-layouts  3.8 us (3%)
    pallas_call x4, Pallas kernels, unit(): pl.pallas_call(functools.partial(unit_body, count, n, near, a_count, b_co...  53.9 us
    ppermute x5, waiting for transfers between devices, to_a(): lax.ppermute(x, 'grid', [((i // gb + s) % ga * gb + i % gb, i) for i in r...  31.6 us
    ppermute x7, waiting for transfers between devices, hop(): lax.ppermute(x, 'band', [(i, (i + distance) % blocks) for i in range(bloc...  16.1 us
    ppermute x7, starting transfers between devices, hop(): lax.ppermute(x, 'band', [(i, (i + distance) % blocks) for i in range(bloc...  9.43 us
    ppermute x5, starting transfers between devices, to_a(): lax.ppermute(x, 'grid', [((i // gb + s) % ga * gb + i % gb, i) for i in r...  7.91 us
    pallas_call x1, Pallas kernels, whole_kernel(): pl.pallas_call(functools.partial(kernel_body, count, len(pieces)), out_sh...  7.38 us
    another operation x2, other arithmetic, local(): jnp.stack([v + returned[j].astype(F32) if j < early else v for j, v in en...  3.66 us
    ppermute x15, starting transfers between devices, to_b(): lax.ppermute(x, 'grid', [(i // gb * gb + (i % gb + t) % gb, i) for i in r...  3.65 us
  transfers between devices with their start and end apart: 27, of which 9 were waited for; matrix products, arithmetic and copies ran while one was open for 9% of the time, Pallas kernels for 41%

profile of v4, /device:TPU:0, one launch (start us, length us, event | category | flops | bytes accessed | tf_op | source)
XLA Modules:
  0.0 148.1 jit_solution(7873768047170843463)
XLA Ops:
  0.0 0.5 collective-permute-start.1
  0.5 1.2 slice.24
  1.7 2.7 %collective-permute-start = (bf16[2,24,9216]{2,1,0:T(8,128)(2,1)S(1)}, bf16[2,24,9216]{2,1,0:T(8,128)(2,1)}, u32[]{:S(2)}, u32[]{:S(2)}) collective-permute-start(bf16[2,24,9216]{2,1,0:T(8,128)(2,1)S(1)} %slice.24), channel_id=1, source_target_pairs={{2,0},{3,1},{0,2},{1,3},{6,4},{7,5},{4,6},{5,7},{10,8},{11,9},{8,1... | collective-permute-start | bytes 2654216 | tf_op jit(solution)/shard_map/ppermute | solution.py:440
  4.4 1.4 slice.27
  5.8 2.6 %collective-permute-start.8 = (bf16[3,24,9216]{2,1,0:T(8,128)(2,1)S(1)}, bf16[3,24,9216]{2,1,0:T(8,128)(2,1)}, u32[]{:S(2)}, u32[]{:S(2)}) collective-permute-start(bf16[3,24,9216]{2,1,0:T(8,128)(2,1)S(1)} %slice.27), channel_id=1, source_target_pairs={{0,4},{4,8},{8,12},{12,16},{16,20},{20,24},{24,28},{28,0},{1,5},{5... | collective-permute-start | bytes 3981320 | tf_op jit(solution)/shard_map/ppermute | solution.py:437
  8.5 1.6 %collective-permute-start.2 = (bf16[24,9216]{1,0:T(8,128)(2,1)S(1)}, bf16[24,9216]{1,0:T(8,128)(2,1)}, u32[]{:S(2)}, u32[]{:S(2)}) collective-permute-start(bf16[24,9216]{1,0:T(8,128)(2,1)S(1)} %convert_element_type.55.refs_0_), channel_id=1, source_target_pairs={{2,0},{3,1},{0,2},{1,3},{6,4},{7,5},{4,6},{5,7},{10,8},{11,9},{8,1... | collective-permute-start | bytes 1327112 | tf_op jit(solution)/shard_map/ppermute | solution.py:440
  10.1 24.0 %collective-permute-done.2.refs_2_ = bf16[24,9216]{1,0:T(8,128)(2,1)} collective-permute-done((bf16[24,9216]{1,0:T(8,128)(2,1)S(1)}, bf16[24,9216]{1,0:T(8,128)(2,1)}, u32[]{:S(2)}, u32[]{:S(2)}) %collective-permute-start.2) | collective-permute-done | bytes 442400 | tf_op jit(solution)/shard_map/ppermute | solution.py:440
  34.2 0.1 collective-permute-start.7
  34.3 1.8 %collective-permute-start.4 = (bf16[2,24,9216]{2,1,0:T(8,128)(2,1)S(1)}, bf16[2,24,9216]{2,1,0:T(8,128)(2,1)}, u32[]{:S(2)}, u32[]{:S(2)}) collective-permute-start(bf16[2,24,9216]{2,1,0:T(8,128)(2,1)S(1)} %slice.26), channel_id=1, source_target_pairs={{2,0},{3,1},{0,2},{1,3},{6,4},{7,5},{4,6},{5,7},{10,8},{11,9},{8,1... | collective-permute-start | bytes 2654216 | tf_op jit(solution)/shard_map/ppermute | solution.py:440
  36.1 1.5 %collective-permute-start.5 = (bf16[2,24,9216]{2,1,0:T(8,128)(2,1)}, bf16[2,24,9216]{2,1,0:T(8,128)(2,1)}, u32[]{:S(2)}, u32[]{:S(2)}) collective-permute-start(bf16[2,24,9216]{2,1,0:T(8,128)(2,1)} %collective-permute-done.refs_2_), channel_id=1, source_target_pairs={{0,4},{4,8},{8,12},{12,16},{16,20},{20,24},{24,28},{28,0},{1,5},{5... | collective-permute-start | bytes 2654216 | tf_op jit(solution)/shard_map/ppermute | solution.py:437
  37.6 3.4 %collective-permute-done.8.refs_8_ = bf16[3,24,9216]{2,1,0:T(8,128)(2,1)} collective-permute-done((bf16[3,24,9216]{2,1,0:T(8,128)(2,1)S(1)}, bf16[3,24,9216]{2,1,0:T(8,128)(2,1)}, u32[]{:S(2)}, u32[]{:S(2)}) %collective-permute-start.8) | collective-permute-done | bytes 1327136 | tf_op jit(solution)/shard_map/ppermute | solution.py:437
  41.0 0.5 collective-permute-start.11
  41.6 7.4 %symmetric_kernel.1.refs_12_ = f32[96,96,128]{2,1,0:T(8,128)} custom-call(s32[1]{0:T(128)} %bitcast.place_ref, bf16[24,9216]{1,0:T(8,128)(2,1)} %copy-done.7, bf16[24,9216]{1,0:T(8,128)(2,1)} %collective-permute-done.6.refs_1_, bf16[24,9216]{1,0:T(8,128)(2,1)} %collective-permute-done.2.refs_2_, bf16[24,9216]{1,0:T(8,128)(2,1)} %collective-permute-done.7.refs_3_, ...), custom_call_target="tpu_custom_call" | custom-call | flops 99999997952 | bytes 1000 | tf_op jit(solution)/shard_map/symmetric_kernel/pallas_call | solution.py:146
  48.9 7.5 %collective-permute-done.4.refs_6_ = bf16[2,24,9216]{2,1,0:T(8,128)(2,1)} collective-permute-done((bf16[2,24,9216]{2,1,0:T(8,128)(2,1)S(1)}, bf16[2,24,9216]{2,1,0:T(8,128)(2,1)}, u32[]{:S(2)}, u32[]{:S(2)}) %collective-permute-start.4) | collective-permute-done | bytes 884768 | tf_op jit(solution)/shard_map/ppermute | solution.py:440
  56.5 4.5 %collective-permute-done.5.refs_10_ = bf16[2,24,9216]{2,1,0:T(8,128)(2,1)} collective-permute-done((bf16[2,24,9216]{2,1,0:T(8,128)(2,1)}, bf16[2,24,9216]{2,1,0:T(8,128)(2,1)}, u32[]{:S(2)}, u32[]{:S(2)}) %collective-permute-start.5) | collective-permute-done | bytes 884768 | tf_op jit(solution)/shard_map/ppermute | solution.py:437
  61.0 0.5 collective-permute-start.12
  61.5 1.0 slice.28
  62.5 0.6 collective-permute-start.17
  63.1 0.6 collective-permute-done.9.refs_7_
  63.7 1.3 collective-permute-done.12.refs_11_
  65.0 13.0 %pair_potentials.4 = (f32[24,9216]{1,0:T(8,128)}, bf16[24,9216]{1,0:T(8,128)(2,1)}, f32[24,9216]{1,0:T(8,128)}, f32[24,9216]{1,0:T(8,128)}, f32[24,9216]{1,0:T(8,128)}, /*index=5*/f32[24,9216]{1,0:T(8,128)}) custom-call(s32[1]{0:T(128)} %bitcast.place_ref, bf16[4,24,9216]{2,1,0:T(8,128)(2,1)} %refs_4_.3, ...), custom_call_target="tpu_custom_call" | custom-call | flops 99999997952 | bytes 1000 | tf_op jit(solution)/shard_map/pair_potentials/pallas_call | solution.py:380
  78.0 1.9 %broadcast_multiply_fusion = bf16[1,24,9216]{2,1,0:T(8,128)(2,1)} fusion(bf16[1,24,9216]{2,1,0:T(8,128)(2,1)} %collective-permute-done.10.refs_8_, bf16[]{:T(256)} %constant.51.clone.1), kind=kLoop, calls=%fused_computation.23 | loop fusion | flops 221184 | bytes 884738 | tf_op jit(solution)/shard_map/mul | solution.py:524
  79.9 1.2 collective-permute-start.14
  81.1 0.5 collective-permute-start.19
  81.6 13.7 %pair_potentials.5 = (f32[24,9216]{1,0:T(8,128)}, bf16[24,9216]{1,0:T(8,128)(2,1)}, f32[24,9216]{1,0:T(8,128)}, f32[24,9216]{1,0:T(8,128)}, f32[24,9216]{1,0:T(8,128)}, /*index=5*/f32[24,9216]{1,0:T(8,128)}) custom-call(s32[1]{0:T(128)} %bitcast.place_ref, bf16[4,24,9216]{2,1,0:T(8,128)(2,1)} %refs_4_.3, ...), custom_call_target="tpu_custom_call" | custom-call | flops 99999997952 | bytes 1000 | tf_op jit(solution)/shard_map/pair_potentials/pallas_call | solution.py:380
  95.3 0.6 collective-permute-start.16
  95.8 0.1 add_convert_fusion.2
  95.9 3.4 %collective-permute-start.21 = (bf16[24,9216]{1,0:T(8,128)(2,1)S(1)}, bf16[24,9216]{1,0:T(8,128)(2,1)}, u32[]{:S(2)}, u32[]{:S(2)}) collective-permute-start(bf16[24,9216]{1,0:T(8,128)(2,1)S(1)} %add_convert_fusion.2), channel_id=1, source_target_pairs={{0,28},{4,0},{8,4},{12,8},{16,12},{20,16},{24,20},{28,24},{1,29},{... | collective-permute-start | bytes 1327112 | tf_op jit(solution)/shard_map/ppermute | solution.py:437
  99.3 13.6 %pair_potentials.6 = (f32[24,9216]{1,0:T(8,128)}, bf16[24,9216]{1,0:T(8,128)(2,1)}, f32[24,9216]{1,0:T(8,128)}, f32[24,9216]{1,0:T(8,128)}, f32[24,9216]{1,0:T(8,128)}, /*index=5*/f32[24,9216]{1,0:T(8,128)}) custom-call(s32[1]{0:T(128)} %bitcast.place_ref, bf16[4,24,9216]{2,1,0:T(8,128)(2,1)} %refs_4_.3, ...), custom_call_target="tpu_custom_call" | custom-call | flops 99999997952 | bytes 1000 | tf_op jit(solution)/shard_map/pair_potentials/pallas_call | solution.py:380
  113.0 0.1 collective-permute-start.20
  113.1 0.5 collective-permute-start.15
  113.6 1.1 add_convert_fusion.3
  114.6 0.1 collective-permute-start.23
  114.7 0.3 collective-permute-done.20
  115.0 1.2 add_convert_fusion.1
  116.3 1.3 collective-permute-start.24
  117.6 13.6 %pair_potentials.7 = (f32[24,9216]{1,0:T(8,128)}, bf16[24,9216]{1,0:T(8,128)(2,1)}, f32[24,9216]{1,0:T(8,128)}, f32[24,9216]{1,0:T(8,128)}, f32[24,9216]{1,0:T(8,128)}, /*index=5*/f32[24,9216]{1,0:T(8,128)}) custom-call(s32[1]{0:T(128)} %bitcast.place_ref, bf16[4,24,9216]{2,1,0:T(8,128)(2,1)} %refs_4_.3, ...), custom_call_target="tpu_custom_call" | custom-call | flops 99999997952 | bytes 1000 | tf_op jit(solution)/shard_map/pair_potentials/pallas_call | solution.py:380
  131.3 0.1 collective-permute-start.25
  131.4 1.7 %convert_bitcast_fusion = (bf16[1,24,9216]{2,1,0:T(8,128)(2,1)S(1)}, bf16[1,24,9216]{2,1,0:T(8,128)(2,1)S(1)}) fusion(f32[24,9216]{1,0:T(8,128)} %get-tuple-element.91, f32[24,9216]{1,0:T(8,128)} %get-tuple-element.90), kind=kLoop, calls=%fused_computation.21 | loop fusion | flops 442368 | bytes 2654208 | tf_op jit(solution)/shard_map/stack | solution.py:534
  133.0 0.1 pad_maximum_fusion.1
  133.1 0.4 collective-permute-start.22
  133.5 0.1 add_convert_fusion
  133.6 0.4 collective-permute-start.26
  134.0 2.4 %collective-permute-done.24 = bf16[24,9216]{1,0:T(8,128)(2,1)} collective-permute-done((bf16[24,9216]{1,0:T(8,128)(2,1)S(1)}, bf16[24,9216]{1,0:T(8,128)(2,1)}, u32[]{:S(2)}, u32[]{:S(2)}) %collective-permute-start.24) | collective-permute-done | bytes 442400 | tf_op jit(solution)/shard_map/ppermute | solution.py:437
  136.5 1.6 %fusion.1 = (f32[1,24,9216]{2,1,0:T(8,128)S(1)}, f32[1,24,9216]{2,1,0:T(8,128)S(1)}, f32[1,24,9216]{2,1,0:T(8,128)S(1)}, f32[1,24,9216]{2,1,0:T(8,128)S(1)}) fusion(f32[24,9216]{1,0:T(8,128)S(1)} %copy-done.5, bf16[24,9216]{1,0:T(8,128)(2,1)} %collective-permute-done.21, pred[]{:T(512)S(6)} %eq.14, bf16[2,24,9216]{2,1,0:T(8,128)(2,1)S(1)} %collective-permute-done.22, ...), kind=kLoop, calls=%fused_computation.6 | loop fusion | flops 2654208 | bytes 7520258 | tf_op jit(solution)/shard_map/stack | solution.py:546
  138.1 2.0 %pad_maximum_fusion = f32[4,24,9216]{2,1,0:T(8,128)} fusion(f32[1,24,9216]{2,1,0:T(8,128)S(1)} %get-tuple-element.101, f32[1,24,9216]{2,1,0:T(8,128)S(1)} %get-tuple-element.102, f32[1,24,9216]{2,1,0:T(8,128)S(1)} %get-tuple-element.98, f32[1,24,9216]{2,1,0:T(8,128)S(1)} %get-tuple-element.97), kind=kLoop, calls=%fused_computation | loop fusion | flops 2654208 | bytes 7077888 | tf_op jit(solution)/shard_map/stack | solution.py:546
  140.1 5.8 %collective-permute-done.26 = bf16[24,9216]{1,0:T(8,128)(2,1)S(1)} collective-permute-done((bf16[24,9216]{1,0:T(8,128)(2,1)S(1)}, bf16[24,9216]{1,0:T(8,128)(2,1)S(1)}, u32[]{:S(2)}, u32[]{:S(2)}) %collective-permute-start.26) | collective-permute-done | bytes 442400 | tf_op jit(solution)/shard_map/ppermute | solution.py:437
  145.9 2.2 %fusion.7 = f32[4,24,9216]{2,1,0:T(8,128)} fusion(f32[4,24,9216]{2,1,0:T(8,128)} %pad_maximum_fusion, bf16[24,9216]{1,0:T(8,128)(2,1)S(1)} %collective-permute-done.26), kind=kLoop, calls=%fused_computation.13 | loop fusion | flops 442368 | bytes 2211840 | tf_op jit(solution)/shard_map/dynamic_update_slice | solution.py:549
  (43 shorter events, 0.2 us)
Async XLA Ops:
  0.0 10.1 %copy-start = (bf16[4,24,9216]{2,1,0:T(8,128)(2,1)S(1)}, bf16[4,24,9216]{2,1,0:T(8,128)(2,1)}, u32[]{:S(2)}) copy-start(bf16[4,24,9216]{2,1,0:T(8,128)(2,1)} %refs_4_.3) | copy-start | bytes 5308420
  0.0 8.5 %copy-start.4 = (f32[24,9216]{1,0:T(8,128)S(1)}, f32[24,9216]{1,0:T(8,128)}, u32[]{:S(2)}) copy-start(f32[24,9216]{1,0:T(8,128)} %param.17) | copy-start | bytes 2654212
  0.0 4.4 %collective-permute-start.1 = (bf16[4,24,9216]{2,1,0:T(8,128)(2,1)}, bf16[4,24,9216]{2,1,0:T(8,128)(2,1)}, u32[]{:S(2)}, u32[]{:S(2)}) collective-permute-start(bf16[4,24,9216]{2,1,0:T(8,128)(2,1)} %refs_4_.3), channel_id=1, source_target_pairs={{1,0},{0,1},{3,2},{2,3},{5,4},{4,5},{7,6},{6,7},{9,8},{8,9},{11,10... | collective-permute-start | bytes 5308424 | tf_op jit(solution)/shard_map/ppermute | solution.py:443
  1.7 32.5 %collective-permute-start = (bf16[2,24,9216]{2,1,0:T(8,128)(2,1)S(1)}, bf16[2,24,9216]{2,1,0:T(8,128)(2,1)}, u32[]{:S(2)}, u32[]{:S(2)}) collective-permute-start(bf16[2,24,9216]{2,1,0:T(8,128)(2,1)S(1)} %slice.24), channel_id=1, source_target_pairs={{2,0},{3,1},{0,2},{1,3},{6,4},{7,5},{4,6},{5,7},{10,8},{11,9},{8,1... | collective-permute-start | bytes 2654216 | tf_op jit(solution)/shard_map/ppermute | solution.py:440
  5.8 35.2 %collective-permute-start.8 = (bf16[3,24,9216]{2,1,0:T(8,128)(2,1)S(1)}, bf16[3,24,9216]{2,1,0:T(8,128)(2,1)}, u32[]{:S(2)}, u32[]{:S(2)}) collective-permute-start(bf16[3,24,9216]{2,1,0:T(8,128)(2,1)S(1)} %slice.27), channel_id=1, source_target_pairs={{0,4},{4,8},{8,12},{12,16},{16,20},{20,24},{24,28},{28,0},{1,5},{5... | collective-permute-start | bytes 3981320 | tf_op jit(solution)/shard_map/ppermute | solution.py:437
  8.5 33.0 %copy-start.7 = (bf16[24,9216]{1,0:T(8,128)(2,1)}, bf16[24,9216]{1,0:T(8,128)(2,1)S(1)}, u32[]{:S(2)}) copy-start(bf16[24,9216]{1,0:T(8,128)(2,1)S(1)} %convert_element_type.55.refs_0_) | copy-start | bytes 1327108
  8.5 25.6 %collective-permute-start.2 = (bf16[24,9216]{1,0:T(8,128)(2,1)S(1)}, bf16[24,9216]{1,0:T(8,128)(2,1)}, u32[]{:S(2)}, u32[]{:S(2)}) collective-permute-start(bf16[24,9216]{1,0:T(8,128)(2,1)S(1)} %convert_element_type.55.refs_0_), channel_id=1, source_target_pairs={{2,0},{3,1},{0,2},{1,3},{6,4},{7,5},{4,6},{5,7},{10,8},{11,9},{8,1... | collective-permute-start | bytes 1327112 | tf_op jit(solution)/shard_map/ppermute | solution.py:440
  10.1 31.0 %collective-permute-start.6 = (bf16[24,9216]{1,0:T(8,128)(2,1)S(1)}, bf16[24,9216]{1,0:T(8,128)(2,1)}, u32[]{:S(2)}, u32[]{:S(2)}) collective-permute-start(bf16[24,9216]{1,0:T(8,128)(2,1)S(1)} %convert_element_type.55.refs_0_), channel_id=1, source_target_pairs={{1,0},{0,1},{3,2},{2,3},{5,4},{4,5},{7,6},{6,7},{9,8},{8,9},{11,10... | collective-permute-start | bytes 1327112 | tf_op jit(solution)/shard_map/ppermute | solution.py:443
  34.2 7.3 %collective-permute-start.7 = (bf16[24,9216]{1,0:T(8,128)(2,1)}, bf16[24,9216]{1,0:T(8,128)(2,1)}, u32[]{:S(2)}, u32[]{:S(2)}) collective-permute-start(bf16[24,9216]{1,0:T(8,128)(2,1)} %collective-permute-done.2.refs_2_), channel_id=1, source_target_pairs={{1,0},{0,1},{3,2},{2,3},{5,4},{4,5},{7,6},{6,7},{9,8},{8,9},{11,10... | collective-permute-start | bytes 1327112 | tf_op jit(solution)/shard_map/ppermute | solution.py:443
  34.3 22.2 %collective-permute-start.4 = (bf16[2,24,9216]{2,1,0:T(8,128)(2,1)S(1)}, bf16[2,24,9216]{2,1,0:T(8,128)(2,1)}, u32[]{:S(2)}, u32[]{:S(2)}) collective-permute-start(bf16[2,24,9216]{2,1,0:T(8,128)(2,1)S(1)} %slice.26), channel_id=1, source_target_pairs={{2,0},{3,1},{0,2},{1,3},{6,4},{7,5},{4,6},{5,7},{10,8},{11,9},{8,1... | collective-permute-start | bytes 2654216 | tf_op jit(solution)/shard_map/ppermute | solution.py:440
  36.1 24.8 %collective-permute-start.5 = (bf16[2,24,9216]{2,1,0:T(8,128)(2,1)}, bf16[2,24,9216]{2,1,0:T(8,128)(2,1)}, u32[]{:S(2)}, u32[]{:S(2)}) collective-permute-start(bf16[2,24,9216]{2,1,0:T(8,128)(2,1)} %collective-permute-done.refs_2_), channel_id=1, source_target_pairs={{0,4},{4,8},{8,12},{12,16},{16,20},{20,24},{24,28},{28,0},{1,5},{5... | collective-permute-start | bytes 2654216 | tf_op jit(solution)/shard_map/ppermute | solution.py:437
  41.0 22.1 %collective-permute-start.3 = (bf16[2,24,9216]{2,1,0:T(8,128)(2,1)}, bf16[2,24,9216]{2,1,0:T(8,128)(2,1)}, u32[]{:S(2)}, u32[]{:S(2)}) collective-permute-start(bf16[2,24,9216]{2,1,0:T(8,128)(2,1)} %collective-permute-done.refs_2_), channel_id=1, source_target_pairs={{1,0},{0,1},{3,2},{2,3},{5,4},{4,5},{7,6},{6,7},{9,8},{8,9},{11,10... | collective-permute-start | bytes 2654216 | tf_op jit(solution)/shard_map/ppermute | solution.py:443
  41.0 23.9 %collective-permute-start.11 = (bf16[3,24,9216]{2,1,0:T(8,128)(2,1)}, bf16[3,24,9216]{2,1,0:T(8,128)(2,1)}, u32[]{:S(2)}, u32[]{:S(2)}) collective-permute-start(bf16[3,24,9216]{2,1,0:T(8,128)(2,1)} %collective-permute-done.8.refs_8_), channel_id=1, source_target_pairs={{1,0},{0,1},{3,2},{2,3},{5,4},{4,5},{7,6},{6,7},{9,8},{8,9},{11,10... | collective-permute-start | bytes 3981320 | tf_op jit(solution)/shard_map/ppermute | solution.py:443
  61.0 2.8 %collective-permute-start.9 = (bf16[2,24,9216]{2,1,0:T(8,128)(2,1)}, bf16[2,24,9216]{2,1,0:T(8,128)(2,1)}, u32[]{:S(2)}, u32[]{:S(2)}) collective-permute-start(bf16[2,24,9216]{2,1,0:T(8,128)(2,1)} %collective-permute-done.4.refs_6_), channel_id=1, source_target_pairs={{1,0},{0,1},{3,2},{2,3},{5,4},{4,5},{7,6},{6,7},{9,8},{8,9},{11,10... | collective-permute-start | bytes 2654216 | tf_op jit(solution)/shard_map/ppermute | solution.py:443
  61.0 4.0 %collective-permute-start.12 = (bf16[2,24,9216]{2,1,0:T(8,128)(2,1)}, bf16[2,24,9216]{2,1,0:T(8,128)(2,1)}, u32[]{:S(2)}, u32[]{:S(2)}) collective-permute-start(bf16[2,24,9216]{2,1,0:T(8,128)(2,1)} %collective-permute-done.5.refs_10_), channel_id=1, source_target_pairs={{1,0},{0,1},{3,2},{2,3},{5,4},{4,5},{7,6},{6,7},{9,8},{8,9},{11,10... | collective-permute-start | bytes 2654216 | tf_op jit(solution)/shard_map/ppermute | solution.py:443
  62.5 19.1 %collective-permute-start.17 = (bf16[1,24,9216]{2,1,0:T(8,128)(2,1)S(1)}, bf16[1,24,9216]{2,1,0:T(8,128)(2,1)}, u32[]{:S(2)}, u32[]{:S(2)}) collective-permute-start(bf16[1,24,9216]{2,1,0:T(8,128)(2,1)S(1)} %slice.28), channel_id=1, source_target_pairs={{2,0},{3,1},{0,2},{1,3},{6,4},{7,5},{4,6},{5,7},{10,8},{11,9},{8,1... | collective-permute-start | bytes 1327112 | tf_op jit(solution)/shard_map/ppermute | solution.py:440
  63.1 14.9 %collective-permute-start.10 = (bf16[1,24,9216]{2,1,0:T(8,128)(2,1)S(1)}, bf16[1,24,9216]{2,1,0:T(8,128)(2,1)}, u32[]{:S(2)}, u32[]{:S(2)}) collective-permute-start(bf16[1,24,9216]{2,1,0:T(8,128)(2,1)S(1)} %slice.25), channel_id=1, source_target_pairs={{0,4},{4,8},{8,12},{12,16},{16,20},{20,24},{24,28},{28,0},{1,5},{5... | collective-permute-start | bytes 1327112 | tf_op jit(solution)/shard_map/ppermute | solution.py:437
  79.9 33.2 %collective-permute-start.14 = (bf16[1,24,9216]{2,1,0:T(8,128)(2,1)}, bf16[1,24,9216]{2,1,0:T(8,128)(2,1)}, u32[]{:S(2)}, u32[]{:S(2)}) collective-permute-start(bf16[1,24,9216]{2,1,0:T(8,128)(2,1)} %broadcast_multiply_fusion), channel_id=1, source_target_pairs={{2,0},{3,1},{0,2},{1,3},{6,4},{7,5},{4,6},{5,7},{10,8},{11,9},{8,1... | collective-permute-start | bytes 1327112 | tf_op jit(solution)/shard_map/ppermute | solution.py:440
  81.1 36.5 %collective-permute-start.13 = (bf16[1,24,9216]{2,1,0:T(8,128)(2,1)}, bf16[1,24,9216]{2,1,0:T(8,128)(2,1)}, u32[]{:S(2)}, u32[]{:S(2)}) collective-permute-start(bf16[1,24,9216]{2,1,0:T(8,128)(2,1)} %collective-permute-done.10.refs_8_), channel_id=1, source_target_pairs={{1,0},{0,1},{3,2},{2,3},{5,4},{4,5},{7,6},{6,7},{9,8},{8,9},{11,10... | collective-permute-start | bytes 1327112 | tf_op jit(solution)/shard_map/ppermute | solution.py:443
  81.1 14.7 %collective-permute-start.19 = (bf16[24,9216]{1,0:T(8,128)(2,1)}, bf16[24,9216]{1,0:T(8,128)(2,1)S(1)}, u32[]{:S(2)}, u32[]{:S(2)}) collective-permute-start(bf16[24,9216]{1,0:T(8,128)(2,1)} %get-tuple-element.77), channel_id=1, source_target_pairs={{1,0},{0,1},{3,2},{2,3},{5,4},{4,5},{7,6},{6,7},{9,8},{8,9},{11,10... | collective-permute-start | bytes 1327112 | tf_op jit(solution)/shard_map/ppermute | solution.py:443
  81.6 17.7 %collective-permute-start.18 = (bf16[1,24,9216]{2,1,0:T(8,128)(2,1)}, bf16[1,24,9216]{2,1,0:T(8,128)(2,1)}, u32[]{:S(2)}, u32[]{:S(2)}) collective-permute-start(bf16[1,24,9216]{2,1,0:T(8,128)(2,1)} %collective-permute-done.17.refs_10_), channel_id=1, source_target_pairs={{1,0},{0,1},{3,2},{2,3},{5,4},{4,5},{7,6},{6,7},{9,8},{8,9},{11,10... | collective-permute-start | bytes 1327112 | tf_op jit(solution)/shard_map/ppermute | solution.py:443
  81.6 14.2 %copy-start.2 = (f32[24,9216]{1,0:T(8,128)S(1)}, f32[24,9216]{1,0:T(8,128)}, u32[]{:S(2)}) copy-start(f32[24,9216]{1,0:T(8,128)} %get-tuple-element.66) | copy-start | bytes 2654212
  95.3 18.3 %collective-permute-start.16 = (bf16[24,9216]{1,0:T(8,128)(2,1)}, bf16[24,9216]{1,0:T(8,128)(2,1)}, u32[]{:S(2)}, u32[]{:S(2)}) collective-permute-start(bf16[24,9216]{1,0:T(8,128)(2,1)} %get-tuple-element.75), channel_id=1, source_target_pairs={{1,0},{0,1},{3,2},{2,3},{5,4},{4,5},{7,6},{6,7},{9,8},{8,9},{11,10... | collective-permute-start | bytes 1327112 | tf_op jit(solution)/shard_map/ppermute | solution.py:443
  95.9 21.7 %collective-permute-start.21 = (bf16[24,9216]{1,0:T(8,128)(2,1)S(1)}, bf16[24,9216]{1,0:T(8,128)(2,1)}, u32[]{:S(2)}, u32[]{:S(2)}) collective-permute-start(bf16[24,9216]{1,0:T(8,128)(2,1)S(1)} %add_convert_fusion.2), channel_id=1, source_target_pairs={{0,28},{4,0},{8,4},{12,8},{16,12},{20,16},{24,20},{28,24},{1,29},{... | collective-permute-start | bytes 1327112 | tf_op jit(solution)/shard_map/ppermute | solution.py:437
  99.3 14.2 %copy-start.1 = (f32[24,9216]{1,0:T(8,128)S(1)}, f32[24,9216]{1,0:T(8,128)}, u32[]{:S(2)}) copy-start(f32[24,9216]{1,0:T(8,128)} %get-tuple-element.73) | copy-start | bytes 2654212
  113.0 2.1 %collective-permute-start.20 = (bf16[24,9216]{1,0:T(8,128)(2,1)}, bf16[24,9216]{1,0:T(8,128)(2,1)S(1)}, u32[]{:S(2)}, u32[]{:S(2)}) collective-permute-start(bf16[24,9216]{1,0:T(8,128)(2,1)} %get-tuple-element.84), channel_id=1, source_target_pairs={{1,0},{0,1},{3,2},{2,3},{5,4},{4,5},{7,6},{6,7},{9,8},{8,9},{11,10... | collective-permute-start | bytes 1327112 | tf_op jit(solution)/shard_map/ppermute | solution.py:443
  113.1 4.6 %collective-permute-start.15 = (bf16[1,24,9216]{2,1,0:T(8,128)(2,1)}, bf16[1,24,9216]{2,1,0:T(8,128)(2,1)}, u32[]{:S(2)}, u32[]{:S(2)}) collective-permute-start(bf16[1,24,9216]{2,1,0:T(8,128)(2,1)} %collective-permute-done.14.refs_10_), channel_id=1, source_target_pairs={{1,0},{0,1},{3,2},{2,3},{5,4},{4,5},{7,6},{6,7},{9,8},{8,9},{11,10... | collective-permute-start | bytes 1327112 | tf_op jit(solution)/shard_map/ppermute | solution.py:443
  114.6 16.6 %collective-permute-start.23 = (bf16[24,9216]{1,0:T(8,128)(2,1)S(1)}, bf16[24,9216]{1,0:T(8,128)(2,1)S(1)}, u32[]{:S(2)}, u32[]{:S(2)}) collective-permute-start(bf16[24,9216]{1,0:T(8,128)(2,1)S(1)} %add_convert_fusion.3), channel_id=1, source_target_pairs={{0,28},{4,0},{8,4},{12,8},{16,12},{20,16},{24,20},{28,24},{1,29},{... | collective-permute-start | bytes 1327112 | tf_op jit(solution)/shard_map/ppermute | solution.py:437
  116.3 20.2 %collective-permute-start.24 = (bf16[24,9216]{1,0:T(8,128)(2,1)S(1)}, bf16[24,9216]{1,0:T(8,128)(2,1)}, u32[]{:S(2)}, u32[]{:S(2)}) collective-permute-start(bf16[24,9216]{1,0:T(8,128)(2,1)S(1)} %add_convert_fusion.1), channel_id=1, source_target_pairs={{0,28},{4,0},{8,4},{12,8},{16,12},{20,16},{24,20},{28,24},{1,29},{... | collective-permute-start | bytes 1327112 | tf_op jit(solution)/shard_map/ppermute | solution.py:437
  131.2 2.3 %copy-start.3 = (f32[24,9216]{1,0:T(8,128)S(1)}, f32[24,9216]{1,0:T(8,128)}, u32[]{:S(2)}) copy-start(f32[24,9216]{1,0:T(8,128)} %get-tuple-element.94) | copy-start | bytes 2654212
  131.2 5.2 %copy-start.5 = (f32[24,9216]{1,0:T(8,128)S(1)}, f32[24,9216]{1,0:T(8,128)}, u32[]{:S(2)}) copy-start(f32[24,9216]{1,0:T(8,128)} %get-tuple-element.92) | copy-start | bytes 2654212
  131.3 5.2 %copy-start.6 = (f32[24,9216]{1,0:T(8,128)S(1)}, f32[24,9216]{1,0:T(8,128)}, u32[]{:S(2)}) copy-start(f32[24,9216]{1,0:T(8,128)} %get-tuple-element.93) | copy-start | bytes 2654212
  131.3 2.3 %collective-permute-start.25 = (bf16[24,9216]{1,0:T(8,128)(2,1)}, bf16[24,9216]{1,0:T(8,128)(2,1)S(1)}, u32[]{:S(2)}, u32[]{:S(2)}) collective-permute-start(bf16[24,9216]{1,0:T(8,128)(2,1)} %get-tuple-element.96), channel_id=1, source_target_pairs={{1,0},{0,1},{3,2},{2,3},{5,4},{4,5},{7,6},{6,7},{9,8},{8,9},{11,10... | collective-permute-start | bytes 1327112 | tf_op jit(solution)/shard_map/ppermute | solution.py:443
  133.1 3.3 %collective-permute-start.22 = (bf16[2,24,9216]{2,1,0:T(8,128)(2,1)S(1)}, bf16[2,24,9216]{2,1,0:T(8,128)(2,1)S(1)}, u32[]{:S(2)}, u32[]{:S(2)}) collective-permute-start(bf16[2,24,9216]{2,1,0:T(8,128)(2,1)S(1)} %pad_maximum_fusion.1), channel_id=1, source_target_pairs={{1,0},{0,1},{3,2},{2,3},{5,4},{4,5},{7,6},{6,7},{9,8},{8,9},{11,10... | collective-permute-start | bytes 2654216 | tf_op jit(solution)/shard_map/ppermute | solution.py:443
  133.6 12.3 %collective-permute-start.26 = (bf16[24,9216]{1,0:T(8,128)(2,1)S(1)}, bf16[24,9216]{1,0:T(8,128)(2,1)S(1)}, u32[]{:S(2)}, u32[]{:S(2)}) collective-permute-start(bf16[24,9216]{1,0:T(8,128)(2,1)S(1)} %add_convert_fusion), channel_id=1, source_target_pairs={{0,28},{4,0},{8,4},{12,8},{16,12},{20,16},{24,20},{28,24},{1,29},{... | collective-permute-start | bytes 1327112 | tf_op jit(solution)/shard_map/ppermute | solution.py:437

commit v5 on v4

--- a/solution.py
+++ b/solution.py
@@ -396,8 +396,8 @@
             pltpu.VMEM((b_count, rows, width), F32),
             pltpu.VMEM((b_count, near - 1, rows, width), BF),
             pltpu.VMEM((a_count, near, rows, width), F32),
-            pltpu.VMEM((2 * count * (count + PITCH), LANES), F32),
-            pltpu.VMEM((2 * count * (count + PITCH), LANES), F32),
+            pltpu.VMEM(((2 * count + 1) * (count + PITCH), LANES), F32),
+            pltpu.VMEM(((2 * count + 1) * (count + PITCH), LANES), F32),
             pltpu.SemaphoreType.DMA((CHUNKS, pieces)),
             pltpu.SemaphoreType.DMA((5,)),
             pltpu.SemaphoreType.DMA((a_count * near,)),

time: 148 us -> 149 us (level)
  no operation moved by 1% of the time
where the time goes in v5:
time: 149 us; the launch traced here: 148 us
  Pallas kernels  61.4 us (41%)
  waiting for transfers between devices  49.8 us (33%)
  starting transfers between devices  21 us (14%)
  other arithmetic  12 us (8%)
  local copies, waits for them, and re-layouts  3.8 us (3%)
    pallas_call x4, Pallas kernels, unit(): pl.pallas_call(functools.partial(unit_body, count, n, near, a_count, b_co...  54.1 us
    ppermute x5, waiting for transfers between devices, to_a(): lax.ppermute(x, 'grid', [((i // gb + s) % ga * gb + i % gb, i) for i in r...  31.6 us
    ppermute x7, waiting for transfers between devices, hop(): lax.ppermute(x, 'band', [(i, (i + distance) % blocks) for i in range(bloc...  16.1 us
    ppermute x7, starting transfers between devices, hop(): lax.ppermute(x, 'band', [(i, (i + distance) % blocks) for i in range(bloc...  9.48 us
    ppermute x5, starting transfers between devices, to_a(): lax.ppermute(x, 'grid', [((i // gb + s) % ga * gb + i % gb, i) for i in r...  7.88 us
    pallas_call x1, Pallas kernels, whole_kernel(): pl.pallas_call(functools.partial(kernel_body, count, len(pieces)), out_sh...  7.38 us
    another operation x2, other arithmetic, local(): jnp.stack([v + returned[j].astype(F32) if j < early else v for j, v in en...  3.66 us
    ppermute x15, starting transfers between devices, to_b(): lax.ppermute(x, 'grid', [(i // gb * gb + (i % gb + t) % gb, i) for i in r...  3.66 us
  transfers between devices with their start and end apart: 27, of which 9 were waited for; matrix products, arithmetic and copies ran while one was open for 9% of the time, Pallas kernels for 41%

profile of v5, /device:TPU:0, one launch (start us, length us, event | category | flops | bytes accessed | tf_op | source)
XLA Modules:
  0.0 148.3 jit_solution(16027735156104327736)
XLA Ops:
  0.0 0.5 collective-permute-start.1
  0.5 1.2 slice.24
  1.7 2.7 %collective-permute-start = (bf16[2,24,9216]{2,1,0:T(8,128)(2,1)S(1)}, bf16[2,24,9216]{2,1,0:T(8,128)(2,1)}, u32[]{:S(2)}, u32[]{:S(2)}) collective-permute-start(bf16[2,24,9216]{2,1,0:T(8,128)(2,1)S(1)} %slice.24), channel_id=1, source_target_pairs={{2,0},{3,1},{0,2},{1,3},{6,4},{7,5},{4,6},{5,7},{10,8},{11,9},{8,1... | collective-permute-start | bytes 2654216 | tf_op jit(solution)/shard_map/ppermute | solution.py:440
  4.4 1.4 slice.27
  5.8 2.6 %collective-permute-start.8 = (bf16[3,24,9216]{2,1,0:T(8,128)(2,1)S(1)}, bf16[3,24,9216]{2,1,0:T(8,128)(2,1)}, u32[]{:S(2)}, u32[]{:S(2)}) collective-permute-start(bf16[3,24,9216]{2,1,0:T(8,128)(2,1)S(1)} %slice.27), channel_id=1, source_target_pairs={{0,4},{4,8},{8,12},{12,16},{16,20},{20,24},{24,28},{28,0},{1,5},{5... | collective-permute-start | bytes 3981320 | tf_op jit(solution)/shard_map/ppermute | solution.py:437
  8.5 1.6 %collective-permute-start.2 = (bf16[24,9216]{1,0:T(8,128)(2,1)S(1)}, bf16[24,9216]{1,0:T(8,128)(2,1)}, u32[]{:S(2)}, u32[]{:S(2)}) collective-permute-start(bf16[24,9216]{1,0:T(8,128)(2,1)S(1)} %convert_element_type.55.refs_0_), channel_id=1, source_target_pairs={{2,0},{3,1},{0,2},{1,3},{6,4},{7,5},{4,6},{5,7},{10,8},{11,9},{8,1... | collective-permute-start | bytes 1327112 | tf_op jit(solution)/shard_map/ppermute | solution.py:440
  10.1 24.0 %collective-permute-done.2.refs_2_ = bf16[24,9216]{1,0:T(8,128)(2,1)} collective-permute-done((bf16[24,9216]{1,0:T(8,128)(2,1)S(1)}, bf16[24,9216]{1,0:T(8,128)(2,1)}, u32[]{:S(2)}, u32[]{:S(2)}) %collective-permute-start.2) | collective-permute-done | bytes 442400 | tf_op jit(solution)/shard_map/ppermute | solution.py:440
  34.2 0.1 collective-permute-start.7
  34.3 1.8 %collective-permute-start.4 = (bf16[2,24,9216]{2,1,0:T(8,128)(2,1)S(1)}, bf16[2,24,9216]{2,1,0:T(8,128)(2,1)}, u32[]{:S(2)}, u32[]{:S(2)}) collective-permute-start(bf16[2,24,9216]{2,1,0:T(8,128)(2,1)S(1)} %slice.26), channel_id=1, source_target_pairs={{2,0},{3,1},{0,2},{1,3},{6,4},{7,5},{4,6},{5,7},{10,8},{11,9},{8,1... | collective-permute-start | bytes 2654216 | tf_op jit(solution)/shard_map/ppermute | solution.py:440
  36.1 1.5 %collective-permute-start.5 = (bf16[2,24,9216]{2,1,0:T(8,128)(2,1)}, bf16[2,24,9216]{2,1,0:T(8,128)(2,1)}, u32[]{:S(2)}, u32[]{:S(2)}) collective-permute-start(bf16[2,24,9216]{2,1,0:T(8,128)(2,1)} %collective-permute-done.refs_2_), channel_id=1, source_target_pairs={{0,4},{4,8},{8,12},{12,16},{16,20},{20,24},{24,28},{28,0},{1,5},{5... | collective-permute-start | bytes 2654216 | tf_op jit(solution)/shard_map/ppermute | solution.py:437
  37.6 3.4 %collective-permute-done.8.refs_8_ = bf16[3,24,9216]{2,1,0:T(8,128)(2,1)} collective-permute-done((bf16[3,24,9216]{2,1,0:T(8,128)(2,1)S(1)}, bf16[3,24,9216]{2,1,0:T(8,128)(2,1)}, u32[]{:S(2)}, u32[]{:S(2)}) %collective-permute-start.8) | collective-permute-done | bytes 1327136 | tf_op jit(solution)/shard_map/ppermute | solution.py:437
  41.0 0.5 collective-permute-start.11
  41.6 7.4 %symmetric_kernel.1.refs_12_ = f32[96,96,128]{2,1,0:T(8,128)} custom-call(s32[1]{0:T(128)} %bitcast.place_ref, bf16[24,9216]{1,0:T(8,128)(2,1)} %copy-done.7, bf16[24,9216]{1,0:T(8,128)(2,1)} %collective-permute-done.6.refs_1_, bf16[24,9216]{1,0:T(8,128)(2,1)} %collective-permute-done.2.refs_2_, bf16[24,9216]{1,0:T(8,128)(2,1)} %collective-permute-done.7.refs_3_, ...), custom_call_target="tpu_custom_call" | custom-call | flops 99999997952 | bytes 1000 | tf_op jit(solution)/shard_map/symmetric_kernel/pallas_call | solution.py:146
  48.9 7.5 %collective-permute-done.4.refs_6_ = bf16[2,24,9216]{2,1,0:T(8,128)(2,1)} collective-permute-done((bf16[2,24,9216]{2,1,0:T(8,128)(2,1)S(1)}, bf16[2,24,9216]{2,1,0:T(8,128)(2,1)}, u32[]{:S(2)}, u32[]{:S(2)}) %collective-permute-start.4) | collective-permute-done | bytes 884768 | tf_op jit(solution)/shard_map/ppermute | solution.py:440
  56.5 4.5 %collective-permute-done.5.refs_10_ = bf16[2,24,9216]{2,1,0:T(8,128)(2,1)} collective-permute-done((bf16[2,24,9216]{2,1,0:T(8,128)(2,1)}, bf16[2,24,9216]{2,1,0:T(8,128)(2,1)}, u32[]{:S(2)}, u32[]{:S(2)}) %collective-permute-start.5) | collective-permute-done | bytes 884768 | tf_op jit(solution)/shard_map/ppermute | solution.py:437
  61.0 0.5 collective-permute-start.12
  61.5 1.0 slice.28
  62.5 0.6 collective-permute-start.17
  63.1 0.6 collective-permute-done.9.refs_7_
  63.7 1.3 collective-permute-done.12.refs_11_
  65.0 13.0 %pair_potentials.4 = (f32[24,9216]{1,0:T(8,128)}, bf16[24,9216]{1,0:T(8,128)(2,1)}, f32[24,9216]{1,0:T(8,128)}, f32[24,9216]{1,0:T(8,128)}, f32[24,9216]{1,0:T(8,128)}, /*index=5*/f32[24,9216]{1,0:T(8,128)}) custom-call(s32[1]{0:T(128)} %bitcast.place_ref, bf16[4,24,9216]{2,1,0:T(8,128)(2,1)} %refs_4_.3, ...), custom_call_target="tpu_custom_call" | custom-call | flops 99999997952 | bytes 1000 | tf_op jit(solution)/shard_map/pair_potentials/pallas_call | solution.py:380
  78.0 1.9 %broadcast_multiply_fusion = bf16[1,24,9216]{2,1,0:T(8,128)(2,1)} fusion(bf16[1,24,9216]{2,1,0:T(8,128)(2,1)} %collective-permute-done.10.refs_8_, bf16[]{:T(256)} %constant.51.clone.1), kind=kLoop, calls=%fused_computation.23 | loop fusion | flops 221184 | bytes 884738 | tf_op jit(solution)/shard_map/mul | solution.py:524
  79.9 1.2 collective-permute-start.14
  81.1 0.5 collective-permute-start.19
  81.6 13.7 %pair_potentials.5 = (f32[24,9216]{1,0:T(8,128)}, bf16[24,9216]{1,0:T(8,128)(2,1)}, f32[24,9216]{1,0:T(8,128)}, f32[24,9216]{1,0:T(8,128)}, f32[24,9216]{1,0:T(8,128)}, /*index=5*/f32[24,9216]{1,0:T(8,128)}) custom-call(s32[1]{0:T(128)} %bitcast.place_ref, bf16[4,24,9216]{2,1,0:T(8,128)(2,1)} %refs_4_.3, ...), custom_call_target="tpu_custom_call" | custom-call | flops 99999997952 | bytes 1000 | tf_op jit(solution)/shard_map/pair_potentials/pallas_call | solution.py:380
  95.3 0.6 collective-permute-start.16
  95.9 0.1 add_convert_fusion.2
  95.9 3.5 %collective-permute-start.21 = (bf16[24,9216]{1,0:T(8,128)(2,1)S(1)}, bf16[24,9216]{1,0:T(8,128)(2,1)}, u32[]{:S(2)}, u32[]{:S(2)}) collective-permute-start(bf16[24,9216]{1,0:T(8,128)(2,1)S(1)} %add_convert_fusion.2), channel_id=1, source_target_pairs={{0,28},{4,0},{8,4},{12,8},{16,12},{20,16},{24,20},{28,24},{1,29},{... | collective-permute-start | bytes 1327112 | tf_op jit(solution)/shard_map/ppermute | solution.py:437
  99.4 13.7 %pair_potentials.6 = (f32[24,9216]{1,0:T(8,128)}, bf16[24,9216]{1,0:T(8,128)(2,1)}, f32[24,9216]{1,0:T(8,128)}, f32[24,9216]{1,0:T(8,128)}, f32[24,9216]{1,0:T(8,128)}, /*index=5*/f32[24,9216]{1,0:T(8,128)}) custom-call(s32[1]{0:T(128)} %bitcast.place_ref, bf16[4,24,9216]{2,1,0:T(8,128)(2,1)} %refs_4_.3, ...), custom_call_target="tpu_custom_call" | custom-call | flops 99999997952 | bytes 1000 | tf_op jit(solution)/shard_map/pair_potentials/pallas_call | solution.py:380
  113.1 0.1 collective-permute-start.20
  113.2 0.5 collective-permute-start.15
  113.7 1.1 add_convert_fusion.3
  114.8 0.1 collective-permute-start.23
  114.9 0.3 collective-permute-done.20
  115.2 1.2 add_convert_fusion.1
  116.4 1.3 collective-permute-start.24
  117.8 13.6 %pair_potentials.7 = (f32[24,9216]{1,0:T(8,128)}, bf16[24,9216]{1,0:T(8,128)(2,1)}, f32[24,9216]{1,0:T(8,128)}, f32[24,9216]{1,0:T(8,128)}, f32[24,9216]{1,0:T(8,128)}, /*index=5*/f32[24,9216]{1,0:T(8,128)}) custom-call(s32[1]{0:T(128)} %bitcast.place_ref, bf16[4,24,9216]{2,1,0:T(8,128)(2,1)} %refs_4_.3, ...), custom_call_target="tpu_custom_call" | custom-call | flops 99999997952 | bytes 1000 | tf_op jit(solution)/shard_map/pair_potentials/pallas_call | solution.py:380
  131.5 0.1 collective-permute-start.25
  131.5 1.7 %convert_bitcast_fusion = (bf16[1,24,9216]{2,1,0:T(8,128)(2,1)S(1)}, bf16[1,24,9216]{2,1,0:T(8,128)(2,1)S(1)}) fusion(f32[24,9216]{1,0:T(8,128)} %get-tuple-element.91, f32[24,9216]{1,0:T(8,128)} %get-tuple-element.90), kind=kLoop, calls=%fused_computation.21 | loop fusion | flops 442368 | bytes 2654208 | tf_op jit(solution)/shard_map/stack | solution.py:534
  133.2 0.1 pad_maximum_fusion.1
  133.3 0.4 collective-permute-start.22
  133.7 0.1 add_convert_fusion
  133.8 0.4 collective-permute-start.26
  134.2 2.4 %collective-permute-done.24 = bf16[24,9216]{1,0:T(8,128)(2,1)} collective-permute-done((bf16[24,9216]{1,0:T(8,128)(2,1)S(1)}, bf16[24,9216]{1,0:T(8,128)(2,1)}, u32[]{:S(2)}, u32[]{:S(2)}) %collective-permute-start.24) | collective-permute-done | bytes 442400 | tf_op jit(solution)/shard_map/ppermute | solution.py:437
  136.6 1.6 %fusion.1 = (f32[1,24,9216]{2,1,0:T(8,128)S(1)}, f32[1,24,9216]{2,1,0:T(8,128)S(1)}, f32[1,24,9216]{2,1,0:T(8,128)S(1)}, f32[1,24,9216]{2,1,0:T(8,128)S(1)}) fusion(f32[24,9216]{1,0:T(8,128)S(1)} %copy-done.5, bf16[24,9216]{1,0:T(8,128)(2,1)} %collective-permute-done.21, pred[]{:T(512)S(6)} %eq.14, bf16[2,24,9216]{2,1,0:T(8,128)(2,1)S(1)} %collective-permute-done.22, ...), kind=kLoop, calls=%fused_computation.6 | loop fusion | flops 2654208 | bytes 7520258 | tf_op jit(solution)/shard_map/stack | solution.py:546
  138.2 2.0 %pad_maximum_fusion = f32[4,24,9216]{2,1,0:T(8,128)} fusion(f32[1,24,9216]{2,1,0:T(8,128)S(1)} %get-tuple-element.101, f32[1,24,9216]{2,1,0:T(8,128)S(1)} %get-tuple-element.102, f32[1,24,9216]{2,1,0:T(8,128)S(1)} %get-tuple-element.98, f32[1,24,9216]{2,1,0:T(8,128)S(1)} %get-tuple-element.97), kind=kLoop, calls=%fused_computation | loop fusion | flops 2654208 | bytes 7077888 | tf_op jit(solution)/shard_map/stack | solution.py:546
  140.3 5.8 %collective-permute-done.26 = bf16[24,9216]{1,0:T(8,128)(2,1)S(1)} collective-permute-done((bf16[24,9216]{1,0:T(8,128)(2,1)S(1)}, bf16[24,9216]{1,0:T(8,128)(2,1)S(1)}, u32[]{:S(2)}, u32[]{:S(2)}) %collective-permute-start.26) | collective-permute-done | bytes 442400 | tf_op jit(solution)/shard_map/ppermute | solution.py:437
  146.1 2.2 %fusion.7 = f32[4,24,9216]{2,1,0:T(8,128)} fusion(f32[4,24,9216]{2,1,0:T(8,128)} %pad_maximum_fusion, bf16[24,9216]{1,0:T(8,128)(2,1)S(1)} %collective-permute-done.26), kind=kLoop, calls=%fused_computation.13 | loop fusion | flops 442368 | bytes 2211840 | tf_op jit(solution)/shard_map/dynamic_update_slice | solution.py:549
  (43 shorter events, 0.2 us)
Async XLA Ops:
  0.0 10.1 %copy-start = (bf16[4,24,9216]{2,1,0:T(8,128)(2,1)S(1)}, bf16[4,24,9216]{2,1,0:T(8,128)(2,1)}, u32[]{:S(2)}) copy-start(bf16[4,24,9216]{2,1,0:T(8,128)(2,1)} %refs_4_.3) | copy-start | bytes 5308420
  0.0 8.5 %copy-start.4 = (f32[24,9216]{1,0:T(8,128)S(1)}, f32[24,9216]{1,0:T(8,128)}, u32[]{:S(2)}) copy-start(f32[24,9216]{1,0:T(8,128)} %param.17) | copy-start | bytes 2654212
  0.0 4.4 %collective-permute-start.1 = (bf16[4,24,9216]{2,1,0:T(8,128)(2,1)}, bf16[4,24,9216]{2,1,0:T(8,128)(2,1)}, u32[]{:S(2)}, u32[]{:S(2)}) collective-permute-start(bf16[4,24,9216]{2,1,0:T(8,128)(2,1)} %refs_4_.3), channel_id=1, source_target_pairs={{1,0},{0,1},{3,2},{2,3},{5,4},{4,5},{7,6},{6,7},{9,8},{8,9},{11,10... | collective-permute-start | bytes 5308424 | tf_op jit(solution)/shard_map/ppermute | solution.py:443
  1.7 32.5 %collective-permute-start = (bf16[2,24,9216]{2,1,0:T(8,128)(2,1)S(1)}, bf16[2,24,9216]{2,1,0:T(8,128)(2,1)}, u32[]{:S(2)}, u32[]{:S(2)}) collective-permute-start(bf16[2,24,9216]{2,1,0:T(8,128)(2,1)S(1)} %slice.24), channel_id=1, source_target_pairs={{2,0},{3,1},{0,2},{1,3},{6,4},{7,5},{4,6},{5,7},{10,8},{11,9},{8,1... | collective-permute-start | bytes 2654216 | tf_op jit(solution)/shard_map/ppermute | solution.py:440
  5.8 35.2 %collective-permute-start.8 = (bf16[3,24,9216]{2,1,0:T(8,128)(2,1)S(1)}, bf16[3,24,9216]{2,1,0:T(8,128)(2,1)}, u32[]{:S(2)}, u32[]{:S(2)}) collective-permute-start(bf16[3,24,9216]{2,1,0:T(8,128)(2,1)S(1)} %slice.27), channel_id=1, source_target_pairs={{0,4},{4,8},{8,12},{12,16},{16,20},{20,24},{24,28},{28,0},{1,5},{5... | collective-permute-start | bytes 3981320 | tf_op jit(solution)/shard_map/ppermute | solution.py:437
  8.5 33.0 %copy-start.7 = (bf16[24,9216]{1,0:T(8,128)(2,1)}, bf16[24,9216]{1,0:T(8,128)(2,1)S(1)}, u32[]{:S(2)}) copy-start(bf16[24,9216]{1,0:T(8,128)(2,1)S(1)} %convert_element_type.55.refs_0_) | copy-start | bytes 1327108
  8.5 25.6 %collective-permute-start.2 = (bf16[24,9216]{1,0:T(8,128)(2,1)S(1)}, bf16[24,9216]{1,0:T(8,128)(2,1)}, u32[]{:S(2)}, u32[]{:S(2)}) collective-permute-start(bf16[24,9216]{1,0:T(8,128)(2,1)S(1)} %convert_element_type.55.refs_0_), channel_id=1, source_target_pairs={{2,0},{3,1},{0,2},{1,3},{6,4},{7,5},{4,6},{5,7},{10,8},{11,9},{8,1... | collective-permute-start | bytes 1327112 | tf_op jit(solution)/shard_map/ppermute | solution.py:440
  10.1 31.0 %collective-permute-start.6 = (bf16[24,9216]{1,0:T(8,128)(2,1)S(1)}, bf16[24,9216]{1,0:T(8,128)(2,1)}, u32[]{:S(2)}, u32[]{:S(2)}) collective-permute-start(bf16[24,9216]{1,0:T(8,128)(2,1)S(1)} %convert_element_type.55.refs_0_), channel_id=1, source_target_pairs={{1,0},{0,1},{3,2},{2,3},{5,4},{4,5},{7,6},{6,7},{9,8},{8,9},{11,10... | collective-permute-start | bytes 1327112 | tf_op jit(solution)/shard_map/ppermute | solution.py:443
  34.2 7.3 %collective-permute-start.7 = (bf16[24,9216]{1,0:T(8,128)(2,1)}, bf16[24,9216]{1,0:T(8,128)(2,1)}, u32[]{:S(2)}, u32[]{:S(2)}) collective-permute-start(bf16[24,9216]{1,0:T(8,128)(2,1)} %collective-permute-done.2.refs_2_), channel_id=1, source_target_pairs={{1,0},{0,1},{3,2},{2,3},{5,4},{4,5},{7,6},{6,7},{9,8},{8,9},{11,10... | collective-permute-start | bytes 1327112 | tf_op jit(solution)/shard_map/ppermute | solution.py:443
  34.3 22.2 %collective-permute-start.4 = (bf16[2,24,9216]{2,1,0:T(8,128)(2,1)S(1)}, bf16[2,24,9216]{2,1,0:T(8,128)(2,1)}, u32[]{:S(2)}, u32[]{:S(2)}) collective-permute-start(bf16[2,24,9216]{2,1,0:T(8,128)(2,1)S(1)} %slice.26), channel_id=1, source_target_pairs={{2,0},{3,1},{0,2},{1,3},{6,4},{7,5},{4,6},{5,7},{10,8},{11,9},{8,1... | collective-permute-start | bytes 2654216 | tf_op jit(solution)/shard_map/ppermute | solution.py:440
  36.1 24.8 %collective-permute-start.5 = (bf16[2,24,9216]{2,1,0:T(8,128)(2,1)}, bf16[2,24,9216]{2,1,0:T(8,128)(2,1)}, u32[]{:S(2)}, u32[]{:S(2)}) collective-permute-start(bf16[2,24,9216]{2,1,0:T(8,128)(2,1)} %collective-permute-done.refs_2_), channel_id=1, source_target_pairs={{0,4},{4,8},{8,12},{12,16},{16,20},{20,24},{24,28},{28,0},{1,5},{5... | collective-permute-start | bytes 2654216 | tf_op jit(solution)/shard_map/ppermute | solution.py:437
  41.0 22.1 %collective-permute-start.3 = (bf16[2,24,9216]{2,1,0:T(8,128)(2,1)}, bf16[2,24,9216]{2,1,0:T(8,128)(2,1)}, u32[]{:S(2)}, u32[]{:S(2)}) collective-permute-start(bf16[2,24,9216]{2,1,0:T(8,128)(2,1)} %collective-permute-done.refs_2_), channel_id=1, source_target_pairs={{1,0},{0,1},{3,2},{2,3},{5,4},{4,5},{7,6},{6,7},{9,8},{8,9},{11,10... | collective-permute-start | bytes 2654216 | tf_op jit(solution)/shard_map/ppermute | solution.py:443
  41.0 23.9 %collective-permute-start.11 = (bf16[3,24,9216]{2,1,0:T(8,128)(2,1)}, bf16[3,24,9216]{2,1,0:T(8,128)(2,1)}, u32[]{:S(2)}, u32[]{:S(2)}) collective-permute-start(bf16[3,24,9216]{2,1,0:T(8,128)(2,1)} %collective-permute-done.8.refs_8_), channel_id=1, source_target_pairs={{1,0},{0,1},{3,2},{2,3},{5,4},{4,5},{7,6},{6,7},{9,8},{8,9},{11,10... | collective-permute-start | bytes 3981320 | tf_op jit(solution)/shard_map/ppermute | solution.py:443
  61.0 2.8 %collective-permute-start.9 = (bf16[2,24,9216]{2,1,0:T(8,128)(2,1)}, bf16[2,24,9216]{2,1,0:T(8,128)(2,1)}, u32[]{:S(2)}, u32[]{:S(2)}) collective-permute-start(bf16[2,24,9216]{2,1,0:T(8,128)(2,1)} %collective-permute-done.4.refs_6_), channel_id=1, source_target_pairs={{1,0},{0,1},{3,2},{2,3},{5,4},{4,5},{7,6},{6,7},{9,8},{8,9},{11,10... | collective-permute-start | bytes 2654216 | tf_op jit(solution)/shard_map/ppermute | solution.py:443
  61.0 4.0 %collective-permute-start.12 = (bf16[2,24,9216]{2,1,0:T(8,128)(2,1)}, bf16[2,24,9216]{2,1,0:T(8,128)(2,1)}, u32[]{:S(2)}, u32[]{:S(2)}) collective-permute-start(bf16[2,24,9216]{2,1,0:T(8,128)(2,1)} %collective-permute-done.5.refs_10_), channel_id=1, source_target_pairs={{1,0},{0,1},{3,2},{2,3},{5,4},{4,5},{7,6},{6,7},{9,8},{8,9},{11,10... | collective-permute-start | bytes 2654216 | tf_op jit(solution)/shard_map/ppermute | solution.py:443
  62.5 19.1 %collective-permute-start.17 = (bf16[1,24,9216]{2,1,0:T(8,128)(2,1)S(1)}, bf16[1,24,9216]{2,1,0:T(8,128)(2,1)}, u32[]{:S(2)}, u32[]{:S(2)}) collective-permute-start(bf16[1,24,9216]{2,1,0:T(8,128)(2,1)S(1)} %slice.28), channel_id=1, source_target_pairs={{2,0},{3,1},{0,2},{1,3},{6,4},{7,5},{4,6},{5,7},{10,8},{11,9},{8,1... | collective-permute-start | bytes 1327112 | tf_op jit(solution)/shard_map/ppermute | solution.py:440
  63.1 14.9 %collective-permute-start.10 = (bf16[1,24,9216]{2,1,0:T(8,128)(2,1)S(1)}, bf16[1,24,9216]{2,1,0:T(8,128)(2,1)}, u32[]{:S(2)}, u32[]{:S(2)}) collective-permute-start(bf16[1,24,9216]{2,1,0:T(8,128)(2,1)S(1)} %slice.25), channel_id=1, source_target_pairs={{0,4},{4,8},{8,12},{12,16},{16,20},{20,24},{24,28},{28,0},{1,5},{5... | collective-permute-start | bytes 1327112 | tf_op jit(solution)/shard_map/ppermute | solution.py:437
  79.9 33.3 %collective-permute-start.14 = (bf16[1,24,9216]{2,1,0:T(8,128)(2,1)}, bf16[1,24,9216]{2,1,0:T(8,128)(2,1)}, u32[]{:S(2)}, u32[]{:S(2)}) collective-permute-start(bf16[1,24,9216]{2,1,0:T(8,128)(2,1)} %broadcast_multiply_fusion), channel_id=1, source_target_pairs={{2,0},{3,1},{0,2},{1,3},{6,4},{7,5},{4,6},{5,7},{10,8},{11,9},{8,1... | collective-permute-start | bytes 1327112 | tf_op jit(solution)/shard_map/ppermute | solution.py:440
  81.1 36.7 %collective-permute-start.13 = (bf16[1,24,9216]{2,1,0:T(8,128)(2,1)}, bf16[1,24,9216]{2,1,0:T(8,128)(2,1)}, u32[]{:S(2)}, u32[]{:S(2)}) collective-permute-start(bf16[1,24,9216]{2,1,0:T(8,128)(2,1)} %collective-permute-done.10.refs_8_), channel_id=1, source_target_pairs={{1,0},{0,1},{3,2},{2,3},{5,4},{4,5},{7,6},{6,7},{9,8},{8,9},{11,10... | collective-permute-start | bytes 1327112 | tf_op jit(solution)/shard_map/ppermute | solution.py:443
  81.1 14.8 %collective-permute-start.19 = (bf16[24,9216]{1,0:T(8,128)(2,1)}, bf16[24,9216]{1,0:T(8,128)(2,1)S(1)}, u32[]{:S(2)}, u32[]{:S(2)}) collective-permute-start(bf16[24,9216]{1,0:T(8,128)(2,1)} %get-tuple-element.77), channel_id=1, source_target_pairs={{1,0},{0,1},{3,2},{2,3},{5,4},{4,5},{7,6},{6,7},{9,8},{8,9},{11,10... | collective-permute-start | bytes 1327112 | tf_op jit(solution)/shard_map/ppermute | solution.py:443
  81.6 17.8 %collective-permute-start.18 = (bf16[1,24,9216]{2,1,0:T(8,128)(2,1)}, bf16[1,24,9216]{2,1,0:T(8,128)(2,1)}, u32[]{:S(2)}, u32[]{:S(2)}) collective-permute-start(bf16[1,24,9216]{2,1,0:T(8,128)(2,1)} %collective-permute-done.17.refs_10_), channel_id=1, source_target_pairs={{1,0},{0,1},{3,2},{2,3},{5,4},{4,5},{7,6},{6,7},{9,8},{8,9},{11,10... | collective-permute-start | bytes 1327112 | tf_op jit(solution)/shard_map/ppermute | solution.py:443
  81.6 14.3 %copy-start.2 = (f32[24,9216]{1,0:T(8,128)S(1)}, f32[24,9216]{1,0:T(8,128)}, u32[]{:S(2)}) copy-start(f32[24,9216]{1,0:T(8,128)} %get-tuple-element.66) | copy-start | bytes 2654212
  95.3 18.4 %collective-permute-start.16 = (bf16[24,9216]{1,0:T(8,128)(2,1)}, bf16[24,9216]{1,0:T(8,128)(2,1)}, u32[]{:S(2)}, u32[]{:S(2)}) collective-permute-start(bf16[24,9216]{1,0:T(8,128)(2,1)} %get-tuple-element.75), channel_id=1, source_target_pairs={{1,0},{0,1},{3,2},{2,3},{5,4},{4,5},{7,6},{6,7},{9,8},{8,9},{11,10... | collective-permute-start | bytes 1327112 | tf_op jit(solution)/shard_map/ppermute | solution.py:443
  95.9 21.8 %collective-permute-start.21 = (bf16[24,9216]{1,0:T(8,128)(2,1)S(1)}, bf16[24,9216]{1,0:T(8,128)(2,1)}, u32[]{:S(2)}, u32[]{:S(2)}) collective-permute-start(bf16[24,9216]{1,0:T(8,128)(2,1)S(1)} %add_convert_fusion.2), channel_id=1, source_target_pairs={{0,28},{4,0},{8,4},{12,8},{16,12},{20,16},{24,20},{28,24},{1,29},{... | collective-permute-start | bytes 1327112 | tf_op jit(solution)/shard_map/ppermute | solution.py:437
  99.4 14.3 %copy-start.1 = (f32[24,9216]{1,0:T(8,128)S(1)}, f32[24,9216]{1,0:T(8,128)}, u32[]{:S(2)}) copy-start(f32[24,9216]{1,0:T(8,128)} %get-tuple-element.73) | copy-start | bytes 2654212
  113.1 2.1 %collective-permute-start.20 = (bf16[24,9216]{1,0:T(8,128)(2,1)}, bf16[24,9216]{1,0:T(8,128)(2,1)S(1)}, u32[]{:S(2)}, u32[]{:S(2)}) collective-permute-start(bf16[24,9216]{1,0:T(8,128)(2,1)} %get-tuple-element.84), channel_id=1, source_target_pairs={{1,0},{0,1},{3,2},{2,3},{5,4},{4,5},{7,6},{6,7},{9,8},{8,9},{11,10... | collective-permute-start | bytes 1327112 | tf_op jit(solution)/shard_map/ppermute | solution.py:443
  113.2 4.6 %collective-permute-start.15 = (bf16[1,24,9216]{2,1,0:T(8,128)(2,1)}, bf16[1,24,9216]{2,1,0:T(8,128)(2,1)}, u32[]{:S(2)}, u32[]{:S(2)}) collective-permute-start(bf16[1,24,9216]{2,1,0:T(8,128)(2,1)} %collective-permute-done.14.refs_10_), channel_id=1, source_target_pairs={{1,0},{0,1},{3,2},{2,3},{5,4},{4,5},{7,6},{6,7},{9,8},{8,9},{11,10... | collective-permute-start | bytes 1327112 | tf_op jit(solution)/shard_map/ppermute | solution.py:443
  114.8 16.7 %collective-permute-start.23 = (bf16[24,9216]{1,0:T(8,128)(2,1)S(1)}, bf16[24,9216]{1,0:T(8,128)(2,1)S(1)}, u32[]{:S(2)}, u32[]{:S(2)}) collective-permute-start(bf16[24,9216]{1,0:T(8,128)(2,1)S(1)} %add_convert_fusion.3), channel_id=1, source_target_pairs={{0,28},{4,0},{8,4},{12,8},{16,12},{20,16},{24,20},{28,24},{1,29},{... | collective-permute-start | bytes 1327112 | tf_op jit(solution)/shard_map/ppermute | solution.py:437
  116.4 20.2 %collective-permute-start.24 = (bf16[24,9216]{1,0:T(8,128)(2,1)S(1)}, bf16[24,9216]{1,0:T(8,128)(2,1)}, u32[]{:S(2)}, u32[]{:S(2)}) collective-permute-start(bf16[24,9216]{1,0:T(8,128)(2,1)S(1)} %add_convert_fusion.1), channel_id=1, source_target_pairs={{0,28},{4,0},{8,4},{12,8},{16,12},{20,16},{24,20},{28,24},{1,29},{... | collective-permute-start | bytes 1327112 | tf_op jit(solution)/shard_map/ppermute | solution.py:437
  131.4 2.3 %copy-start.3 = (f32[24,9216]{1,0:T(8,128)S(1)}, f32[24,9216]{1,0:T(8,128)}, u32[]{:S(2)}) copy-start(f32[24,9216]{1,0:T(8,128)} %get-tuple-element.94) | copy-start | bytes 2654212
  131.4 5.2 %copy-start.5 = (f32[24,9216]{1,0:T(8,128)S(1)}, f32[24,9216]{1,0:T(8,128)}, u32[]{:S(2)}) copy-start(f32[24,9216]{1,0:T(8,128)} %get-tuple-element.92) | copy-start | bytes 2654212
  131.4 5.2 %copy-start.6 = (f32[24,9216]{1,0:T(8,128)S(1)}, f32[24,9216]{1,0:T(8,128)}, u32[]{:S(2)}) copy-start(f32[24,9216]{1,0:T(8,128)} %get-tuple-element.93) | copy-start | bytes 2654212
  131.5 2.3 %collective-permute-start.25 = (bf16[24,9216]{1,0:T(8,128)(2,1)}, bf16[24,9216]{1,0:T(8,128)(2,1)S(1)}, u32[]{:S(2)}, u32[]{:S(2)}) collective-permute-start(bf16[24,9216]{1,0:T(8,128)(2,1)} %get-tuple-element.96), channel_id=1, source_target_pairs={{1,0},{0,1},{3,2},{2,3},{5,4},{4,5},{7,6},{6,7},{9,8},{8,9},{11,10... | collective-permute-start | bytes 1327112 | tf_op jit(solution)/shard_map/ppermute | solution.py:443
  133.3 3.3 %collective-permute-start.22 = (bf16[2,24,9216]{2,1,0:T(8,128)(2,1)S(1)}, bf16[2,24,9216]{2,1,0:T(8,128)(2,1)S(1)}, u32[]{:S(2)}, u32[]{:S(2)}) collective-permute-start(bf16[2,24,9216]{2,1,0:T(8,128)(2,1)S(1)} %pad_maximum_fusion.1), channel_id=1, source_target_pairs={{1,0},{0,1},{3,2},{2,3},{5,4},{4,5},{7,6},{6,7},{9,8},{8,9},{11,10... | collective-permute-start | bytes 2654216 | tf_op jit(solution)/shard_map/ppermute | solution.py:443
  133.8 12.3 %collective-permute-start.26 = (bf16[24,9216]{1,0:T(8,128)(2,1)S(1)}, bf16[24,9216]{1,0:T(8,128)(2,1)S(1)}, u32[]{:S(2)}, u32[]{:S(2)}) collective-permute-start(bf16[24,9216]{1,0:T(8,128)(2,1)S(1)} %add_convert_fusion), channel_id=1, source_target_pairs={{0,28},{4,0},{8,4},{12,8},{16,12},{20,16},{24,20},{28,24},{1,29},{... | collective-permute-start | bytes 1327112 | tf_op jit(solution)/shard_map/ppermute | solution.py:437
